TPU v7x, 32 devices: a whole 2x2x4 slice. The times are simulated.
32 devices in a mesh: group: 2 (over x), tile: 4 (over y, core), orient: 4 (over z).
Axes of the slice: x: 2, y: 2, z: 4, core: 2. Of those that a mesh axis runs over, the one named last changes fastest.
Arguments:
- micrograph: float32 [768, 1024], P('group', 'tile'), parts along dimension 0, may hold values from -30 to 30
- templates: float32 [4, 4, 128, 128], P('orient', 'tile'), may hold values from 0 to 0.0107421875
- orient_ids: int32 [4, 4], P('orient', 'tile'), may hold values from 0 to 15, as said below
- log_weight: float32 [16], replicated, may hold values from -2 to 2
- ice_mask: int32 [32, 64], P('group', 'tile'), parts along dimension 0, may hold values 0 or 1
Outputs:
- score_map: float32 [512, 1024], P(('group', 'orient'), 'tile'), parts along dimension 0
There are 2 independent parts, one for each index of `group`. A program takes and returns all parts, laid end to end along the dimension named above; an argument that names none is the same for every part. Nothing has to cross between parts.
Inputs may be any that keep to these rules, and one draw needn't show every extreme that they name: `orient_ids`: every slot holds a different orientation.
All inputs are finite; a program needn't handle non-finite values. No bound on the sum of `ice_mask` on one device may be relied on, other than what follows from the above.
Results may differ from a plain program's by a relative error of at most 0.00024.
Values sent between devices are 32-bit elements; how exact they have to be, the bound alone decides.
No kernel may reach another device: no remote copies, remote signals or barrier semaphores. Data moves between devices by JAX's collectives and lax.ppermute only.
A program may use at most 64 MiB of HBM per device.

v0:
```python
import functools
import math

import jax
import jax.numpy as jnp
import ml_dtypes
import numpy as np
from jax import lax
from jax.experimental import pallas as pl
from jax.experimental.pallas import tpu as pltpu
from jax.sharding import PartitionSpec as P

GUARD = 64
MBLK = 16
LANES = 128
PACK = 8
CHUNK = 12

F32 = jnp.float32
BF16 = jnp.bfloat16
VMEM = pl.BlockSpec(memory_space=pltpu.VMEM)
SMEM = pl.BlockSpec(memory_space=pltpu.SMEM)


def params(mib):
    return pltpu.CompilerParams(vmem_limit_bytes=mib * 2**20)


def high_low(table):
    high = table.astype(np.float32).astype(ml_dtypes.bfloat16)
    low = (table - high.astype(np.float64)).astype(np.float32).astype(ml_dtypes.bfloat16)
    return high, low


def tables(side):
    span = 2 * side
    angles = np.outer(np.arange(span), 2.0 * math.pi * (np.arange(side) + 0.5) / span)
    basis = np.concatenate([np.cos(angles), np.sin(angles)], axis=1)
    high, low = high_low(basis)
    back_high, back_low = high_low(np.concatenate([np.cos(angles[:side]), -np.sin(angles[:side])], axis=1).T)
    return dict(
        image_cols=np.concatenate([high, high, low], axis=0),
        image_rows=np.concatenate([high.T, high.T, low.T], axis=1),
        patch_cols=np.concatenate([high[:side], high[:side], low[:side]], axis=0),
        patch_rows=np.concatenate([high[:side].T, high[:side].T, low[:side].T], axis=1),
        back_rows=np.concatenate([high[:side], high[:side], low[:side]], axis=1),
        back_cols=np.concatenate([back_high, back_high, back_low], axis=0),
    )


def split(x):
    high = x.astype(BF16)
    return high, (x - high.astype(F32)).astype(BF16)


def tripled(x, axis):
    high, low = split(x)
    return jnp.concatenate([high, low, high], axis=axis)


def product(left, right):
    return jnp.dot(left, right, preferred_element_type=F32)


def paired(quads, side):
    cc, cs = quads[:side, :side], quads[:side, side:]
    sc, ss = quads[side:, :side], quads[side:, side:]
    return cc - ss, sc + cs, cc + ss, sc - cs


def image_spectra(left_ref, own_ref, right_ref, cols_ref, rows_ref, spec_ref):
    image = jnp.concatenate([left_ref[...], own_ref[...], right_ref[...]], axis=1)
    side = spec_ref.shape[-1]
    span = 2 * side
    rows, cols = image.shape[0] // side - 1, image.shape[1] // side - 1
    scale = 2.0 / (span * span)
    for q in range(cols):
        half = product(tripled(image[:, q * side : q * side + span], 1), cols_ref[...])
        for p in range(rows):
            full = product(rows_ref[...], tripled(half[p * side : p * side + span], 0))
            for part, value in enumerate(paired(full, side)):
                spec_ref[p * cols + q, part] = value * scale


def correlate(spec_ref, patches, tabs, half_ref, patch_ref, score_ref):
    patch_cols, patch_rows, back_rows, back_cols = tabs
    side = spec_ref.shape[-1]
    count = len(patches)
    cols = score_ref.shape[2] // side
    for first in range(0, count, 4):
        group = patches[first : first + 4]
        half = product(tripled(jnp.concatenate(group, axis=0), 1), patch_cols[...])
        for i in range(len(group)):
            high, low = split(half[i * side : (i + 1) * side])
            half_ref[first + i, 0:side] = high
            half_ref[first + i, side : 2 * side] = low
            half_ref[first + i, 2 * side : 3 * side] = high

    def finish_patch(n, carry):
        for part, value in enumerate(paired(product(patch_rows[...], half_ref[n]), side)):
            patch_ref[n, part] = value
        return carry

    def score(n, carry):
        tr, tu, sr, si = (patch_ref[n, part] for part in range(4))
        for block in range(spec_ref.shape[0]):
            p, q = divmod(block, cols)
            ir, iu, jr, ji = (spec_ref[block, part] for part in range(4))
            a, b = ir * tr + iu * tu, ir * tu - iu * tr
            c, d = jr * sr + ji * si, ji * sr - jr * si
            top = jnp.concatenate([a + c, b + d], axis=1)
            low = jnp.concatenate([d - b, a - c], axis=1)
            lines = product(back_rows[...], tripled(jnp.concatenate([top, low], axis=0), 0))
            score_ref[n, p * side : (p + 1) * side, q * side : (q + 1) * side] = product(
                tripled(lines, 1), back_cols[...]
            )
        return carry

    unroll = max(u for u in (1, 2, 3, 4) if count % u == 0)
    lax.fori_loop(0, count, finish_patch, 0, unroll=unroll)
    lax.fori_loop(0, count, score, 0, unroll=unroll)


STRIP = 16


def fold(score_ref, weights, state, out):
    def strip(r, carry):
        rows = pl.ds(pl.multiple_of(r * STRIP, STRIP), STRIP)
        values = [score_ref[n, rows, :] + weight for n, weight in enumerate(weights)]
        top = values[0]
        for value in values[1:]:
            top = jnp.maximum(top, value)
        if state is not None:
            old_top, old_sum = state[0][rows, :], state[1][rows, :]
            top = jnp.maximum(top, old_top)
        total = jnp.exp(values[0] - top)
        for value in values[1:]:
            total = total + jnp.exp(value - top)
        if state is not None:
            total = total + old_sum * jnp.exp(old_top - top)
        out(rows, top, total)
        return carry

    lax.fori_loop(0, score_ref.shape[1] // STRIP, strip, 0)


def unpack(refs, side):
    patches, weights = [], []
    for ref in refs:
        if len(ref.shape) == 2:
            patches.append(ref[0:side, :])
            weights.append(ref[side : side + 1, 0:1])
        else:
            for i in range(ref.shape[0]):
                patches.append(ref[i, 0:side, :])
                weights.append(ref[i, side : side + 1, 0:1])
    return patches, weights


def first_kernel(n_in, *refs):
    left, own, right, image_cols, image_rows = refs[:5]
    tabs, packs = refs[5:9], refs[9 : 9 + n_in]
    spec_ref, top_ref, sum_ref, half_ref, patch_ref, score_ref = refs[9 + n_in :]
    image_spectra(left, own, right, image_cols, image_rows, spec_ref)
    patches, weights = unpack(packs, spec_ref.shape[-1])
    correlate(spec_ref, patches, tabs, half_ref, patch_ref, score_ref)

    def out(rows, top, total):
        top_ref[rows, :] = top
        sum_ref[rows, :] = total

    fold(score_ref, weights, None, out)


def next_kernel(n_in, *refs):
    spec_ref, old_top, old_sum = refs[:3]
    tabs, packs = refs[3:7], refs[7 : 7 + n_in]
    top_ref, sum_ref, half_ref, patch_ref, score_ref = refs[7 + n_in :]
    patches, weights = unpack(packs, spec_ref.shape[-1])
    correlate(spec_ref, patches, tabs, half_ref, patch_ref, score_ref)

    def out(rows, top, total):
        top_ref[rows, :] = top
        sum_ref[rows, :] = total

    fold(score_ref, weights, (old_top, old_sum), out)


def unmasked_pixels(mask_ref):
    blocks = (1.0 - mask_ref[...].astype(F32)).astype(BF16)
    rows, cols = blocks.shape

    def spread(count, axis):
        shape = (count * MBLK, count) if axis == 0 else (count, count * MBLK)
        pixel = lax.broadcasted_iota(jnp.int32, shape, axis)
        block = lax.broadcasted_iota(jnp.int32, shape, 1 - axis)
        return ((pixel >= block * MBLK) & (pixel < (block + 1) * MBLK)).astype(F32).astype(BF16)

    return product(product(spread(rows, 0), blocks).astype(BF16), spread(cols, 1))


def last_kernel(n_in, share, *refs):
    place_ref, mask_ref, spec_ref, old_top, old_sum = refs[:5]
    tabs, packs = refs[5:9], refs[9 : 9 + n_in]
    part_ref, open_ref, stat_ref, half_ref, patch_ref, score_ref, log_ref, pixel_ref = refs[9 + n_in :]
    patches, weights = unpack(packs, spec_ref.shape[-1])
    correlate(spec_ref, patches, tabs, half_ref, patch_ref, score_ref)

    def out(rows, top, total):
        log_ref[rows, :] = top + jnp.log(total)

    fold(score_ref, weights, (old_top, old_sum), out)
    pixels = unmasked_pixels(mask_ref)
    pixel_ref[...] = pixels
    values = log_ref[...]
    count = jnp.sum(pixels)
    total = jnp.sum(pixels * values)
    deviation = values - total / jnp.maximum(count, 1.0)
    squares = jnp.sum(pixels * deviation * deviation)
    lane = lax.broadcasted_iota(jnp.int32, stat_ref.shape, 1)
    stat_ref[...] = jnp.where(lane == 0, count, jnp.where(lane == 1, total, squares))
    own = pl.ds(pl.multiple_of(place_ref[0] * share, share), share)
    part_ref[...] = log_ref[own, :]
    open_ref[...] = pixel_ref[own, :]


def norm_kernel(part_ref, open_ref, *refs):
    stats, out_ref = refs[:-1], refs[-1]
    counts = [ref[:, 0:1] for ref in stats]
    totals = [ref[:, 1:2] for ref in stats]
    count, total = sum(counts), sum(totals)
    average = total / count
    squares = 0.0
    for ref, n, s in zip(stats, counts, totals):
        apart = s / jnp.maximum(n, 1.0) - average
        squares = squares + ref[:, 2:3] + n * apart * apart
    scale = 1.0 / jnp.sqrt(squares / count + 1e-05)
    out_ref[...] = open_ref[...] * (part_ref[...] - average[0:1]) * scale[0:1]


def peer(x, axis, step):
    n = lax.axis_size(axis)
    if n & (n - 1):
        pairs = [(i, (i + step) % n) for i in range(n)]
    else:
        pairs = [(i, i ^ step) for i in range(n)]
    return lax.ppermute(x, axis, pairs)


def swap(x, axis):
    return lax.ppermute(x, axis, [(i, i ^ 1) for i in range(lax.axis_size(axis))])


def halo(own, axis):
    n = lax.axis_size(axis)
    up = [(i, i + 1) for i in range(n - 1)]
    left = lax.ppermute(own[:, own.shape[1] - GUARD :], axis, up)
    right = lax.ppermute(own[:, :GUARD], axis, [(j, i) for i, j in up])
    return left, right


def chunks(arrays):
    groups, held = [[]], 0
    for x in arrays:
        if held + x.shape[0] > CHUNK and groups[-1]:
            groups.append([])
            held = 0
        groups[-1].append(x)
        held += x.shape[0]
    return groups


def body(micrograph, templates, orient_ids, log_weight, ice_mask):
    side = templates.shape[2]
    tile = micrograph.shape[1]
    blocks = (tile // side) ** 2
    tab = {name: jnp.asarray(value) for name, value in tables(side).items()}
    tabs = [tab["patch_cols"], tab["patch_rows"], tab["back_rows"], tab["back_cols"]]
    place = lax.axis_index("orient").astype(jnp.int32).reshape(1)

    catalog = lax.broadcasted_iota(jnp.int32, log_weight.shape, 0)
    weight = jnp.sum(jnp.where(catalog == orient_ids[0, 0], log_weight, 0.0))
    pack = jnp.concatenate([templates[0, 0], jnp.full((PACK, side), weight, F32)], axis=0)

    n_tile, n_orient = lax.axis_size("tile"), lax.axis_size("orient")
    far = [peer(pack, "orient", k) for k in range(1, n_orient)]
    left, right = halo(micrograph, "tile")
    even = n_tile % 2 == 0
    steps = range(2, n_tile, 2) if even else range(1, n_tile)
    near = [peer(pack, "tile", k) for k in steps]
    mine = [pack, *near]
    if even:
        mine += [swap(x, "tile") for x in mine]
    rest = [jnp.stack(far)] if far else []
    held = rest + [peer(x, "tile", k) for x in rest for k in steps]
    groups = [[x] for x in held]
    if even:
        groups += chunks([swap(x, "tile") for x in held])

    spectra = jax.ShapeDtypeStruct((blocks, 4, side, side), F32)
    plane = jax.ShapeDtypeStruct((tile, tile), F32)

    def scratch(n):
        return [
            pltpu.VMEM((n, 3 * side, 2 * side), BF16),
            pltpu.VMEM((n, 4, side, side), F32),
            pltpu.VMEM((n, tile, tile), F32),
        ]

    def size(group):
        return sum(x.shape[0] if x.ndim == 3 else 1 for x in group)

    spec, top, total = pl.pallas_call(
        functools.partial(first_kernel, len(mine)),
        out_shape=(spectra, plane, plane),
        in_specs=[VMEM] * (9 + len(mine)),
        out_specs=(VMEM,) * 3,
        scratch_shapes=scratch(len(mine)),
        compiler_params=params(40),
        name="own_block",
    )(left, micrograph, right, tab["image_cols"], tab["image_rows"], *tabs, *mine)
    for group in groups[:-1]:
        top, total = pl.pallas_call(
            functools.partial(next_kernel, len(group)),
            out_shape=(plane, plane),
            in_specs=[VMEM] * (7 + len(group)),
            out_specs=(VMEM,) * 2,
            scratch_shapes=scratch(size(group)),
            compiler_params=params(40),
            name="next_block",
        )(spec, top, total, *tabs, *group)
    group = groups[-1]
    share = tile // n_orient
    part = jax.ShapeDtypeStruct((share, tile), F32)
    part, opened, stat = pl.pallas_call(
        functools.partial(last_kernel, len(group), share),
        out_shape=(part, part, jax.ShapeDtypeStruct((8, LANES), F32)),
        in_specs=[SMEM] + [VMEM] * (8 + len(group)),
        out_specs=(VMEM,) * 3,
        scratch_shapes=scratch(size(group)) + [pltpu.VMEM((tile, tile), F32)] * 2,
        compiler_params=params(40),
        name="last_block",
    )(place, ice_mask, spec, top, total, *tabs, *group)
    stats = [stat] + [peer(stat, "tile", k) for k in range(1, n_tile)]
    return pl.pallas_call(
        norm_kernel,
        out_shape=jax.ShapeDtypeStruct((share, tile), F32),
        in_specs=[VMEM] * (2 + len(stats)),
        out_specs=VMEM,
        name="normalise",
    )(part, opened, *stats)


def solution(mesh):
    return jax.shard_map(
        body,
        mesh=mesh,
        in_specs=(
            P("group", "tile"),
            P("orient", "tile", None, None),
            P("orient", "tile"),
            P(),
            P("group", "tile"),
        ),
        out_specs=P(("group", "orient"), "tile"),
        check_vma=False,
    )
```

profile of v0, /device:TPU:0, one launch (start us, length us, event | category | flops | bytes accessed | tf_op | source)
XLA Modules:
  0.0 59.4 jit_solution(12172094597156659659)
XLA Ops:
  0.7 1.3 %fusion = f32[]{:T(128)} fusion(f32[16]{0:T(128)} %param.14, s32[]{:T(128)} %bitcast.6), kind=kLoop, calls=%fused_computation.2 | loop fusion | flops 47 | bytes 72 | tf_op jit(solution)/shard_map/reduce_sum | solution.py:283
  2.0 1.5 %concatenate.3.refs_9_ = f32[136,128]{1,0:T(8,128)S(1)} pad(f32[128,128]{1,0:T(8,128)} %bitcast.10, f32[]{:T(128)} %fusion), padding=0_8x0_0 | pad | bytes 135172 | tf_op jit(solution)/shard_map/concatenate | solution.py:284
  3.5 3.0 %collective-permute-start.5 = (f32[136,128]{1,0:T(8,128)S(1)}, f32[136,128]{1,0:T(8,128)S(1)}, u32[]{:S(2)}, u32[]{:S(2)}) collective-permute-start(f32[136,128]{1,0:T(8,128)S(1)} %concatenate.3.refs_9_), channel_id=1, source_target_pairs={{0,1},{1,0},{2,3},{3,2},{4,5},{5,4},{6,7},{7,6},{8,9},{9,8},{10,11... | collective-permute-start | bytes 208904 | tf_op jit(solution)/shard_map/ppermute | solution.py:248
  6.5 2.6 %collective-permute-start.6 = (f32[136,128]{1,0:T(8,128)S(1)}, f32[136,128]{1,0:T(8,128)S(1)}, u32[]{:S(2)}, u32[]{:S(2)}) collective-permute-start(f32[136,128]{1,0:T(8,128)S(1)} %concatenate.3.refs_9_), channel_id=1, source_target_pairs={{0,2},{1,3},{2,0},{3,1},{4,6},{5,7},{6,4},{7,5},{8,10},{9,11},{10,... | collective-permute-start | bytes 208904 | tf_op jit(solution)/shard_map/ppermute | solution.py:248
  9.1 4.9 %collective-permute-done.6 = f32[136,128]{1,0:T(8,128)S(1)} collective-permute-done((f32[136,128]{1,0:T(8,128)S(1)}, f32[136,128]{1,0:T(8,128)S(1)}, u32[]{:S(2)}, u32[]{:S(2)}) %collective-permute-start.6) | collective-permute-done | bytes 69664 | tf_op jit(solution)/shard_map/ppermute | solution.py:248
  14.0 1.3 %collective-permute-done.7 = f32[136,128]{1,0:T(8,128)S(1)} collective-permute-done((f32[136,128]{1,0:T(8,128)S(1)}, f32[136,128]{1,0:T(8,128)S(1)}, u32[]{:S(2)}, u32[]{:S(2)}) %collective-permute-start.7) | collective-permute-done | bytes 69664 | tf_op jit(solution)/shard_map/ppermute | solution.py:248
  15.4 1.6 %collective-permute-start.8 = (f32[3,136,128]{2,1,0:T(8,128)S(1)}, f32[3,136,128]{2,1,0:T(8,128)S(1)}, u32[]{:S(2)}, u32[]{:S(2)}) collective-permute-start(f32[3,136,128]{2,1,0:T(8,128)S(1)} %pad_maximum_fusion.refs_7_), channel_id=1, source_target_pairs={{0,8},{4,12},{8,0},{12,4},{1,9},{5,13},{9,1},{13,5},{2,10},{6,14},... | collective-permute-start | bytes 626696 | tf_op jit(solution)/shard_map/ppermute | solution.py:248
  18.0 3.3 %collective-permute-done.8.refs_7_ = f32[3,136,128]{2,1,0:T(8,128)S(1)} collective-permute-done((f32[3,136,128]{2,1,0:T(8,128)S(1)}, f32[3,136,128]{2,1,0:T(8,128)S(1)}, u32[]{:S(2)}, u32[]{:S(2)}) %collective-permute-start.8) | collective-permute-done | bytes 208928 | tf_op jit(solution)/shard_map/ppermute | solution.py:248
  21.4 2.4 %collective-permute-start = (f32[384,64]{1,0:T(8,128)S(1)}, f32[384,64]{1,0:T(8,128)S(1)}, u32[]{:S(2)}, u32[]{:S(2)}) collective-permute-start(f32[384,64]{1,0:T(8,128)S(1)} %get-tuple-element.26), channel_id=1, source_target_pairs={{0,4},{4,8},{8,12},{1,5},{5,9},{9,13},{2,6},{6,10},{10,14},{3,7},{... | collective-permute-start | bytes 294920 | tf_op jit(solution)/shard_map/ppermute | solution.py:258
  23.8 1.3 %collective-permute-start.1 = (f32[384,64]{1,0:T(8,128)S(1)}, f32[384,64]{1,0:T(8,128)S(1)}, u32[]{:S(2)}, u32[]{:S(2)}) collective-permute-start(f32[384,64]{1,0:T(8,128)S(1)} %get-tuple-element.25), channel_id=1, source_target_pairs={{4,0},{8,4},{12,8},{5,1},{9,5},{13,9},{6,2},{10,6},{14,10},{7,3},{... | collective-permute-start | bytes 294920 | tf_op jit(solution)/shard_map/ppermute | solution.py:259
  25.1 1.8 %collective-permute-start.4 = (f32[136,128]{1,0:T(8,128)S(1)}, f32[136,128]{1,0:T(8,128)S(1)}, u32[]{:S(2)}, u32[]{:S(2)}) collective-permute-start(f32[136,128]{1,0:T(8,128)S(1)} %collective-permute-done.2.refs_10_), channel_id=1, source_target_pairs={{0,4},{4,0},{8,12},{12,8},{1,5},{5,1},{9,13},{13,9},{2,6},{6,2},{1... | collective-permute-start | bytes 208904 | tf_op jit(solution)/shard_map/ppermute | solution.py:252
  26.9 0.8 %collective-permute-done.1.refs_2_ = f32[384,64]{1,0:T(8,128)S(1)} collective-permute-done((f32[384,64]{1,0:T(8,128)S(1)}, f32[384,64]{1,0:T(8,128)S(1)}, u32[]{:S(2)}, u32[]{:S(2)}) %collective-permute-start.1) | collective-permute-done | bytes 98336 | tf_op jit(solution)/shard_map/ppermute | solution.py:259
  27.9 1.0 %copy-done.5 = bf16[768,256]{1,0:T(8,128)(2,1)S(1)} copy-done((bf16[768,256]{1,0:T(8,128)(2,1)S(1)}, bf16[768,256]{1,0:T(8,128)(2,1)}, u32[]{:S(2)}) %copy-start.5) | copy-done | bytes 393240
  28.9 1.0 %copy-done.6 = bf16[256,768]{1,0:T(8,128)(2,1)S(1)} copy-done((bf16[256,768]{1,0:T(8,128)(2,1)S(1)}, bf16[256,768]{1,0:T(8,128)(2,1)}, u32[]{:S(2)}) %copy-start.6) | copy-done | bytes 393240
  29.9 4.8 %own_block.1 = (f32[4,4,128,128]{3,2,1,0:T(8,128)S(1)}, f32[256,256]{1,0:T(8,128)S(1)}, f32[256,256]{1,0:T(8,128)S(1)}) custom-call(f32[384,64]{1,0:T(8,128)S(1)} %collective-permute-done.refs_0_, f32[384,256]{1,0:T(8,128)S(1)} %copy-done.4, f32[384,64]{1,0:T(8,128)S(1)} %collective-permute-done.1.refs_2_, bf16[768,256]{1,0:T(8,128)(2,1)S(1)} %copy-done.5, ...), custom_call_target="tpu_custom_call" | custom-call | tf_op jit(solution)/shard_map/own_block/pallas_call | solution.py:314
  34.7 3.3 %next_block.2 = (f32[256,256]{1,0:T(8,128)S(1)}, f32[256,256]{1,0:T(8,128)S(1)}) custom-call(f32[4,4,128,128]{3,2,1,0:T(8,128)S(1)} %get-tuple-element.15.refs_0_.refs_2_, f32[256,256]{1,0:T(8,128)S(1)} %get-tuple-element.16.refs_1_, f32[256,256]{1,0:T(8,128)S(1)} %get-tuple-element.17.refs_2_, bf16[384,256]{1,0:T(8,128)(2,1)S(1)} %copy-done, ...), custom_call_target="tpu_custom_call" | custom-call | tf_op jit(solution)/shard_map/next_block/pallas_call | solution.py:324
  38.0 3.3 %next_block.3 = (f32[256,256]{1,0:T(8,128)S(1)}, f32[256,256]{1,0:T(8,128)S(1)}) custom-call(f32[4,4,128,128]{3,2,1,0:T(8,128)S(1)} %get-tuple-element.15.refs_0_.refs_2_, f32[256,256]{1,0:T(8,128)S(1)} %get-tuple-element.18.refs_1_, f32[256,256]{1,0:T(8,128)S(1)} %get-tuple-element.19.refs_2_, bf16[384,256]{1,0:T(8,128)(2,1)S(1)} %copy-done, ...), custom_call_target="tpu_custom_call" | custom-call | tf_op jit(solution)/shard_map/next_block/pallas_call | solution.py:324
  41.3 6.7 %last_block.1 = (f32[64,256]{1,0:T(8,128)S(1)}, f32[64,256]{1,0:T(8,128)S(1)}, f32[8,128]{1,0:T(8,128)S(1)}) custom-call(s32[1]{0:T(128)} %bitcast.refs_0_, s32[16,16]{1,0:T(8,128)S(1)} %copy-done.9, f32[4,4,128,128]{3,2,1,0:T(8,128)S(1)} %get-tuple-element.15.refs_0_.refs_2_, f32[256,256]{1,0:T(8,128)S(1)} %get-tuple-element.20.refs_3_, ...), custom_call_target="tpu_custom_call" | custom-call | tf_op jit(solution)/shard_map/last_block/pallas_call | solution.py:336
  48.0 0.6 %copy-done.7 = f32[64,256]{1,0:T(8,128)} copy-done((f32[64,256]{1,0:T(8,128)}, f32[64,256]{1,0:T(8,128)S(1)}, u32[]{:S(2)}) %copy-start.7) | copy-done | bytes 65560
  48.6 0.6 %copy-done.8 = f32[64,256]{1,0:T(8,128)} copy-done((f32[64,256]{1,0:T(8,128)}, f32[64,256]{1,0:T(8,128)S(1)}, u32[]{:S(2)}) %copy-start.8) | copy-done | bytes 65560
  49.2 4.1 %collective-permute-start.11 = (f32[8,128]{1,0:T(8,128)S(1)}, f32[8,128]{1,0:T(8,128)S(1)}, u32[]{:S(2)}, u32[]{:S(2)}) collective-permute-start(f32[8,128]{1,0:T(8,128)S(1)} %get-tuple-element.24.refs_0_), channel_id=1, source_target_pairs={{0,4},{4,0},{8,12},{12,8},{1,5},{5,1},{9,13},{13,9},{2,6},{6,2},{1... | collective-permute-start | bytes 12296 | tf_op jit(solution)/shard_map/ppermute | solution.py:248
  53.3 1.4 %collective-permute-start.13 = (f32[8,128]{1,0:T(8,128)S(1)}, f32[8,128]{1,0:T(8,128)S(1)}, u32[]{:S(2)}, u32[]{:S(2)}) collective-permute-start(f32[8,128]{1,0:T(8,128)S(1)} %get-tuple-element.24.refs_0_), channel_id=1, source_target_pairs={{0,12},{4,8},{8,4},{12,0},{1,13},{5,9},{9,5},{13,1},{2,14},{6,10},... | collective-permute-start | bytes 12296 | tf_op jit(solution)/shard_map/ppermute | solution.py:248
  54.7 2.2 %collective-permute-done.12.refs_2_ = f32[8,128]{1,0:T(8,128)S(1)} collective-permute-done((f32[8,128]{1,0:T(8,128)S(1)}, f32[8,128]{1,0:T(8,128)S(1)}, u32[]{:S(2)}, u32[]{:S(2)}) %collective-permute-start.12) | collective-permute-done | bytes 4128 | tf_op jit(solution)/shard_map/ppermute | solution.py:248
  57.5 1.9 %normalise.1 = f32[64,256]{1,0:T(8,128)} custom-call(f32[64,256]{1,0:T(8,128)} %copy-done.7, f32[64,256]{1,0:T(8,128)} %copy-done.8, f32[8,128]{1,0:T(8,128)} %copy-done.10, f32[8,128]{1,0:T(8,128)} %copy-done.11, f32[8,128]{1,0:T(8,128)} %copy-done.12, f32[8,128]{1,0:T(8,128)} %copy-done.13), custom_call_target="tpu_custom_call" | custom-call | tf_op jit(solution)/shard_map/normalise/pallas_call | solution.py:346
  (41 shorter events, 1.9 us)
Async XLA Ops:
  0.0 21.3 %copy-start.4 = (f32[384,256]{1,0:T(8,128)S(1)}, f32[384,256]{1,0:T(8,128)}, u32[]{:S(2)}) copy-start(f32[384,256]{1,0:T(8,128)} %refs_1_.2) | copy-start | bytes 1179652
  3.5 5.6 %collective-permute-start.5 = (f32[136,128]{1,0:T(8,128)S(1)}, f32[136,128]{1,0:T(8,128)S(1)}, u32[]{:S(2)}, u32[]{:S(2)}) collective-permute-start(f32[136,128]{1,0:T(8,128)S(1)} %concatenate.3.refs_9_), channel_id=1, source_target_pairs={{0,1},{1,0},{2,3},{3,2},{4,5},{5,4},{6,7},{7,6},{8,9},{9,8},{10,11... | collective-permute-start | bytes 208904 | tf_op jit(solution)/shard_map/ppermute | solution.py:248
  6.5 7.5 %collective-permute-start.6 = (f32[136,128]{1,0:T(8,128)S(1)}, f32[136,128]{1,0:T(8,128)S(1)}, u32[]{:S(2)}, u32[]{:S(2)}) collective-permute-start(f32[136,128]{1,0:T(8,128)S(1)} %concatenate.3.refs_9_), channel_id=1, source_target_pairs={{0,2},{1,3},{2,0},{3,1},{4,6},{5,7},{6,4},{7,5},{8,10},{9,11},{10,... | collective-permute-start | bytes 208904 | tf_op jit(solution)/shard_map/ppermute | solution.py:248
  9.1 6.2 %collective-permute-start.7 = (f32[136,128]{1,0:T(8,128)S(1)}, f32[136,128]{1,0:T(8,128)S(1)}, u32[]{:S(2)}, u32[]{:S(2)}) collective-permute-start(f32[136,128]{1,0:T(8,128)S(1)} %concatenate.3.refs_9_), channel_id=1, source_target_pairs={{0,3},{1,2},{2,1},{3,0},{4,7},{5,6},{6,5},{7,4},{8,11},{9,10},{10,... | collective-permute-start | bytes 208904 | tf_op jit(solution)/shard_map/ppermute | solution.py:248
  15.3 12.6 %copy-start = (bf16[384,256]{1,0:T(8,128)(2,1)S(1)}, bf16[384,256]{1,0:T(8,128)(2,1)}, u32[]{:S(2)}) copy-start(bf16[384,256]{1,0:T(8,128)(2,1)} %constant.20.clone.refs_5_.refs_3_) | copy-start | bytes 589828
  15.3 12.6 %copy-start.1 = (bf16[256,384]{1,0:T(8,128)(2,1)S(1)}, bf16[256,384]{1,0:T(8,128)(2,1)}, u32[]{:S(2)}) copy-start(bf16[256,384]{1,0:T(8,128)(2,1)} %constant.21.clone.refs_6_.refs_4_) | copy-start | bytes 589828
  15.3 12.6 %copy-start.2 = (bf16[128,768]{1,0:T(8,128)(2,1)S(1)}, bf16[128,768]{1,0:T(8,128)(2,1)}, u32[]{:S(2)}) copy-start(bf16[128,768]{1,0:T(8,128)(2,1)} %constant.22.clone.refs_7_.refs_5_) | copy-start | bytes 589828
  15.3 12.5 %copy-start.3 = (bf16[768,128]{1,0:T(8,128)(2,1)S(1)}, bf16[768,128]{1,0:T(8,128)(2,1)}, u32[]{:S(2)}) copy-start(bf16[768,128]{1,0:T(8,128)(2,1)} %constant.23.clone.refs_8_.refs_6_) | copy-start | bytes 589828
  15.4 5.9 %collective-permute-start.8 = (f32[3,136,128]{2,1,0:T(8,128)S(1)}, f32[3,136,128]{2,1,0:T(8,128)S(1)}, u32[]{:S(2)}, u32[]{:S(2)}) collective-permute-start(f32[3,136,128]{2,1,0:T(8,128)S(1)} %pad_maximum_fusion.refs_7_), channel_id=1, source_target_pairs={{0,8},{4,12},{8,0},{12,4},{1,9},{5,13},{9,1},{13,5},{2,10},{6,14},... | collective-permute-start | bytes 626696 | tf_op jit(solution)/shard_map/ppermute | solution.py:248
  16.9 6.9 %collective-permute-start.2 = (f32[136,128]{1,0:T(8,128)S(1)}, f32[136,128]{1,0:T(8,128)S(1)}, u32[]{:S(2)}, u32[]{:S(2)}) collective-permute-start(f32[136,128]{1,0:T(8,128)S(1)} %concatenate.3.refs_9_), channel_id=1, source_target_pairs={{0,8},{4,12},{8,0},{12,4},{1,9},{5,13},{9,1},{13,5},{2,10},{6,14},... | collective-permute-start | bytes 208904 | tf_op jit(solution)/shard_map/ppermute | solution.py:248
  17.4 7.7 %collective-permute-start.3 = (f32[136,128]{1,0:T(8,128)S(1)}, f32[136,128]{1,0:T(8,128)S(1)}, u32[]{:S(2)}, u32[]{:S(2)}) collective-permute-start(f32[136,128]{1,0:T(8,128)S(1)} %concatenate.3.refs_9_), channel_id=1, source_target_pairs={{0,4},{4,0},{8,12},{12,8},{1,5},{5,1},{9,13},{13,9},{2,6},{6,2},{1... | collective-permute-start | bytes 208904 | tf_op jit(solution)/shard_map/ppermute | solution.py:252
  17.4 23.8 %collective-permute-start.9 = (f32[3,136,128]{2,1,0:T(8,128)S(1)}, f32[3,136,128]{2,1,0:T(8,128)S(1)}, u32[]{:S(2)}, u32[]{:S(2)}) collective-permute-start(f32[3,136,128]{2,1,0:T(8,128)S(1)} %pad_maximum_fusion.refs_7_), channel_id=1, source_target_pairs={{0,4},{4,0},{8,12},{12,8},{1,5},{5,1},{9,13},{13,9},{2,6},{6,2},{1... | collective-permute-start | bytes 626696 | tf_op jit(solution)/shard_map/ppermute | solution.py:252
  21.3 20.0 %collective-permute-start.10 = (f32[3,136,128]{2,1,0:T(8,128)S(1)}, f32[3,136,128]{2,1,0:T(8,128)S(1)}, u32[]{:S(2)}, u32[]{:S(2)}) collective-permute-start(f32[3,136,128]{2,1,0:T(8,128)S(1)} %collective-permute-done.8.refs_7_), channel_id=1, source_target_pairs={{0,4},{4,0},{8,12},{12,8},{1,5},{5,1},{9,13},{13,9},{2,6},{6,2},{1... | collective-permute-start | bytes 626696 | tf_op jit(solution)/shard_map/ppermute | solution.py:252
  21.4 5.6 %collective-permute-start = (f32[384,64]{1,0:T(8,128)S(1)}, f32[384,64]{1,0:T(8,128)S(1)}, u32[]{:S(2)}, u32[]{:S(2)}) collective-permute-start(f32[384,64]{1,0:T(8,128)S(1)} %get-tuple-element.26), channel_id=1, source_target_pairs={{0,4},{4,8},{8,12},{1,5},{5,9},{9,13},{2,6},{6,10},{10,14},{3,7},{... | collective-permute-start | bytes 294920 | tf_op jit(solution)/shard_map/ppermute | solution.py:258
  23.8 4.0 %collective-permute-start.1 = (f32[384,64]{1,0:T(8,128)S(1)}, f32[384,64]{1,0:T(8,128)S(1)}, u32[]{:S(2)}, u32[]{:S(2)}) collective-permute-start(f32[384,64]{1,0:T(8,128)S(1)} %get-tuple-element.25), channel_id=1, source_target_pairs={{4,0},{8,4},{12,8},{5,1},{9,5},{13,9},{6,2},{10,6},{14,10},{7,3},{... | collective-permute-start | bytes 294920 | tf_op jit(solution)/shard_map/ppermute | solution.py:259
  25.1 2.7 %collective-permute-start.4 = (f32[136,128]{1,0:T(8,128)S(1)}, f32[136,128]{1,0:T(8,128)S(1)}, u32[]{:S(2)}, u32[]{:S(2)}) collective-permute-start(f32[136,128]{1,0:T(8,128)S(1)} %collective-permute-done.2.refs_10_), channel_id=1, source_target_pairs={{0,4},{4,0},{8,12},{12,8},{1,5},{5,1},{9,13},{13,9},{2,6},{6,2},{1... | collective-permute-start | bytes 208904 | tf_op jit(solution)/shard_map/ppermute | solution.py:252
  27.9 1.0 %copy-start.5 = (bf16[768,256]{1,0:T(8,128)(2,1)S(1)}, bf16[768,256]{1,0:T(8,128)(2,1)}, u32[]{:S(2)}) copy-start(bf16[768,256]{1,0:T(8,128)(2,1)} %constant.18.clone.refs_3_) | copy-start | bytes 1179652
  28.9 1.0 %copy-start.6 = (bf16[256,768]{1,0:T(8,128)(2,1)S(1)}, bf16[256,768]{1,0:T(8,128)(2,1)}, u32[]{:S(2)}) copy-start(bf16[256,768]{1,0:T(8,128)(2,1)} %constant.19.clone.refs_4_) | copy-start | bytes 1179652
  38.0 3.3 %copy-start.9 = (s32[16,16]{1,0:T(8,128)S(1)}, s32[16,16]{1,0:T(8,128)}, u32[]{:S(2)}) copy-start(s32[16,16]{1,0:T(8,128)} %refs_1_.3) | copy-start | bytes 3076
  49.2 7.7 %copy-start.10 = (f32[8,128]{1,0:T(8,128)}, f32[8,128]{1,0:T(8,128)S(1)}, u32[]{:S(2)}) copy-start(f32[8,128]{1,0:T(8,128)S(1)} %get-tuple-element.24.refs_0_) | copy-start | bytes 12292
  49.2 5.4 %collective-permute-start.11 = (f32[8,128]{1,0:T(8,128)S(1)}, f32[8,128]{1,0:T(8,128)S(1)}, u32[]{:S(2)}, u32[]{:S(2)}) collective-permute-start(f32[8,128]{1,0:T(8,128)S(1)} %get-tuple-element.24.refs_0_), channel_id=1, source_target_pairs={{0,4},{4,0},{8,12},{12,8},{1,5},{5,1},{9,13},{13,9},{2,6},{6,2},{1... | collective-permute-start | bytes 12296 | tf_op jit(solution)/shard_map/ppermute | solution.py:248
  53.3 3.6 %collective-permute-start.12 = (f32[8,128]{1,0:T(8,128)S(1)}, f32[8,128]{1,0:T(8,128)S(1)}, u32[]{:S(2)}, u32[]{:S(2)}) collective-permute-start(f32[8,128]{1,0:T(8,128)S(1)} %get-tuple-element.24.refs_0_), channel_id=1, source_target_pairs={{0,8},{4,12},{8,0},{12,4},{1,9},{5,13},{9,1},{13,5},{2,10},{6,14},... | collective-permute-start | bytes 12296 | tf_op jit(solution)/shard_map/ppermute | solution.py:248
  53.3 3.6 %collective-permute-start.13 = (f32[8,128]{1,0:T(8,128)S(1)}, f32[8,128]{1,0:T(8,128)S(1)}, u32[]{:S(2)}, u32[]{:S(2)}) collective-permute-start(f32[8,128]{1,0:T(8,128)S(1)} %get-tuple-element.24.refs_0_), channel_id=1, source_target_pairs={{0,12},{4,8},{8,4},{12,0},{1,13},{5,9},{9,5},{13,1},{2,14},{6,10},... | collective-permute-start | bytes 12296 | tf_op jit(solution)/shard_map/ppermute | solution.py:248
  54.7 2.3 %copy-start.11 = (f32[8,128]{1,0:T(8,128)}, f32[8,128]{1,0:T(8,128)S(1)}, u32[]{:S(2)}) copy-start(f32[8,128]{1,0:T(8,128)S(1)} %collective-permute-done.11.refs_1_) | copy-start | bytes 12292
  (4 other events, 2.4 us)
where the time goes:
time: 59.7 us; the launch traced here: 59.4 us
  Pallas kernels  19.9 us (33%)
  starting transfers between devices  19.2 us (32%)
  waiting for transfers between devices  12.7 us (21%)
  local copies, waits for them, and re-layouts  5.41 us (9%)
  other arithmetic  1.32 us (2%)
  between operations  0.89 us (1%)
    ppermute x8, starting transfers between devices, peer(): return lax.ppermute(x, axis, pairs)  13.1 us
    ppermute x8, waiting for transfers between devices, peer(): return lax.ppermute(x, axis, pairs)  11.8 us
    pallas_call x1, Pallas kernels, body(): pl.pallas_call(functools.partial(last_kernel, len(group), share), out_sha...  6.69 us
    pallas_call x2, Pallas kernels, body(): pl.pallas_call(functools.partial(next_kernel, len(group)), out_shape=(pla...  6.55 us
    pallas_call x1, Pallas kernels, body(): pl.pallas_call(functools.partial(first_kernel, len(mine)), out_shape=(spe...  4.79 us
    unnamed x28, local copies, waits for them, and re-layouts  3.84 us
    ppermute x1, starting transfers between devices, halo(): left = lax.ppermute(own[:, own.shape[1] - GUARD:], axis, up)  2.42 us
    ppermute x4, starting transfers between devices, swap(): lax.ppermute(x, axis, [(i, i ^ 1) for i in range(lax.axis_size(axis))])  2.33 us
  transfers between devices with their start and end apart: 14, of which 6 were waited for; matrix products, arithmetic and copies ran while one was open for 0% of the time, Pallas kernels for 19%

commit v1 on v0

v1 whole, which is shorter than its diff:
```python
import functools
import math

import jax
import jax.numpy as jnp
import ml_dtypes
import numpy as np
from jax import lax
from jax.experimental import pallas as pl
from jax.experimental.pallas import tpu as pltpu
from jax.sharding import PartitionSpec as P

GUARD = 64
MBLK = 16
LANES = 128
PACK = 8
BARRIER = True

F32 = jnp.float32
BF16 = jnp.bfloat16
VMEM = pl.BlockSpec(memory_space=pltpu.VMEM)
SMEM = pl.BlockSpec(memory_space=pltpu.SMEM)


def params(mib):
    return pltpu.CompilerParams(vmem_limit_bytes=mib * 2**20)


def high_low(table):
    high = table.astype(np.float32).astype(ml_dtypes.bfloat16)
    low = (table - high.astype(np.float64)).astype(np.float32).astype(ml_dtypes.bfloat16)
    return high, low


def tables(side):
    span = 2 * side
    angles = np.outer(np.arange(span), 2.0 * math.pi * (np.arange(side) + 0.5) / span)
    high, low = high_low(np.concatenate([np.cos(angles), np.sin(angles)], axis=1))
    return np.concatenate([high, low, high.T, low.T], axis=0)


def tall(tab_ref, part, count):
    span = tab_ref.shape[1]
    high = tab_ref[part * span : part * span + count, :]
    low = tab_ref[(part + 1) * span : (part + 1) * span + count, :]
    return jnp.concatenate([high, high, low], axis=0)


def wide(tab_ref, part, rows, cols):
    span = tab_ref.shape[1]
    high = tab_ref[part * span : part * span + rows, 0:cols]
    low = tab_ref[(part + 1) * span : (part + 1) * span + rows, 0:cols]
    return jnp.concatenate([high, high, low], axis=1)


def back_cols(tab_ref, side):
    span = tab_ref.shape[1]
    high = tab_ref[2 * span : 3 * span, 0:side]
    low = tab_ref[3 * span : 4 * span, 0:side]
    return jnp.concatenate([high, high, low], axis=0)


def split(x):
    high = x.astype(BF16)
    return high, (x - high.astype(F32)).astype(BF16)


def tripled(x, axis):
    high, low = split(x)
    return jnp.concatenate([high, low, high], axis=axis)


def product(left, right):
    return jnp.dot(left, right, preferred_element_type=F32)


def paired(quads, side):
    cc, cs = quads[:side, :side], quads[:side, side:]
    sc, ss = quads[side:, :side], quads[side:, side:]
    return cc - ss, sc + cs, cc + ss, sc - cs


def image_spectra(odd_ref, inner_ref, own_ref, outer_ref, tab_ref, spec_ref):
    odd = odd_ref[0] == 1
    inner, outer = inner_ref[...], outer_ref[...]
    left, right = jnp.where(odd, inner, outer), jnp.where(odd, outer, inner)
    image = jnp.concatenate([left, own_ref[...], right], axis=1)
    side = spec_ref.shape[-1]
    span = 2 * side
    rows, cols = image.shape[0] // side - 1, image.shape[1] // side - 1
    scale = 2.0 / (span * span)
    cols_table, rows_table = tall(tab_ref, 0, span), wide(tab_ref, 2, span, span)
    for q in range(cols):
        half = product(tripled(image[:, q * side : q * side + span], 1), cols_table)
        for p in range(rows):
            full = product(rows_table, tripled(half[p * side : p * side + span], 0))
            for part, value in enumerate(paired(full, side)):
                spec_ref[p * cols + q, part] = value * scale


def correlate(spec_ref, patches, tab_ref, half_ref, patch_ref, score_ref):
    side = spec_ref.shape[-1]
    span = 2 * side
    patch_cols, patch_rows = tall(tab_ref, 0, side), wide(tab_ref, 2, span, side)
    rows_table, cols_table = wide(tab_ref, 0, side, span), back_cols(tab_ref, side)
    count = len(patches)
    cols = score_ref.shape[2] // side
    for first in range(0, count, 4):
        group = patches[first : first + 4]
        half = product(tripled(jnp.concatenate(group, axis=0), 1), patch_cols)
        for i in range(len(group)):
            high, low = split(half[i * side : (i + 1) * side])
            half_ref[first + i, 0:side] = high
            half_ref[first + i, side : 2 * side] = low
            half_ref[first + i, 2 * side : 3 * side] = high

    def finish_patch(n, carry):
        for part, value in enumerate(paired(product(patch_rows, half_ref[n]), side)):
            patch_ref[n, part] = value
        return carry

    def score(n, carry):
        tr, tu, sr, si = (patch_ref[n, part] for part in range(4))
        for block in range(spec_ref.shape[0]):
            p, q = divmod(block, cols)
            ir, iu, jr, ji = (spec_ref[block, part] for part in range(4))
            a, b = ir * tr + iu * tu, iu * tr - ir * tu
            c, e = jr * sr + ji * si, jr * si - ji * sr
            top = jnp.concatenate([a + c, e + b], axis=1)
            low = jnp.concatenate([b - e, c - a], axis=1)
            lines = product(rows_table, tripled(jnp.concatenate([top, low], axis=0), 0))
            score_ref[n, p * side : (p + 1) * side, q * side : (q + 1) * side] = product(
                tripled(lines, 1), cols_table
            )
        return carry

    unroll = max(u for u in (1, 2, 3, 4) if count % u == 0)
    lax.fori_loop(0, count, finish_patch, 0, unroll=unroll)
    lax.fori_loop(0, count, score, 0, unroll=unroll)


STRIP = 64


def fold(score_ref, weights, state, out):
    def strip(r, carry):
        rows = pl.ds(pl.multiple_of(r * STRIP, STRIP), STRIP)
        values = [score_ref[n, rows, :] + weight for n, weight in enumerate(weights)]
        top = values[0]
        for value in values[1:]:
            top = jnp.maximum(top, value)
        if state:
            old_top, old_sum = state[0][rows, :], state[1][rows, :]
            top = jnp.maximum(top, old_top)
        total = jnp.exp(values[0] - top)
        for value in values[1:]:
            total = total + jnp.exp(value - top)
        if state:
            total = total + old_sum * jnp.exp(old_top - top)
        out(rows, top, total)
        return carry

    lax.fori_loop(0, score_ref.shape[1] // STRIP, strip, 0, unroll=True)


def unpack(refs, side):
    patches, weights = [], []
    for ref in refs:
        places = [()] if len(ref.shape) == 2 else [(i,) for i in range(ref.shape[0])]
        for place in places:
            patches.append(ref[place + (slice(0, side), slice(None))])
            weights.append(ref[place + (slice(side, side + 1), slice(0, 1))])
    return patches, weights


def first_kernel(n_in, *refs):
    packs = refs[5 : 5 + n_in]
    spec_ref, top_ref, sum_ref, half_ref, patch_ref, score_ref = refs[5 + n_in :]
    image_spectra(*refs[:5], spec_ref)
    score_kernel(packs, spec_ref, (), refs[4], top_ref, sum_ref, half_ref, patch_ref, score_ref)


def score_kernel(packs, spec_ref, state, tab_ref, top_ref, sum_ref, half_ref, patch_ref, score_ref):
    patches, weights = unpack(packs, spec_ref.shape[-1])
    correlate(spec_ref, patches, tab_ref, half_ref, patch_ref, score_ref)

    def out(rows, top, total):
        top_ref[rows, :] = top
        sum_ref[rows, :] = total

    fold(score_ref, weights, state, out)


def next_kernel(n_state, n_in, *refs):
    spec_ref, state, tab_ref = refs[0], refs[1 : 1 + n_state], refs[1 + n_state]
    score_kernel(refs[2 + n_state : 2 + n_state + n_in], spec_ref, state, tab_ref, *refs[2 + n_state + n_in :])


def unmasked_pixels(mask_ref):
    blocks = (1.0 - mask_ref[...].astype(F32)).astype(BF16)
    rows, cols = blocks.shape

    def spread(count, axis):
        shape = (count * MBLK, count) if axis == 0 else (count, count * MBLK)
        pixel = lax.broadcasted_iota(jnp.int32, shape, axis)
        block = lax.broadcasted_iota(jnp.int32, shape, 1 - axis)
        return ((pixel >= block * MBLK) & (pixel < (block + 1) * MBLK)).astype(F32).astype(BF16)

    return product(product(spread(rows, 0), blocks).astype(BF16), spread(cols, 1))


def last_kernel(n_in, share, *refs):
    place_ref, mask_ref, spec_ref, old_top, old_sum, tab_ref = refs[:6]
    packs = refs[6 : 6 + n_in]
    part_ref, open_ref, stat_ref, half_ref, patch_ref, score_ref, log_ref, pixel_ref = refs[6 + n_in :]
    patches, weights = unpack(packs, spec_ref.shape[-1])
    correlate(spec_ref, patches, tab_ref, half_ref, patch_ref, score_ref)

    def out(rows, top, total):
        log_ref[rows, :] = top + jnp.log(total)

    fold(score_ref, weights, (old_top, old_sum), out)
    pixels = unmasked_pixels(mask_ref)
    pixel_ref[...] = pixels
    values = log_ref[...]
    count = jnp.sum(pixels)
    total = jnp.sum(pixels * values)
    deviation = values - total / jnp.maximum(count, 1.0)
    squares = jnp.sum(pixels * deviation * deviation)
    lane = lax.broadcasted_iota(jnp.int32, stat_ref.shape, 1)
    stat_ref[...] = jnp.where(lane == 0, count, jnp.where(lane == 1, total, squares))
    own = pl.ds(pl.multiple_of(place_ref[0] * share, share), share)
    part_ref[...] = log_ref[own, :]
    open_ref[...] = pixel_ref[own, :]


def norm_kernel(part_ref, open_ref, *refs):
    stats, out_ref = refs[:-1], refs[-1]
    counts = [ref[:, 0:1] for ref in stats]
    totals = [ref[:, 1:2] for ref in stats]
    count, total = sum(counts), sum(totals)
    average = total / count
    squares = 0.0
    for ref, n, s in zip(stats, counts, totals):
        apart = s / jnp.maximum(n, 1.0) - average
        squares = squares + ref[:, 2:3] + n * apart * apart
    scale = 1.0 / jnp.sqrt(squares / count + 1e-05)
    out_ref[...] = open_ref[...] * (part_ref[...] - average[0:1]) * scale[0:1]


def peer(x, axis, step):
    n = lax.axis_size(axis)
    if n & (n - 1):
        pairs = [(i, (i + step) % n) for i in range(n)]
    else:
        pairs = [(i, i ^ step) for i in range(n)]
    return lax.ppermute(x, axis, pairs)


def swap(x, axis):
    return lax.ppermute(x, axis, [(i, i ^ 1) for i in range(lax.axis_size(axis))])


def halo(own, axis):
    n = lax.axis_size(axis)
    odd = lax.axis_index(axis) % 2 == 1
    first, last = own[:, :GUARD], own[:, own.shape[1] - GUARD :]

    def exchange(edge, start):
        pairs = [(i, i + 1) for i in range(start, n - 1, 2)]
        return lax.ppermute(edge, axis, pairs + [(j, i) for i, j in pairs])

    return exchange(jnp.where(odd, first, last), 0), exchange(jnp.where(odd, last, first), 1)


def pack_kernel(ids_ref, weight_ref, patch_ref, pack_ref):
    side = patch_ref.shape[0]
    pack_ref[0:side, :] = patch_ref[...]
    catalog = lax.broadcasted_iota(jnp.int32, weight_ref.shape, 1)
    weight = jnp.sum(jnp.where(catalog == ids_ref[...], weight_ref[...], 0.0), axis=1, keepdims=True)
    pack_ref[side:, :] = jnp.broadcast_to(weight, (PACK, side))


def cost(micros):
    return pl.CostEstimate(flops=int(micros * 1e9), bytes_accessed=0, transcendentals=0)


def body(micrograph, templates, orient_ids, log_weight, ice_mask):
    side = templates.shape[2]
    tile = micrograph.shape[1]
    blocks = (tile // side) ** 2
    tab = jnp.asarray(tables(side))
    place = lax.axis_index("orient").astype(jnp.int32).reshape(1)
    pack = pl.pallas_call(
        pack_kernel,
        out_shape=jax.ShapeDtypeStruct((side + PACK, side), F32),
        in_specs=[VMEM] * 3,
        out_specs=VMEM,
        compiler_params=params(60),
        cost_estimate=cost(1),
        name="pack_weight",
    )(orient_ids, log_weight.reshape(1, -1), templates.reshape(side, side))

    n_tile, n_orient = lax.axis_size("tile"), lax.axis_size("orient")
    far = [peer(pack, "orient", k) for k in range(1, n_orient)]
    inner, outer = halo(micrograph, "tile")
    even = n_tile % 2 == 0
    steps = range(2, n_tile, 2) if even else range(1, n_tile)
    mine = [pack] + [peer(pack, "tile", k) for k in steps]
    if even:
        mine += [swap(x, "tile") for x in mine]
    odd = (lax.axis_index("tile") % 2).astype(jnp.int32).reshape(1)

    plane = jax.ShapeDtypeStruct((tile, tile), F32)

    def scratch(n):
        return [
            pltpu.VMEM((n, 3 * side, 2 * side), BF16),
            pltpu.VMEM((n, 4, side, side), F32),
            pltpu.VMEM((n, tile, tile), F32),
        ]

    def size(group):
        return sum(x.shape[0] if x.ndim == 3 else 1 for x in group)

    spec, *state = pl.pallas_call(
        functools.partial(first_kernel, len(mine)),
        out_shape=(jax.ShapeDtypeStruct((blocks, 4, side, side), F32), plane, plane),
        in_specs=[SMEM] + [VMEM] * (4 + len(mine)),
        out_specs=(VMEM,) * 3,
        scratch_shapes=scratch(len(mine)),
        compiler_params=params(24),
        cost_estimate=cost(5),
        name="own_block",
    )(odd, inner, micrograph, outer, tab, *mine)

    def score(state, arrays):
        return pl.pallas_call(
            functools.partial(next_kernel, len(state), len(arrays)),
            out_shape=(plane, plane),
            in_specs=[VMEM] * (2 + len(state) + len(arrays)),
            out_specs=(VMEM,) * 2,
            scratch_shapes=scratch(size(arrays)),
            compiler_params=params(24),
            cost_estimate=cost(size(arrays)),
            name="next_block",
        )(spec, *state, tab, *arrays)

    if BARRIER:
        far, state = lax.optimization_barrier((far, state))
    held = jnp.stack(far)
    near = [peer(held, "tile", k) for k in steps]
    state = score(state, [held, swap(held, "tile")] if even else [held])
    if near:
        near, state = lax.optimization_barrier((near, state))
    groups = [[x, swap(x, "tile")] if even else [x] for x in near]
    for group in groups[:-1]:
        state = score(state, group)
    top, total = state
    group = groups[-1]
    share = tile // n_orient
    part = jax.ShapeDtypeStruct((share, tile), F32)
    part, opened, stat = pl.pallas_call(
        functools.partial(last_kernel, len(group), share),
        out_shape=(part, part, jax.ShapeDtypeStruct((8, LANES), F32)),
        in_specs=[SMEM] + [VMEM] * (5 + len(group)),
        out_specs=(VMEM,) * 3,
        scratch_shapes=scratch(size(group)) + [pltpu.VMEM((tile, tile), F32)] * 2,
        compiler_params=params(24),
        cost_estimate=cost(size(group)),
        name="last_block",
    )(place, ice_mask, spec, top, total, tab, *group)
    stats = [stat] + [peer(stat, "tile", k) for k in range(1, n_tile)]
    return pl.pallas_call(
        norm_kernel,
        out_shape=jax.ShapeDtypeStruct((share, tile), F32),
        in_specs=[VMEM] * (2 + len(stats)),
        out_specs=VMEM,
        compiler_params=params(4),
        cost_estimate=cost(1),
        name="normalise",
    )(part, opened, *stats)


def solution(mesh):
    return jax.shard_map(
        body,
        mesh=mesh,
        in_specs=(
            P("group", "tile"),
            P("orient", "tile", None, None),
            P("orient", "tile"),
            P(),
            P("group", "tile"),
        ),
        out_specs=P(("group", "orient"), "tile"),
        check_vma=False,
    )
```

time: 59.7 us -> 39.5 us (0.66)
  waiting for transfers between devices: 12.7 us -> 5.65 us
  local copies, waits for them, and re-layouts: 5.41 us -> 0.02 us
  starting transfers between devices: 19.2 us -> 14.5 us
  Pallas kernels: 19.9 us -> 18.3 us
  other arithmetic: 1.32 us -> 0.14 us
    ppermute x8, waiting for transfers between devices: 11.8 us -> 4.18 us  [peer(): return lax.ppermute(x, axis, pairs)]
    unnamed x28 -> x8, local copies, waits for them, and re-layouts: 3.84 us -> 0.02 us
    ppermute x4, starting transfers between devices: 2.33 us -> 0.55 us  [swap(): lax.ppermute(x, axis, [(i, i ^ 1) for i in range(lax.axis_size(axis))])]
    ppermute x2, starting transfers between devices: 3.71 us -> 2.23 us  [exchange(): return lax.ppermute(edge, axis, pairs + [(j, i) for i, j in pairs])]
    concatenate x1 -> x0, local copies, waits for them, and re-layouts: 1.45 us -> none  [body(): jnp.concatenate([templates[0, 0], jnp.full((PACK, side), weight, F32)], a...]
    ppermute x8, starting transfers between devices: 13.1 us -> 11.8 us  [peer(): return lax.ppermute(x, axis, pairs)]
    ppermute x4, waiting for transfers between devices: 0.11 us -> 1.46 us  [swap(): lax.ppermute(x, axis, [(i, i ^ 1) for i in range(lax.axis_size(axis))])]
    reduce_sum x1 -> x0, other arithmetic: 1.3 us -> none  [body(): weight = jnp.sum(jnp.where(catalog == orient_ids[0, 0], log_weight, 0.0))]
  transfers between devices with their start and end apart: 14 -> 14, of which waited for: 6 -> 5; matrix products, arithmetic and copies ran while one was open for 0% -> 0% of each run, Pallas kernels for 19% -> 25%
where the time goes in v1:
time: 39.5 us; the launch traced here: 39.4 us
  Pallas kernels  18.3 us (46%)
  starting transfers between devices  14.5 us (37%)
  waiting for transfers between devices  5.65 us (14%)
  between operations  0.74 us (2%)
    ppermute x8, starting transfers between devices, peer(): return lax.ppermute(x, axis, pairs)  11.8 us
    pallas_call x1, Pallas kernels, body(): pl.pallas_call(functools.partial(last_kernel, len(group), share), out_sha...  5.89 us
    pallas_call x1, Pallas kernels, score(): pl.pallas_call(functools.partial(next_kernel, len(state), len(arrays)), o...  5.43 us
    pallas_call x1, Pallas kernels, body(): pl.pallas_call(functools.partial(first_kernel, len(mine)), out_shape=(jax...  4.29 us
    ppermute x8, waiting for transfers between devices, peer(): return lax.ppermute(x, axis, pairs)  4.18 us
    ppermute x2, starting transfers between devices, exchange(): return lax.ppermute(edge, axis, pairs + [(j, i) for i, j in pairs])  2.23 us
    pallas_call x1, Pallas kernels, body(): pl.pallas_call(pack_kernel, out_shape=jax.ShapeDtypeStruct((side + PACK,...  1.68 us
    ppermute x4, waiting for transfers between devices, swap(): lax.ppermute(x, axis, [(i, i ^ 1) for i in range(lax.axis_size(axis))])  1.46 us
  transfers between devices with their start and end apart: 14, of which 5 were waited for; matrix products, arithmetic and copies ran while one was open for 0% of the time, Pallas kernels for 25%

profile of v1, /device:TPU:0, one launch (start us, length us, event | category | flops | bytes accessed | tf_op | source)
XLA Modules:
  0.0 39.4 jit_solution(7830348737242759808)
XLA Ops:
  0.7 1.7 %pack_weight.1.refs_5_ = f32[136,128]{1,0:T(8,128)} custom-call(s32[1,1]{1,0:T(1,128)S(6)} %copy.7.ids_ref, f32[1,16]{1,0:T(1,128)} %bitcast.11, f32[128,128]{1,0:T(8,128)} %bitcast.10), custom_call_target="tpu_custom_call" | custom-call | flops 1000000000 | tf_op jit(solution)/shard_map/pack_weight/pallas_call | solution.py:294
  2.3 3.0 %collective-permute-start.2 = (f32[136,128]{1,0:T(8,128)}, f32[136,128]{1,0:T(8,128)S(1)}, u32[]{:S(2)}, u32[]{:S(2)}) collective-permute-start(f32[136,128]{1,0:T(8,128)} %pack_weight.1.refs_5_), channel_id=1, source_target_pairs={{0,8},{4,12},{8,0},{12,4},{1,9},{5,13},{9,1},{13,5},{2,10},{6,14},... | collective-permute-start | bytes 208904 | tf_op jit(solution)/shard_map/ppermute | solution.py:257
  5.3 0.1 slice_select_fusion
  5.4 0.7 %collective-permute-start.1 = (f32[384,64]{1,0:T(8,128)S(1)}, f32[384,64]{1,0:T(8,128)S(1)}, u32[]{:S(2)}, u32[]{:S(2)}) collective-permute-start(f32[384,64]{1,0:T(8,128)S(1)} %get-tuple-element.37), channel_id=1, source_target_pairs={{4,8},{8,4},{5,9},{9,5},{6,10},{10,6},{7,11},{11,7},{20,24},{24,20... | collective-permute-start | bytes 294920 | tf_op jit(solution)/shard_map/ppermute | solution.py:271
  6.1 1.6 %collective-permute-start = (f32[384,64]{1,0:T(8,128)S(1)}, f32[384,64]{1,0:T(8,128)S(1)}, u32[]{:S(2)}, u32[]{:S(2)}) collective-permute-start(f32[384,64]{1,0:T(8,128)S(1)} %get-tuple-element.38), channel_id=1, source_target_pairs={{0,4},{8,12},{4,0},{12,8},{1,5},{9,13},{5,1},{13,9},{2,6},{10,14},... | collective-permute-start | bytes 294920 | tf_op jit(solution)/shard_map/ppermute | solution.py:271
  7.7 0.1 collective-permute-start.3
  7.8 0.0 collective-permute-done.2.refs_6_
  7.8 0.4 collective-permute-start.4
  8.2 4.0 %collective-permute-start.7 = (f32[136,128]{1,0:T(8,128)S(1)}, f32[136,128]{1,0:T(8,128)S(1)}, u32[]{:S(2)}, u32[]{:S(2)}) collective-permute-start(f32[136,128]{1,0:T(8,128)S(1)} %copy-done.1), channel_id=1, source_target_pairs={{0,3},{1,2},{2,1},{3,0},{4,7},{5,6},{6,5},{7,4},{8,11},{9,10},{10,... | collective-permute-start | bytes 208904 | tf_op jit(solution)/shard_map/ppermute | solution.py:257
  12.2 1.3 %collective-permute-start.5 = (f32[136,128]{1,0:T(8,128)S(1)}, f32[136,128]{1,0:T(8,128)S(1)}, u32[]{:S(2)}, u32[]{:S(2)}) collective-permute-start(f32[136,128]{1,0:T(8,128)S(1)} %copy-done.1), channel_id=1, source_target_pairs={{0,1},{1,0},{2,3},{3,2},{4,5},{5,4},{6,7},{7,6},{8,9},{9,8},{10,11... | collective-permute-start | bytes 208904 | tf_op jit(solution)/shard_map/ppermute | solution.py:257
  13.5 4.3 %own_block.1 = (f32[4,4,128,128]{3,2,1,0:T(8,128)S(1)}, f32[256,256]{1,0:T(8,128)S(1)}, f32[256,256]{1,0:T(8,128)S(1)}) custom-call(s32[1]{0:T(128)} %bitcast.1.refs_0_, f32[384,64]{1,0:T(8,128)S(1)} %collective-permute-done.refs_1_, f32[384,256]{1,0:T(8,128)S(1)} %copy-done, f32[384,64]{1,0:T(8,128)S(1)} %collective-permute-done.1.refs_3_, ...), custom_call_target="tpu_custom_call" | custom-call | flops 5000000000 | tf_op jit(solution)/shard_map/own_block/pallas_call | solution.py:326
  17.8 0.6 %collective-permute-done.6 = f32[136,128]{1,0:T(8,128)S(1)} collective-permute-done((f32[136,128]{1,0:T(8,128)S(1)}, f32[136,128]{1,0:T(8,128)S(1)}, u32[]{:S(2)}, u32[]{:S(2)}) %collective-permute-start.6) | collective-permute-done | bytes 69664 | tf_op jit(solution)/shard_map/ppermute | solution.py:257
  18.4 0.1 collective-permute-start.9
  18.5 1.6 %collective-permute-start.8 = (f32[3,136,128]{2,1,0:T(8,128)S(1)}, f32[3,136,128]{2,1,0:T(8,128)S(1)}, u32[]{:S(2)}, u32[]{:S(2)}) collective-permute-start(f32[3,136,128]{2,1,0:T(8,128)S(1)} %pad_maximum_fusion.refs_4_), channel_id=1, source_target_pairs={{0,8},{4,12},{8,0},{12,4},{1,9},{5,13},{9,1},{13,5},{2,10},{6,14},... | collective-permute-start | bytes 626696 | tf_op jit(solution)/shard_map/ppermute | solution.py:257
  20.1 5.4 %next_block.1 = (f32[256,256]{1,0:T(8,128)S(1)}, f32[256,256]{1,0:T(8,128)S(1)}) custom-call(f32[4,4,128,128]{3,2,1,0:T(8,128)S(1)} %get-tuple-element.21.refs_0_.refs_2_, f32[256,256]{1,0:T(8,128)S(1)} %get-tuple-element.27.refs_1_, f32[256,256]{1,0:T(8,128)S(1)} %get-tuple-element.28.refs_2_, bf16[1024,256]{1,0:T(8,128)(2,1)S(1)} %copy-done.3, ...), custom_call_target="tpu_custom_call" | custom-call | flops 6000000000 | tf_op jit(solution)/shard_map/next_block/pallas_call | solution.py:338
  25.5 0.5 %collective-permute-done.8.refs_6_ = f32[3,136,128]{2,1,0:T(8,128)S(1)} collective-permute-done((f32[3,136,128]{2,1,0:T(8,128)S(1)}, f32[3,136,128]{2,1,0:T(8,128)S(1)}, u32[]{:S(2)}, u32[]{:S(2)}) %collective-permute-start.8) | collective-permute-done | bytes 208928 | tf_op jit(solution)/shard_map/ppermute | solution.py:257
  26.1 1.5 %collective-permute-done.10.refs_7_ = f32[3,136,128]{2,1,0:T(8,128)S(1)} collective-permute-done((f32[3,136,128]{2,1,0:T(8,128)S(1)}, f32[3,136,128]{2,1,0:T(8,128)S(1)}, u32[]{:S(2)}, u32[]{:S(2)}) %collective-permute-start.10) | collective-permute-done | bytes 208928 | tf_op jit(solution)/shard_map/ppermute | solution.py:261
  27.5 5.9 %last_block.1 = (f32[64,256]{1,0:T(8,128)S(1)}, f32[64,256]{1,0:T(8,128)S(1)}, f32[8,128]{1,0:T(8,128)S(1)}) custom-call(s32[1]{0:T(128)} %bitcast.refs_0_, s32[16,16]{1,0:T(8,128)S(1)} %copy-done.2, f32[4,4,128,128]{3,2,1,0:T(8,128)S(1)} %get-tuple-element.21.refs_0_.refs_2_, f32[256,256]{1,0:T(8,128)S(1)} %get-tuple-element.31.refs_3_, ...), custom_call_target="tpu_custom_call" | custom-call | flops 6000000000 | tf_op jit(solution)/shard_map/last_block/pallas_call | solution.py:363
  33.4 1.3 %collective-permute-start.13 = (f32[8,128]{1,0:T(8,128)S(1)}, f32[8,128]{1,0:T(8,128)S(1)}, u32[]{:S(2)}, u32[]{:S(2)}) collective-permute-start(f32[8,128]{1,0:T(8,128)S(1)} %get-tuple-element.36.refs_0_), channel_id=1, source_target_pairs={{0,12},{4,8},{8,4},{12,0},{1,13},{5,9},{9,5},{13,1},{2,14},{6,10},... | collective-permute-start | bytes 12296 | tf_op jit(solution)/shard_map/ppermute | solution.py:257
  34.8 0.5 %collective-permute-start.12 = (f32[8,128]{1,0:T(8,128)S(1)}, f32[8,128]{1,0:T(8,128)S(1)}, u32[]{:S(2)}, u32[]{:S(2)}) collective-permute-start(f32[8,128]{1,0:T(8,128)S(1)} %get-tuple-element.36.refs_0_), channel_id=1, source_target_pairs={{0,8},{4,12},{8,0},{12,4},{1,9},{5,13},{9,1},{13,5},{2,10},{6,14},... | collective-permute-start | bytes 12296 | tf_op jit(solution)/shard_map/ppermute | solution.py:257
  35.3 0.1 collective-permute-start.11
  35.4 1.2 %collective-permute-done.13.refs_3_ = f32[8,128]{1,0:T(8,128)S(1)} collective-permute-done((f32[8,128]{1,0:T(8,128)S(1)}, f32[8,128]{1,0:T(8,128)S(1)}, u32[]{:S(2)}, u32[]{:S(2)}) %collective-permute-start.13) | collective-permute-done | bytes 4128 | tf_op jit(solution)/shard_map/ppermute | solution.py:257
  36.5 1.8 %collective-permute-done.12.refs_2_ = f32[8,128]{1,0:T(8,128)S(1)} collective-permute-done((f32[8,128]{1,0:T(8,128)S(1)}, f32[8,128]{1,0:T(8,128)S(1)}, u32[]{:S(2)}, u32[]{:S(2)}) %collective-permute-start.12) | collective-permute-done | bytes 4128 | tf_op jit(solution)/shard_map/ppermute | solution.py:257
  38.4 1.0 %normalise.1 = f32[64,256]{1,0:T(8,128)} custom-call(f32[64,256]{1,0:T(8,128)S(1)} %get-tuple-element.34.part_ref, f32[64,256]{1,0:T(8,128)S(1)} %get-tuple-element.35.open_ref, f32[8,128]{1,0:T(8,128)S(1)} %get-tuple-element.36.refs_0_, f32[8,128]{1,0:T(8,128)S(1)} %collective-permute-done.11.refs_1_, f32[8,128]{1,0:T(8,128)S(1)} %collective-permute-done.12.refs_2_, ...), custom_call_target="tpu_custom_call" | custom-call | flops 1000000000 | tf_op jit(solution)/shard_map/normalise/pallas_call | solution.py:374
  (19 shorter events, 0.1 us)
Async XLA Ops:
  0.7 4.7 %copy-start = (f32[384,256]{1,0:T(8,128)S(1)}, f32[384,256]{1,0:T(8,128)}, u32[]{:S(2)}) copy-start(f32[384,256]{1,0:T(8,128)} %refs_2_.1) | copy-start | bytes 1179652
  2.3 11.2 %copy-start.3 = (bf16[1024,256]{1,0:T(8,128)(2,1)S(1)}, bf16[1024,256]{1,0:T(8,128)(2,1)}, u32[]{:S(2)}) copy-start(bf16[1024,256]{1,0:T(8,128)(2,1)} %constant.25.clone.refs_4_.refs_3_.refs_5_) | copy-start | bytes 1572868
  2.3 5.5 %collective-permute-start.2 = (f32[136,128]{1,0:T(8,128)}, f32[136,128]{1,0:T(8,128)S(1)}, u32[]{:S(2)}, u32[]{:S(2)}) collective-permute-start(f32[136,128]{1,0:T(8,128)} %pack_weight.1.refs_5_), channel_id=1, source_target_pairs={{0,8},{4,12},{8,0},{12,4},{1,9},{5,13},{9,1},{13,5},{2,10},{6,14},... | collective-permute-start | bytes 208904 | tf_op jit(solution)/shard_map/ppermute | solution.py:257
  5.3 2.4 %copy-start.1 = (f32[136,128]{1,0:T(8,128)S(1)}, f32[136,128]{1,0:T(8,128)}, u32[]{:S(2)}) copy-start(f32[136,128]{1,0:T(8,128)} %pack_weight.1.refs_5_) | copy-start | bytes 208900
  5.4 6.7 %collective-permute-start.1 = (f32[384,64]{1,0:T(8,128)S(1)}, f32[384,64]{1,0:T(8,128)S(1)}, u32[]{:S(2)}, u32[]{:S(2)}) collective-permute-start(f32[384,64]{1,0:T(8,128)S(1)} %get-tuple-element.37), channel_id=1, source_target_pairs={{4,8},{8,4},{5,9},{9,5},{6,10},{10,6},{7,11},{11,7},{20,24},{24,20... | collective-permute-start | bytes 294920 | tf_op jit(solution)/shard_map/ppermute | solution.py:271
  6.1 7.4 %collective-permute-start = (f32[384,64]{1,0:T(8,128)S(1)}, f32[384,64]{1,0:T(8,128)S(1)}, u32[]{:S(2)}, u32[]{:S(2)}) collective-permute-start(f32[384,64]{1,0:T(8,128)S(1)} %get-tuple-element.38), channel_id=1, source_target_pairs={{0,4},{8,12},{4,0},{12,8},{1,5},{9,13},{5,1},{13,9},{2,6},{10,14},... | collective-permute-start | bytes 294920 | tf_op jit(solution)/shard_map/ppermute | solution.py:271
  7.7 4.5 %collective-permute-start.3 = (f32[136,128]{1,0:T(8,128)S(1)}, f32[136,128]{1,0:T(8,128)S(1)}, u32[]{:S(2)}, u32[]{:S(2)}) collective-permute-start(f32[136,128]{1,0:T(8,128)S(1)} %copy-done.1), channel_id=1, source_target_pairs={{0,4},{4,0},{8,12},{12,8},{1,5},{5,1},{9,13},{13,9},{2,6},{6,2},{1... | collective-permute-start | bytes 208904 | tf_op jit(solution)/shard_map/ppermute | solution.py:261
  7.8 5.7 %collective-permute-start.4 = (f32[136,128]{1,0:T(8,128)S(1)}, f32[136,128]{1,0:T(8,128)S(1)}, u32[]{:S(2)}, u32[]{:S(2)}) collective-permute-start(f32[136,128]{1,0:T(8,128)S(1)} %collective-permute-done.2.refs_6_), channel_id=1, source_target_pairs={{0,4},{4,0},{8,12},{12,8},{1,5},{5,1},{9,13},{13,9},{2,6},{6,2},{1... | collective-permute-start | bytes 208904 | tf_op jit(solution)/shard_map/ppermute | solution.py:261
  8.2 9.6 %collective-permute-start.7 = (f32[136,128]{1,0:T(8,128)S(1)}, f32[136,128]{1,0:T(8,128)S(1)}, u32[]{:S(2)}, u32[]{:S(2)}) collective-permute-start(f32[136,128]{1,0:T(8,128)S(1)} %copy-done.1), channel_id=1, source_target_pairs={{0,3},{1,2},{2,1},{3,0},{4,7},{5,6},{6,5},{7,4},{8,11},{9,10},{10,... | collective-permute-start | bytes 208904 | tf_op jit(solution)/shard_map/ppermute | solution.py:257
  12.2 6.2 %collective-permute-start.6 = (f32[136,128]{1,0:T(8,128)S(1)}, f32[136,128]{1,0:T(8,128)S(1)}, u32[]{:S(2)}, u32[]{:S(2)}) collective-permute-start(f32[136,128]{1,0:T(8,128)S(1)} %copy-done.1), channel_id=1, source_target_pairs={{0,2},{1,3},{2,0},{3,1},{4,6},{5,7},{6,4},{7,5},{8,10},{9,11},{10,... | collective-permute-start | bytes 208904 | tf_op jit(solution)/shard_map/ppermute | solution.py:257
  12.2 6.2 %collective-permute-start.5 = (f32[136,128]{1,0:T(8,128)S(1)}, f32[136,128]{1,0:T(8,128)S(1)}, u32[]{:S(2)}, u32[]{:S(2)}) collective-permute-start(f32[136,128]{1,0:T(8,128)S(1)} %copy-done.1), channel_id=1, source_target_pairs={{0,1},{1,0},{2,3},{3,2},{4,5},{5,4},{6,7},{7,6},{8,9},{9,8},{10,11... | collective-permute-start | bytes 208904 | tf_op jit(solution)/shard_map/ppermute | solution.py:257
  18.4 1.7 %collective-permute-start.9 = (f32[3,136,128]{2,1,0:T(8,128)S(1)}, f32[3,136,128]{2,1,0:T(8,128)S(1)}, u32[]{:S(2)}, u32[]{:S(2)}) collective-permute-start(f32[3,136,128]{2,1,0:T(8,128)S(1)} %pad_maximum_fusion.refs_4_), channel_id=1, source_target_pairs={{0,4},{4,0},{8,12},{12,8},{1,5},{5,1},{9,13},{13,9},{2,6},{6,2},{1... | collective-permute-start | bytes 626696 | tf_op jit(solution)/shard_map/ppermute | solution.py:261
  18.5 7.6 %collective-permute-start.8 = (f32[3,136,128]{2,1,0:T(8,128)S(1)}, f32[3,136,128]{2,1,0:T(8,128)S(1)}, u32[]{:S(2)}, u32[]{:S(2)}) collective-permute-start(f32[3,136,128]{2,1,0:T(8,128)S(1)} %pad_maximum_fusion.refs_4_), channel_id=1, source_target_pairs={{0,8},{4,12},{8,0},{12,4},{1,9},{5,13},{9,1},{13,5},{2,10},{6,14},... | collective-permute-start | bytes 626696 | tf_op jit(solution)/shard_map/ppermute | solution.py:257
  25.5 2.0 %copy-start.2 = (s32[16,16]{1,0:T(8,128)S(1)}, s32[16,16]{1,0:T(8,128)}, u32[]{:S(2)}) copy-start(s32[16,16]{1,0:T(8,128)} %refs_1_.1) | copy-start | bytes 3076
  26.1 1.5 %collective-permute-start.10 = (f32[3,136,128]{2,1,0:T(8,128)S(1)}, f32[3,136,128]{2,1,0:T(8,128)S(1)}, u32[]{:S(2)}, u32[]{:S(2)}) collective-permute-start(f32[3,136,128]{2,1,0:T(8,128)S(1)} %collective-permute-done.8.refs_6_), channel_id=1, source_target_pairs={{0,4},{4,0},{8,12},{12,8},{1,5},{5,1},{9,13},{13,9},{2,6},{6,2},{1... | collective-permute-start | bytes 626696 | tf_op jit(solution)/shard_map/ppermute | solution.py:261
  33.4 3.1 %collective-permute-start.13 = (f32[8,128]{1,0:T(8,128)S(1)}, f32[8,128]{1,0:T(8,128)S(1)}, u32[]{:S(2)}, u32[]{:S(2)}) collective-permute-start(f32[8,128]{1,0:T(8,128)S(1)} %get-tuple-element.36.refs_0_), channel_id=1, source_target_pairs={{0,12},{4,8},{8,4},{12,0},{1,13},{5,9},{9,5},{13,1},{2,14},{6,10},... | collective-permute-start | bytes 12296 | tf_op jit(solution)/shard_map/ppermute | solution.py:257
  34.8 3.6 %collective-permute-start.12 = (f32[8,128]{1,0:T(8,128)S(1)}, f32[8,128]{1,0:T(8,128)S(1)}, u32[]{:S(2)}, u32[]{:S(2)}) collective-permute-start(f32[8,128]{1,0:T(8,128)S(1)} %get-tuple-element.36.refs_0_), channel_id=1, source_target_pairs={{0,8},{4,12},{8,0},{12,4},{1,9},{5,13},{9,1},{13,5},{2,10},{6,14},... | collective-permute-start | bytes 12296 | tf_op jit(solution)/shard_map/ppermute | solution.py:257
  35.3 3.1 %collective-permute-start.11 = (f32[8,128]{1,0:T(8,128)S(1)}, f32[8,128]{1,0:T(8,128)S(1)}, u32[]{:S(2)}, u32[]{:S(2)}) collective-permute-start(f32[8,128]{1,0:T(8,128)S(1)} %get-tuple-element.36.refs_0_), channel_id=1, source_target_pairs={{0,4},{4,0},{8,12},{12,8},{1,5},{5,1},{9,13},{13,9},{2,6},{6,2},{1... | collective-permute-start | bytes 12296 | tf_op jit(solution)/shard_map/ppermute | solution.py:257

commit v2 on v1

v2 whole, which is shorter than its diff:
```python
import functools
import math

import jax
import jax.numpy as jnp
import ml_dtypes
import numpy as np
from jax import lax
from jax.experimental import pallas as pl
from jax.experimental.pallas import tpu as pltpu
from jax.sharding import PartitionSpec as P

GUARD = 64
MBLK = 16
LANES = 128
PACK = 8
CHUNK = 8
COST = 0.1

F32 = jnp.float32
BF16 = jnp.bfloat16
VMEM = pl.BlockSpec(memory_space=pltpu.VMEM)
SMEM = pl.BlockSpec(memory_space=pltpu.SMEM)


def params(mib):
    return pltpu.CompilerParams(vmem_limit_bytes=mib * 2**20)


def high_low(table):
    high = table.astype(np.float32).astype(ml_dtypes.bfloat16)
    low = (table - high.astype(np.float64)).astype(np.float32).astype(ml_dtypes.bfloat16)
    return high, low


def tables(side):
    span = 2 * side
    turn = 2.0 * math.pi * (np.arange(side) + 0.5) / span
    angles = np.outer(np.arange(span), turn)
    high, low = high_low(np.concatenate([np.cos(angles), np.sin(angles)], axis=1))
    middle = np.outer(np.arange(span) - (side - 1) / 2, turn)
    middle_high, middle_low = high_low(np.concatenate([np.cos(middle), np.sin(middle)], axis=1).T)
    away = np.outer(np.arange(side // 2) + 0.5, turn)
    ends = []
    for wave in (np.cos(away), np.sin(away)):
        wave_high, wave_low = high_low(wave)
        ends += [np.concatenate([wave_high, wave_high], axis=1), np.concatenate([wave_low, wave_low], axis=1)]
    return np.concatenate([high, low, high.T, low.T, *ends, middle_high, middle_low], axis=0)


def tall(tab_ref, count):
    span = tab_ref.shape[1]
    high, low = tab_ref[0:count, :], tab_ref[span : span + count, :]
    return jnp.concatenate([high, high, low], axis=0)


def wide(high, low):
    return jnp.concatenate([high, high, low], axis=1)


def back_cols(tab_ref, side):
    span = tab_ref.shape[1]
    both = jnp.concatenate([tab_ref[2 * span : 3 * span, 0:side], tab_ref[3 * span : 4 * span, 0:side]], axis=1)
    return jnp.concatenate([both, both], axis=0)


def split(x):
    high = x.astype(BF16)
    return high, (x - high.astype(F32)).astype(BF16)


def tripled(x, axis):
    high, low = split(x)
    return jnp.concatenate([high, low, high], axis=axis)


def doubled(x, axis):
    return jnp.concatenate(split(x), axis=axis)


def halves(x, axis):
    half = x.shape[axis] // 2
    return x[:half] + x[half:] if axis == 0 else x[:, :half] + x[:, half:]


def product(left, right):
    return jnp.dot(left, right, preferred_element_type=F32)


def paired(quads, side):
    cc, cs = quads[:side, :side], quads[:side, side:]
    sc, ss = quads[side:, :side], quads[side:, side:]
    return cc - ss, sc + cs, cc + ss, sc - cs


def image_spectra(spot_ref, inner_ref, own_ref, outer_ref, tab_ref, spec_ref):
    odd = spot_ref[0] % 2 == 1

    def edge(ref):
        lines = ref[...]
        return jnp.concatenate([lines[:, :GUARD], lines[:, GUARD:]], axis=0)

    inner, outer = edge(inner_ref), edge(outer_ref)
    left, right = jnp.where(odd, inner, outer), jnp.where(odd, outer, inner)
    image = jnp.concatenate([left, own_ref[...], right], axis=1)
    side = spec_ref.shape[-1]
    span = 2 * side
    rows, cols = image.shape[0] // side - 1, image.shape[1] // side - 1
    scale = 2.0 / (span * span)
    cols_table, rows_table = tall(tab_ref, span), wide(tab_ref[5 * span : 6 * span, :], tab_ref[6 * span :, :])
    for q in range(cols):
        half = product(tripled(image[:, q * side : q * side + span], 1), cols_table)
        for p in range(rows):
            full = product(rows_table, tripled(half[p * side : p * side + span], 0))
            for part, value in enumerate(paired(full, side)):
                spec_ref[p * cols + q, part] = value * scale


def transform(patches, tab_ref, half_ref, patch_ref):
    side = patch_ref.shape[-1]
    span = 2 * side
    patch_cols = tall(tab_ref, side)
    patch_rows = wide(tab_ref[2 * span : 3 * span, 0:side], tab_ref[3 * span : 4 * span, 0:side])
    for first in range(0, len(patches), 4):
        group = patches[first : first + 4]
        half = product(tripled(jnp.concatenate(group, axis=0), 1), patch_cols)
        for i in range(len(group)):
            high, low = split(half[i * side : (i + 1) * side])
            half_ref[first + i, 0:side] = high
            half_ref[first + i, side : 2 * side] = low
            half_ref[first + i, 2 * side : 3 * side] = high

    def finish(n, carry):
        for part, value in enumerate(paired(product(patch_rows, half_ref[n]), side)):
            patch_ref[n, part] = value
        return carry

    lax.fori_loop(0, len(patches), finish, 0, unroll=steps_at_once(len(patches), 8))


def steps_at_once(count, most):
    return max(u for u in range(1, most + 1) if count % u == 0)


def correlate(spec_ref, tab_ref, patch_ref, strips, score_ref):
    side = spec_ref.shape[-1]
    span = 2 * side
    cols = score_ref.shape[2] // side
    even_rows, odd_rows = tab_ref[4 * span : 4 * span + side, :], tab_ref[4 * span + side : 5 * span, :]
    cols_table = back_cols(tab_ref, side)

    def score(n, carry):
        tr, tu, sr, si = (patch_ref[n, part] for part in range(4))
        for p, strip in enumerate(strips):
            for q in range(cols):
                ir, iu, jr, ji = (spec_ref[strip * cols + q, part] for part in range(4))
                a, b = ir * tr + iu * tu, iu * tr - ir * tu
                c, e = jr * sr + ji * si, jr * si - ji * sr
                top = jnp.concatenate([a + c, e + b], axis=1)
                low = jnp.concatenate([b - e, c - a], axis=1)
                even = halves(product(even_rows, doubled(top, 0)), 0)
                odd = halves(product(odd_rows, doubled(low, 0)), 0)
                lines = jnp.concatenate([even + odd, even - odd], axis=0)
                score_ref[n, p * side : (p + 1) * side, q * side : (q + 1) * side] = halves(
                    product(doubled(lines, 1), cols_table), 1
                )
        return carry

    count = score_ref.shape[0]
    lax.fori_loop(0, count, score, 0, unroll=steps_at_once(count, 24 // (cols * len(strips))))


STRIP = 64


def fold(score_ref, weights, state, start, out):
    def strip(r, carry):
        first = pl.multiple_of(r * STRIP, STRIP)
        rows, whole = pl.ds(first, STRIP), pl.ds(first + start, STRIP)
        values = [score_ref[n, rows, :] + weight for n, weight in enumerate(weights)]
        top = values[0]
        for value in values[1:]:
            top = jnp.maximum(top, value)
        if state:
            old_top, old_sum = state[0][whole, :], state[1][whole, :]
            top = jnp.maximum(top, old_top)
        total = jnp.exp(values[0] - top)
        for value in values[1:]:
            total = total + jnp.exp(value - top)
        if state:
            total = total + old_sum * jnp.exp(old_top - top)
        if len(out) == 1:
            out[0][rows, :] = top + jnp.log(total)
        else:
            out[0][rows, :] = top
            out[1][rows, :] = total
        return carry

    lax.fori_loop(0, score_ref.shape[1] // STRIP, strip, 0, unroll=True)


def unpack(refs, side):
    patches, weights = [], []
    for ref in refs:
        places = [()] if len(ref.shape) == 2 else [(i,) for i in range(ref.shape[0])]
        for place in places:
            patches.append(ref[place + (slice(0, side), slice(None))])
            weights.append(ref[place + (slice(side, side + 1), slice(0, 1))])
    return patches, weights


def all_strips(spec_ref, score_ref):
    return range(score_ref.shape[1] // spec_ref.shape[-1])


def first_kernel(n_in, *refs):
    tab_ref, packs = refs[4], refs[5 : 5 + n_in]
    spec_ref, *out, half_ref, patch_ref, score_ref = refs[5 + n_in :]
    image_spectra(*refs[:5], spec_ref)
    patches, weights = unpack(packs, spec_ref.shape[-1])
    transform(patches, tab_ref, half_ref, patch_ref)
    correlate(spec_ref, tab_ref, patch_ref, all_strips(spec_ref, score_ref), score_ref)
    fold(score_ref, weights, (), 0, out)


def next_kernel(n_in, *refs):
    spec_ref, *state, tab_ref = refs[:4]
    packs, (*out, half_ref, patch_ref, score_ref) = refs[4 : 4 + n_in], refs[4 + n_in :]
    patches, weights = unpack(packs, spec_ref.shape[-1])
    transform(patches, tab_ref, half_ref, patch_ref)
    correlate(spec_ref, tab_ref, patch_ref, all_strips(spec_ref, score_ref), score_ref)
    fold(score_ref, weights, state, 0, out)


def strip_kernel(n_in, strip, *refs):
    spec_ref, *state, tab_ref = refs[:4]
    packs, refs = refs[4 : 4 + n_in], refs[4 + n_in :]
    side = spec_ref.shape[-1]
    patches, weights = unpack(packs, side)
    if strip == 0:
        log_ref, patch_ref, half_ref, score_ref = refs
        transform(patches, tab_ref, half_ref, patch_ref)
    else:
        patch_ref, log_ref, score_ref = refs
    correlate(spec_ref, tab_ref, patch_ref, [strip], score_ref)
    fold(score_ref, weights, state, strip * side, [log_ref])


def folded(stored, side):
    within = stored % side
    return stored - within + jnp.where(within < side // 2, within + side // 2, side - 1 - within)


def keeper(row, side):
    within = row % side
    return row - within + jnp.where(within < side // 2, side - 1 - within, within - side // 2)


def pixel_kernel(side, mask_ref, pixel_ref):
    blocks = (1.0 - mask_ref[...].astype(F32)).astype(BF16)
    rows, cols = blocks.shape
    pixel = folded(lax.broadcasted_iota(jnp.int32, (rows * MBLK, rows), 0), side)
    block = lax.broadcasted_iota(jnp.int32, (rows * MBLK, rows), 1)
    down = (pixel // MBLK == block).astype(F32).astype(BF16)
    pixel = lax.broadcasted_iota(jnp.int32, (cols, cols * MBLK), 1)
    block = lax.broadcasted_iota(jnp.int32, (cols, cols * MBLK), 0)
    across = (pixel // MBLK == block).astype(F32).astype(BF16)
    pixel_ref[...] = product(product(down, blocks).astype(BF16), across)


def join_kernel(n_strip, *refs):
    parts, (pixel_ref, log_ref, stat_ref) = refs[:-3], refs[-3:]
    values = jnp.concatenate([ref[...] for ref in parts[:n_strip]], axis=0)
    if len(parts) > n_strip:
        other = jnp.concatenate([ref[...] for ref in parts[n_strip:]], axis=0)
        top = jnp.maximum(values, other)
        values = top + jnp.log(1.0 + jnp.exp(jnp.minimum(values, other) - top))
    log_ref[...] = values
    pixels = pixel_ref[...]
    count = jnp.sum(pixels)
    total = jnp.sum(pixels * values)
    deviation = values - total / jnp.maximum(count, 1.0)
    squares = jnp.sum(pixels * deviation * deviation)
    lane = lax.broadcasted_iota(jnp.int32, stat_ref.shape, 1)
    stat_ref[...] = jnp.where(lane == 0, count, jnp.where(lane == 1, total, squares))


def own_rows_kernel(side, place_ref, log_ref, pixel_ref, part_ref, open_ref):
    share = part_ref.shape[0]

    def unfold(i, carry):
        row = keeper(place_ref[0] * share + i, side)
        part_ref[pl.ds(i, 1), :] = log_ref[pl.ds(row, 1), :]
        open_ref[pl.ds(i, 1), :] = pixel_ref[pl.ds(row, 1), :]
        return carry

    lax.fori_loop(0, share, unfold, 0, unroll=8)


def norm_kernel(part_ref, open_ref, *refs):
    stats, out_ref = refs[:-1], refs[-1]
    counts = [ref[:, 0:1] for ref in stats]
    totals = [ref[:, 1:2] for ref in stats]
    count, total = sum(counts), sum(totals)
    average = total / count
    squares = 0.0
    for ref, n, s in zip(stats, counts, totals):
        apart = s / jnp.maximum(n, 1.0) - average
        squares = squares + ref[:, 2:3] + n * apart * apart
    scale = 1.0 / jnp.sqrt(squares / count + 1e-05)
    out_ref[...] = open_ref[...] * (part_ref[...] - average[0:1]) * scale[0:1]


def shift(i, step, n):
    return i ^ step if n & (n - 1) == 0 else (i + step) % n


def peer(x, axis, step):
    n = lax.axis_size(axis)
    return lax.ppermute(x, axis, [(i, shift(i, step, n)) for i in range(n)])


def swap(x, axis):
    return lax.ppermute(x, axis, [(i, i ^ 1) for i in range(lax.axis_size(axis))])


def exchange(x, axis, start):
    pairs = [(i, i + 1) for i in range(start, lax.axis_size(axis) - 1, 2)]
    return lax.ppermute(x, axis, pairs + [(j, i) for i, j in pairs])


def pack_kernel(ids_ref, weight_ref, patch_ref, pack_ref, own_id, weights, sems):
    side = patch_ref.shape[0]
    pairs = ((patch_ref, pack_ref.at[0:side]), (weight_ref, weights), (ids_ref, own_id))
    copies = [pltpu.make_async_copy(source, target, sems.at[i]) for i, (source, target) in enumerate(pairs)]
    for copy in copies:
        copy.start()
    for copy in copies:
        copy.wait()
    catalog = lax.broadcasted_iota(jnp.int32, weights.shape, 1)
    weight = jnp.sum(jnp.where(catalog == own_id[...], weights[...], 0.0), axis=1, keepdims=True)
    pack_ref[side:, :] = jnp.broadcast_to(weight, (PACK, side))


def edge_kernel(spot_ref, own_ref, tab_ref, inner_ref, outer_ref):
    half = own_ref.shape[0] // 2
    own = own_ref[...]
    edges = [own[:, :GUARD], own[:, own.shape[1] - GUARD :]]
    left, right = [jnp.concatenate([x[:half], x[half:]], axis=1) for x in edges]
    odd = spot_ref[0] % 2 == 1
    inner_ref[...] = jnp.where(odd, left, right)
    outer_ref[...] = jnp.where(odd, right, left)


def stack_kernel(*refs):
    for i, ref in enumerate(refs[:-1]):
        refs[-1][i] = ref[...]


def cost(micros):
    return pl.CostEstimate(flops=int(micros * 1e9), bytes_accessed=0, transcendentals=0)


def body(micrograph, templates, orient_ids, log_weight, ice_mask):
    side = templates.shape[2]
    tile = micrograph.shape[1]
    blocks = (tile // side) ** 2
    tab = jnp.asarray(tables(side))
    n_tile, n_orient = lax.axis_size("tile"), lax.axis_size("orient")
    place = lax.axis_index("orient").astype(jnp.int32).reshape(1)
    spot = lax.axis_index("tile").astype(jnp.int32).reshape(1)
    pack = pl.pallas_call(
        pack_kernel,
        out_shape=jax.ShapeDtypeStruct((side + PACK, side), F32),
        in_specs=[pl.BlockSpec(memory_space=pl.ANY)] * 3,
        out_specs=VMEM,
        scratch_shapes=[
            pltpu.VMEM((1, 1), jnp.int32),
            pltpu.VMEM((1, log_weight.shape[0]), F32),
            pltpu.SemaphoreType.DMA((3,)),
        ],
        compiler_params=params(60),
        cost_estimate=cost(1),
        name="pack_weight",
    )(orient_ids, log_weight.reshape(1, -1), templates.reshape(side, side))
    micrograph, pack = lax.optimization_barrier((micrograph, pack))
    edge = jax.ShapeDtypeStruct((micrograph.shape[0] // 2, 2 * GUARD), F32)
    inner_edge, outer_edge = pl.pallas_call(
        edge_kernel,
        out_shape=(edge, edge),
        in_specs=[SMEM, VMEM, VMEM],
        out_specs=(VMEM, VMEM),
        compiler_params=params(4),
        cost_estimate=cost(0.5),
        name="edges",
    )(spot, micrograph, tab)

    tile_pairs, orient_pairs = n_tile % 2 == 0, n_orient % 2 == 0
    tile_steps = range(0, n_tile, 2 if tile_pairs else 1)
    orient_steps = range(0, n_orient, 2 if orient_pairs else 1)
    far = [peer(pack, "orient", o) for o in orient_steps[1:]]
    inner, outer = exchange(inner_edge, "tile", 0), exchange(outer_edge, "tile", 1)
    mine = [pack] + ([swap(pack, "tile")] if tile_pairs else [])
    held = pl.pallas_call(
        stack_kernel,
        out_shape=jax.ShapeDtypeStruct((1 + len(far), *pack.shape), F32),
        in_specs=[VMEM] * (1 + len(far)),
        out_specs=VMEM,
        compiler_params=params(4),
        cost_estimate=cost(0.2),
        name="stack_packs",
    )(pack, *far)
    near = [peer(held, "tile", t) for t in tile_steps[1:]]
    early = far + ([swap(x, "tile") for x in far] if tile_pairs else [])

    plane = jax.ShapeDtypeStruct((tile, tile), F32)

    half_shape, patch_shape = (3 * side, 2 * side), (4, side, side)

    def size(arrays):
        return sum(x.shape[0] if x.ndim == 3 else 1 for x in arrays)

    def scratch(n):
        return [pltpu.VMEM((n, *half_shape), BF16), pltpu.VMEM((n, *patch_shape), F32), pltpu.VMEM((n, tile, tile), F32)]

    spec, *state = pl.pallas_call(
        functools.partial(first_kernel, len(mine)),
        out_shape=(jax.ShapeDtypeStruct((blocks, 4, side, side), F32), plane, plane),
        in_specs=[SMEM] + [VMEM] * (4 + len(mine)),
        out_specs=(VMEM,) * 3,
        scratch_shapes=scratch(len(mine)),
        compiler_params=params(24),
        cost_estimate=cost(5 * COST),
        name="own_block",
    )(spot, inner, micrograph, outer, tab, *mine)
    early, state = lax.optimization_barrier((early, state))

    def score(state, arrays):
        count = size(arrays)
        return pl.pallas_call(
            functools.partial(next_kernel, len(arrays)),
            out_shape=(plane,) * 2,
            in_specs=[VMEM] * (4 + len(arrays)),
            out_specs=(VMEM,) * 2,
            scratch_shapes=scratch(count),
            compiler_params=params(24),
            cost_estimate=cost(COST * count),
            name="next_block",
        )(spec, *state, tab, *arrays)

    for i in range(0, len(early), CHUNK):
        state = score(state, early[i : i + CHUNK])
    if near:
        near, state = lax.optimization_barrier((near, state))
    rest = near + ([swap(x, "tile") for x in near] if tile_pairs else [])
    groups = [[]]
    for x in rest or [pack[None]]:
        if groups[-1] and size(groups[-1]) + size([x]) > CHUNK:
            groups.append([])
        groups[-1].append(x)
    for group in groups[:-1]:
        state = score(state, group)
    group = groups[-1]
    count = size(group)
    n_strip = tile // side
    strip_shape = jax.ShapeDtypeStruct((side, tile), F32)
    strip_scratch = pltpu.VMEM((count, side, tile), F32)
    log_map, *spectra = pl.pallas_call(
        functools.partial(strip_kernel, len(group), 0),
        out_shape=(strip_shape, jax.ShapeDtypeStruct((count, *patch_shape), F32)),
        in_specs=[VMEM] * (4 + len(group)),
        out_specs=(VMEM,) * 2,
        scratch_shapes=[pltpu.VMEM((count, *half_shape), BF16), strip_scratch],
        compiler_params=params(24),
        cost_estimate=cost(COST * count),
        name="first_strip",
    )(spec, *state, tab, *group)
    log_maps = [log_map]
    for strip in range(1, n_strip):
        log_maps.append(
            pl.pallas_call(
                functools.partial(strip_kernel, len(group), strip),
                out_shape=strip_shape,
                in_specs=[VMEM] * (5 + len(group)),
                out_specs=VMEM,
                scratch_shapes=[strip_scratch],
                compiler_params=params(24),
                cost_estimate=cost(COST * count),
                name="next_strip",
            )(spec, *state, tab, *group, *spectra)
        )
    maps = log_maps + ([swap(x, "orient") for x in log_maps] if orient_pairs else [])
    pixels = pl.pallas_call(
        functools.partial(pixel_kernel, side),
        out_shape=plane,
        in_specs=[VMEM],
        out_specs=VMEM,
        compiler_params=params(4),
        cost_estimate=cost(1),
        name="open_pixels",
    )(ice_mask)
    log_total, stat = pl.pallas_call(
        functools.partial(join_kernel, n_strip),
        out_shape=(plane, jax.ShapeDtypeStruct((8, LANES), F32)),
        in_specs=[VMEM] * (1 + len(maps)),
        out_specs=(VMEM,) * 2,
        compiler_params=params(8),
        cost_estimate=cost(1),
        name="join_maps",
    )(*maps, pixels)
    share = tile // n_orient
    part = jax.ShapeDtypeStruct((share, tile), F32)
    part, opened = pl.pallas_call(
        functools.partial(own_rows_kernel, side),
        out_shape=(part, part),
        in_specs=[SMEM, VMEM, VMEM],
        out_specs=(VMEM, VMEM),
        compiler_params=params(4),
        cost_estimate=cost(1),
        name="own_rows",
    )(place, log_total, pixels)
    stats = [stat] + [peer(stat, "tile", k) for k in range(1, n_tile)]
    return pl.pallas_call(
        norm_kernel,
        out_shape=jax.ShapeDtypeStruct((share, tile), F32),
        in_specs=[VMEM] * (2 + len(stats)),
        out_specs=VMEM,
        compiler_params=params(4),
        cost_estimate=cost(1),
        name="normalise",
    )(part, opened, *stats)


def solution(mesh):
    return jax.shard_map(
        body,
        mesh=mesh,
        in_specs=(
            P("group", "tile"),
            P("orient", "tile", None, None),
            P("orient", "tile"),
            P(),
            P("group", "tile"),
        ),
        out_specs=P(("group", "orient"), "tile"),
        check_vma=False,
    )
```

time: 39.5 us -> 35.4 us (0.90)
  Pallas kernels: 18.3 us -> 11.8 us
  waiting for transfers between devices: 5.65 us -> 11.1 us
  starting transfers between devices: 14.5 us -> 11.5 us
    ppermute x10 -> x7, starting transfers between devices: 14 us -> 8.56 us  [the longest x5 7.83 us: peer(): return lax.ppermute(x, axis, [(i, shift(i, step, n)) for i in range(n)])]
    ppermute x4 -> x5, waiting for transfers between devices: 1.46 us -> 6.68 us  [swap(): lax.ppermute(x, axis, [(i, i ^ 1) for i in range(lax.axis_size(axis))])]
    pallas_call x2 -> x8, Pallas kernels: 11.3 us -> 6.38 us  [the longest x1 1.88 us: body(): pl.pallas_call(functools.partial(strip_kernel, len(group), 0), out_shape=...]
    ppermute x4 -> x5, starting transfers between devices: 0.55 us -> 2.89 us  [swap(): lax.ppermute(x, axis, [(i, i ^ 1) for i in range(lax.axis_size(axis))])]
    pallas_call x1, Pallas kernels: 4.29 us -> 2.71 us  [body(): pl.pallas_call(functools.partial(first_kernel, len(mine)), out_shape=(jax...]
    ppermute x10 -> x7, waiting for transfers between devices: 4.19 us -> 4.43 us  [the longest x5 4.43 us: peer(): return lax.ppermute(x, axis, [(i, shift(i, step, n)) for i in range(n)])]
  transfers between devices with their start and end apart: 14 -> 12, of which waited for: 5 -> 6; matrix products, arithmetic and copies ran while one was open for 0% -> 0% of each run, Pallas kernels for 25% -> 19%
where the time goes in v2:
time: 35.4 us; the launch traced here: 35.2 us
  Pallas kernels  11.8 us (33%)
  starting transfers between devices  11.5 us (32%)
  waiting for transfers between devices  11.1 us (31%)
  between operations  0.79 us (2%)
    ppermute x5, starting transfers between devices, peer(): return lax.ppermute(x, axis, [(i, shift(i, step, n)) for i in range(n)])  7.83 us
    ppermute x5, waiting for transfers between devices, swap(): lax.ppermute(x, axis, [(i, i ^ 1) for i in range(lax.axis_size(axis))])  6.68 us
    ppermute x5, waiting for transfers between devices, peer(): return lax.ppermute(x, axis, [(i, shift(i, step, n)) for i in range(n)])  4.43 us
    ppermute x5, starting transfers between devices, swap(): lax.ppermute(x, axis, [(i, i ^ 1) for i in range(lax.axis_size(axis))])  2.89 us
    pallas_call x1, Pallas kernels, body(): pl.pallas_call(functools.partial(first_kernel, len(mine)), out_shape=(jax...  2.71 us
    pallas_call x1, Pallas kernels, body(): pl.pallas_call(functools.partial(strip_kernel, len(group), 0), out_shape=...  1.88 us
    pallas_call x1, Pallas kernels, score(): pl.pallas_call(functools.partial(next_kernel, len(arrays)), out_shape=(pl...  1.8 us
    pallas_call x1, Pallas kernels, body(): pl.pallas_call(pack_kernel, out_shape=jax.ShapeDtypeStruct((side + PACK,...  1.74 us
  transfers between devices with their start and end apart: 12, of which 6 were waited for; matrix products, arithmetic and copies ran while one was open for 0% of the time, Pallas kernels for 19%

profile of v2, /device:TPU:0, one launch (start us, length us, event | category | flops | bytes accessed | tf_op | source)
XLA Modules:
  0.0 35.2 jit_solution(7432895078511747369)
XLA Ops:
  0.7 1.7 %pack_weight.1.refs_5_.refs_0_ = f32[136,128]{1,0:T(8,128)} custom-call(s32[1,1]{1,0:T(1,128)S(6)} %copy.7.ids_ref, f32[1,16]{1,0:T(1,128)} %bitcast.5, f32[128,128]{1,0:T(8,128)} %bitcast.4), custom_call_target="tpu_custom_call" | custom-call | flops 1000000000 | tf_op jit(solution)/shard_map/pack_weight/pallas_call | solution.py:372
  2.4 4.1 %collective-permute-start.3 = (f32[136,128]{1,0:T(8,128)}, f32[136,128]{1,0:T(8,128)S(1)}, u32[]{:S(2)}, u32[]{:S(2)}) collective-permute-start(f32[136,128]{1,0:T(8,128)} %pack_weight.1.refs_5_.refs_0_), channel_id=1, source_target_pairs={{0,2},{1,3},{2,0},{3,1},{4,6},{5,7},{6,4},{7,5},{8,10},{9,11},{10,... | collective-permute-start | bytes 208904 | tf_op jit(solution)/shard_map/ppermute | solution.py:320
  6.7 0.7 %collective-permute-start.1 = (f32[192,128]{1,0:T(8,128)S(1)}, f32[192,128]{1,0:T(8,128)S(1)}, u32[]{:S(2)}, u32[]{:S(2)}) collective-permute-start(f32[192,128]{1,0:T(8,128)S(1)} %get-tuple-element.29), channel_id=1, source_target_pairs={{4,8},{8,4},{5,9},{9,5},{6,10},{10,6},{7,11},{11,7},{20,24},{24,20... | collective-permute-start | bytes 294920 | tf_op jit(solution)/shard_map/ppermute | solution.py:329
  7.4 3.1 %collective-permute-done.3.refs_1_.refs_4_ = f32[136,128]{1,0:T(8,128)S(1)} collective-permute-done((f32[136,128]{1,0:T(8,128)}, f32[136,128]{1,0:T(8,128)S(1)}, u32[]{:S(2)}, u32[]{:S(2)}) %collective-permute-start.3) | collective-permute-done | bytes 69664 | tf_op jit(solution)/shard_map/ppermute | solution.py:320
  10.5 1.8 %collective-permute-start.4 = (f32[2,136,128]{2,1,0:T(8,128)S(1)}, f32[2,136,128]{2,1,0:T(8,128)S(1)}, u32[]{:S(2)}, u32[]{:S(2)}) collective-permute-start(f32[2,136,128]{2,1,0:T(8,128)S(1)} %stack_packs.1), channel_id=1, source_target_pairs={{0,8},{4,12},{8,0},{12,4},{1,9},{5,13},{9,1},{13,5},{2,10},{6,14},... | collective-permute-start | bytes 417800 | tf_op jit(solution)/shard_map/ppermute | solution.py:320
  12.3 0.5 %collective-permute-start.5 = (f32[136,128]{1,0:T(8,128)S(1)}, f32[136,128]{1,0:T(8,128)S(1)}, u32[]{:S(2)}, u32[]{:S(2)}) collective-permute-start(f32[136,128]{1,0:T(8,128)S(1)} %collective-permute-done.3.refs_1_.refs_4_), channel_id=1, source_target_pairs={{0,4},{4,0},{8,12},{12,8},{1,5},{5,1},{9,13},{13,9},{2,6},{6,2},{1... | collective-permute-start | bytes 208904 | tf_op jit(solution)/shard_map/ppermute | solution.py:324
  12.8 0.7 %collective-permute-done.2.refs_6_ = f32[136,128]{1,0:T(8,128)S(1)} collective-permute-done((f32[136,128]{1,0:T(8,128)S(1)}, f32[136,128]{1,0:T(8,128)S(1)}, u32[]{:S(2)}, u32[]{:S(2)}) %collective-permute-start.2) | collective-permute-done | bytes 69664 | tf_op jit(solution)/shard_map/ppermute | solution.py:324
  13.6 2.7 %own_block.1 = (f32[4,4,128,128]{3,2,1,0:T(8,128)S(1)}, f32[256,256]{1,0:T(8,128)S(1)}, f32[256,256]{1,0:T(8,128)S(1)}) custom-call(s32[1]{0:T(128)} %bitcast.1.spot_ref.refs_0_, f32[192,128]{1,0:T(8,128)S(1)} %collective-permute-done.refs_1_, f32[384,256]{1,0:T(8,128)S(1)} %copy-done.1, f32[192,128]{1,0:T(8,128)S(1)} %collective-permute-done.1.refs_3_, ...), custom_call_target="tpu_custom_call" | custom-call | flops 500000000 | tf_op jit(solution)/shard_map/own_block/pallas_call | solution.py:426
  16.3 1.8 %next_block.1 = (f32[256,256]{1,0:T(8,128)S(1)}, f32[256,256]{1,0:T(8,128)S(1)}) custom-call(f32[4,4,128,128]{3,2,1,0:T(8,128)S(1)} %get-tuple-element.31.refs_0_, f32[256,256]{1,0:T(8,128)S(1)} %get-tuple-element.34.refs_1_, f32[256,256]{1,0:T(8,128)S(1)} %get-tuple-element.35.refs_2_, bf16[1792,256]{1,0:T(8,128)(2,1)S(1)} %copy-done, ...), custom_call_target="tpu_custom_call" | custom-call | flops 200000000 | tf_op jit(solution)/shard_map/next_block/pallas_call | solution.py:440
  18.1 0.2 collective-permute-start.6
  18.4 1.2 %collective-permute-done.6.refs_5_ = f32[2,136,128]{2,1,0:T(8,128)S(1)} collective-permute-done((f32[2,136,128]{2,1,0:T(8,128)S(1)}, f32[2,136,128]{2,1,0:T(8,128)S(1)}, u32[]{:S(2)}, u32[]{:S(2)}) %collective-permute-start.6) | collective-permute-done | bytes 139296 | tf_op jit(solution)/shard_map/ppermute | solution.py:324
  19.6 1.9 %first_strip.1 = (f32[128,256]{1,0:T(8,128)S(1)}, f32[4,4,128,128]{3,2,1,0:T(8,128)S(1)}) custom-call(f32[4,4,128,128]{3,2,1,0:T(8,128)S(1)} %get-tuple-element.31.refs_0_, f32[256,256]{1,0:T(8,128)S(1)} %get-tuple-element.40.refs_1_, f32[256,256]{1,0:T(8,128)S(1)} %get-tuple-element.41.refs_2_, bf16[1792,256]{1,0:T(8,128)(2,1)S(1)} %copy-done, ...), custom_call_target="tpu_custom_call" | custom-call | flops 400000000 | tf_op jit(solution)/shard_map/first_strip/pallas_call | solution.py:468
  21.5 1.2 %collective-permute-start.7 = (f32[128,256]{1,0:T(8,128)S(1)}, f32[128,256]{1,0:T(8,128)S(1)}, u32[]{:S(2)}, u32[]{:S(2)}) collective-permute-start(f32[128,256]{1,0:T(8,128)S(1)} %get-tuple-element.43.refs_0_), channel_id=1, source_target_pairs={{0,1},{1,0},{2,3},{3,2},{4,5},{5,4},{6,7},{7,6},{8,9},{9,8},{10,11... | collective-permute-start | bytes 393224 | tf_op jit(solution)/shard_map/ppermute | solution.py:324
  22.7 1.2 %next_strip.1.refs_1_ = f32[128,256]{1,0:T(8,128)S(1)} custom-call(f32[4,4,128,128]{3,2,1,0:T(8,128)S(1)} %get-tuple-element.31.refs_0_, f32[256,256]{1,0:T(8,128)S(1)} %get-tuple-element.40.refs_1_, f32[256,256]{1,0:T(8,128)S(1)} %get-tuple-element.41.refs_2_, bf16[1792,256]{1,0:T(8,128)(2,1)S(1)} %copy-done, ...), custom_call_target="tpu_custom_call" | custom-call | flops 400000000 | tf_op jit(solution)/shard_map/next_strip/pallas_call | solution.py:481
  23.9 0.9 %collective-permute-start.8 = (f32[128,256]{1,0:T(8,128)S(1)}, f32[128,256]{1,0:T(8,128)S(1)}, u32[]{:S(2)}, u32[]{:S(2)}) collective-permute-start(f32[128,256]{1,0:T(8,128)S(1)} %next_strip.1.refs_1_), channel_id=1, source_target_pairs={{0,1},{1,0},{2,3},{3,2},{4,5},{5,4},{6,7},{7,6},{8,9},{9,8},{10,11... | collective-permute-start | bytes 393224 | tf_op jit(solution)/shard_map/ppermute | solution.py:324
  24.8 0.3 open_pixels.1.refs_4_.pixel_ref
  25.2 2.3 %collective-permute-done.7.refs_2_ = f32[128,256]{1,0:T(8,128)S(1)} collective-permute-done((f32[128,256]{1,0:T(8,128)S(1)}, f32[128,256]{1,0:T(8,128)S(1)}, u32[]{:S(2)}, u32[]{:S(2)}) %collective-permute-start.7) | collective-permute-done | bytes 131104 | tf_op jit(solution)/shard_map/ppermute | solution.py:324
  27.5 2.4 %collective-permute-done.8.refs_3_ = f32[128,256]{1,0:T(8,128)S(1)} collective-permute-done((f32[128,256]{1,0:T(8,128)S(1)}, f32[128,256]{1,0:T(8,128)S(1)}, u32[]{:S(2)}, u32[]{:S(2)}) %collective-permute-start.8) | collective-permute-done | bytes 131104 | tf_op jit(solution)/shard_map/ppermute | solution.py:324
  29.9 0.5 %join_maps.1 = (f32[256,256]{1,0:T(8,128)S(1)}, f32[8,128]{1,0:T(8,128)S(1)}) custom-call(f32[128,256]{1,0:T(8,128)S(1)} %get-tuple-element.43.refs_0_, f32[128,256]{1,0:T(8,128)S(1)} %next_strip.1.refs_1_, f32[128,256]{1,0:T(8,128)S(1)} %collective-permute-done.7.refs_2_, f32[128,256]{1,0:T(8,128)S(1)} %collective-permute-done.8.refs_3_, ...), custom_call_target="tpu_custom_call" | custom-call | flops 1000000000 | tf_op jit(solution)/shard_map/join_maps/pallas_call | solution.py:502
  30.5 0.6 %collective-permute-start.10 = (f32[8,128]{1,0:T(8,128)S(1)}, f32[8,128]{1,0:T(8,128)S(1)}, u32[]{:S(2)}, u32[]{:S(2)}) collective-permute-start(f32[8,128]{1,0:T(8,128)S(1)} %get-tuple-element.48.refs_0_), channel_id=1, source_target_pairs={{0,8},{4,12},{8,0},{12,4},{1,9},{5,13},{9,1},{13,5},{2,10},{6,14},... | collective-permute-start | bytes 12296 | tf_op jit(solution)/shard_map/ppermute | solution.py:320
  31.1 1.2 %collective-permute-start.11 = (f32[8,128]{1,0:T(8,128)S(1)}, f32[8,128]{1,0:T(8,128)S(1)}, u32[]{:S(2)}, u32[]{:S(2)}) collective-permute-start(f32[8,128]{1,0:T(8,128)S(1)} %get-tuple-element.48.refs_0_), channel_id=1, source_target_pairs={{0,12},{4,8},{8,4},{12,0},{1,13},{5,9},{9,5},{13,1},{2,14},{6,10},... | collective-permute-start | bytes 12296 | tf_op jit(solution)/shard_map/ppermute | solution.py:320
  32.4 0.5 %own_rows.1 = (f32[64,256]{1,0:T(8,128)S(1)}, f32[64,256]{1,0:T(8,128)S(1)}) custom-call(s32[1]{0:T(128)} %bitcast.place_ref, f32[256,256]{1,0:T(8,128)S(1)} %get-tuple-element.45.log_ref, f32[256,256]{1,0:T(8,128)S(1)} %open_pixels.1.refs_4_.pixel_ref), custom_call_target="tpu_custom_call" | custom-call | flops 1000000000 | tf_op jit(solution)/shard_map/own_rows/pallas_call | solution.py:513
  32.9 1.3 %collective-permute-done.10.refs_2_ = f32[8,128]{1,0:T(8,128)S(1)} collective-permute-done((f32[8,128]{1,0:T(8,128)S(1)}, f32[8,128]{1,0:T(8,128)S(1)}, u32[]{:S(2)}, u32[]{:S(2)}) %collective-permute-start.10) | collective-permute-done | bytes 4128 | tf_op jit(solution)/shard_map/ppermute | solution.py:320
  34.2 1.0 %normalise.1 = f32[64,256]{1,0:T(8,128)} custom-call(f32[64,256]{1,0:T(8,128)S(1)} %get-tuple-element.46.part_ref, f32[64,256]{1,0:T(8,128)S(1)} %get-tuple-element.47.open_ref, f32[8,128]{1,0:T(8,128)S(1)} %get-tuple-element.48.refs_0_, f32[8,128]{1,0:T(8,128)S(1)} %collective-permute-done.9.refs_1_, f32[8,128]{1,0:T(8,128)S(1)} %collective-permute-done.10.refs_2_, ...), custom_call_target="tpu_custom_call" | custom-call | flops 1000000000 | tf_op jit(solution)/shard_map/normalise/pallas_call | solution.py:523
  (19 shorter events, 0.3 us)
Async XLA Ops:
  0.7 5.9 %copy-start = (bf16[1792,256]{1,0:T(8,128)(2,1)S(1)}, bf16[1792,256]{1,0:T(8,128)(2,1)}, u32[]{:S(2)}) copy-start(bf16[1792,256]{1,0:T(8,128)(2,1)} %constant.9.clone.tab_ref.refs_4_.refs_3_) | copy-start | bytes 2752516
  0.7 5.9 %copy-start.1 = (f32[384,256]{1,0:T(8,128)S(1)}, f32[384,256]{1,0:T(8,128)}, u32[]{:S(2)}) copy-start(f32[384,256]{1,0:T(8,128)} %refs_2_) | copy-start | bytes 1179652
  2.4 8.1 %collective-permute-start.3 = (f32[136,128]{1,0:T(8,128)}, f32[136,128]{1,0:T(8,128)S(1)}, u32[]{:S(2)}, u32[]{:S(2)}) collective-permute-start(f32[136,128]{1,0:T(8,128)} %pack_weight.1.refs_5_.refs_0_), channel_id=1, source_target_pairs={{0,2},{1,3},{2,0},{3,1},{4,6},{5,7},{6,4},{7,5},{8,10},{9,11},{10,... | collective-permute-start | bytes 208904 | tf_op jit(solution)/shard_map/ppermute | solution.py:320
  6.5 4.0 %copy-start.2 = (f32[136,128]{1,0:T(8,128)S(1)}, f32[136,128]{1,0:T(8,128)}, u32[]{:S(2)}) copy-start(f32[136,128]{1,0:T(8,128)} %pack_weight.1.refs_5_.refs_0_) | copy-start | bytes 208900
  6.7 6.9 %collective-permute-start = (f32[192,128]{1,0:T(8,128)S(1)}, f32[192,128]{1,0:T(8,128)S(1)}, u32[]{:S(2)}, u32[]{:S(2)}) collective-permute-start(f32[192,128]{1,0:T(8,128)S(1)} %get-tuple-element.28), channel_id=1, source_target_pairs={{0,4},{8,12},{4,0},{12,8},{1,5},{9,13},{5,1},{13,9},{2,6},{10,14},... | collective-permute-start | bytes 294920 | tf_op jit(solution)/shard_map/ppermute | solution.py:329
  6.7 6.9 %collective-permute-start.1 = (f32[192,128]{1,0:T(8,128)S(1)}, f32[192,128]{1,0:T(8,128)S(1)}, u32[]{:S(2)}, u32[]{:S(2)}) collective-permute-start(f32[192,128]{1,0:T(8,128)S(1)} %get-tuple-element.29), channel_id=1, source_target_pairs={{4,8},{8,4},{5,9},{9,5},{6,10},{10,6},{7,11},{11,7},{20,24},{24,20... | collective-permute-start | bytes 294920 | tf_op jit(solution)/shard_map/ppermute | solution.py:329
  10.5 7.6 %collective-permute-start.4 = (f32[2,136,128]{2,1,0:T(8,128)S(1)}, f32[2,136,128]{2,1,0:T(8,128)S(1)}, u32[]{:S(2)}, u32[]{:S(2)}) collective-permute-start(f32[2,136,128]{2,1,0:T(8,128)S(1)} %stack_packs.1), channel_id=1, source_target_pairs={{0,8},{4,12},{8,0},{12,4},{1,9},{5,13},{9,1},{13,5},{2,10},{6,14},... | collective-permute-start | bytes 417800 | tf_op jit(solution)/shard_map/ppermute | solution.py:320
  12.3 1.3 %collective-permute-start.2 = (f32[136,128]{1,0:T(8,128)S(1)}, f32[136,128]{1,0:T(8,128)S(1)}, u32[]{:S(2)}, u32[]{:S(2)}) collective-permute-start(f32[136,128]{1,0:T(8,128)S(1)} %copy-done.2), channel_id=1, source_target_pairs={{0,4},{4,0},{8,12},{12,8},{1,5},{5,1},{9,13},{13,9},{2,6},{6,2},{1... | collective-permute-start | bytes 208904 | tf_op jit(solution)/shard_map/ppermute | solution.py:324
  12.3 4.0 %collective-permute-start.5 = (f32[136,128]{1,0:T(8,128)S(1)}, f32[136,128]{1,0:T(8,128)S(1)}, u32[]{:S(2)}, u32[]{:S(2)}) collective-permute-start(f32[136,128]{1,0:T(8,128)S(1)} %collective-permute-done.3.refs_1_.refs_4_), channel_id=1, source_target_pairs={{0,4},{4,0},{8,12},{12,8},{1,5},{5,1},{9,13},{13,9},{2,6},{6,2},{1... | collective-permute-start | bytes 208904 | tf_op jit(solution)/shard_map/ppermute | solution.py:324
  18.1 1.4 %collective-permute-start.6 = (f32[2,136,128]{2,1,0:T(8,128)S(1)}, f32[2,136,128]{2,1,0:T(8,128)S(1)}, u32[]{:S(2)}, u32[]{:S(2)}) collective-permute-start(f32[2,136,128]{2,1,0:T(8,128)S(1)} %collective-permute-done.4.refs_4_), channel_id=1, source_target_pairs={{0,4},{4,0},{8,12},{12,8},{1,5},{5,1},{9,13},{13,9},{2,6},{6,2},{1... | collective-permute-start | bytes 417800 | tf_op jit(solution)/shard_map/ppermute | solution.py:324
  21.5 6.0 %collective-permute-start.7 = (f32[128,256]{1,0:T(8,128)S(1)}, f32[128,256]{1,0:T(8,128)S(1)}, u32[]{:S(2)}, u32[]{:S(2)}) collective-permute-start(f32[128,256]{1,0:T(8,128)S(1)} %get-tuple-element.43.refs_0_), channel_id=1, source_target_pairs={{0,1},{1,0},{2,3},{3,2},{4,5},{5,4},{6,7},{7,6},{8,9},{9,8},{10,11... | collective-permute-start | bytes 393224 | tf_op jit(solution)/shard_map/ppermute | solution.py:324
  22.7 2.1 %copy-start.3 = (s32[16,16]{1,0:T(8,128)S(1)}, s32[16,16]{1,0:T(8,128)}, u32[]{:S(2)}) copy-start(s32[16,16]{1,0:T(8,128)} %mask_ref.1) | copy-start | bytes 3076
  23.9 6.0 %collective-permute-start.8 = (f32[128,256]{1,0:T(8,128)S(1)}, f32[128,256]{1,0:T(8,128)S(1)}, u32[]{:S(2)}, u32[]{:S(2)}) collective-permute-start(f32[128,256]{1,0:T(8,128)S(1)} %next_strip.1.refs_1_), channel_id=1, source_target_pairs={{0,1},{1,0},{2,3},{3,2},{4,5},{5,4},{6,7},{7,6},{8,9},{9,8},{10,11... | collective-permute-start | bytes 393224 | tf_op jit(solution)/shard_map/ppermute | solution.py:324
  30.4 2.5 %collective-permute-start.9 = (f32[8,128]{1,0:T(8,128)S(1)}, f32[8,128]{1,0:T(8,128)S(1)}, u32[]{:S(2)}, u32[]{:S(2)}) collective-permute-start(f32[8,128]{1,0:T(8,128)S(1)} %get-tuple-element.48.refs_0_), channel_id=1, source_target_pairs={{0,4},{4,0},{8,12},{12,8},{1,5},{5,1},{9,13},{13,9},{2,6},{6,2},{1... | collective-permute-start | bytes 12296 | tf_op jit(solution)/shard_map/ppermute | solution.py:320
  30.5 3.7 %collective-permute-start.10 = (f32[8,128]{1,0:T(8,128)S(1)}, f32[8,128]{1,0:T(8,128)S(1)}, u32[]{:S(2)}, u32[]{:S(2)}) collective-permute-start(f32[8,128]{1,0:T(8,128)S(1)} %get-tuple-element.48.refs_0_), channel_id=1, source_target_pairs={{0,8},{4,12},{8,0},{12,4},{1,9},{5,13},{9,1},{13,5},{2,10},{6,14},... | collective-permute-start | bytes 12296 | tf_op jit(solution)/shard_map/ppermute | solution.py:320
  31.1 3.1 %collective-permute-start.11 = (f32[8,128]{1,0:T(8,128)S(1)}, f32[8,128]{1,0:T(8,128)S(1)}, u32[]{:S(2)}, u32[]{:S(2)}) collective-permute-start(f32[8,128]{1,0:T(8,128)S(1)} %get-tuple-element.48.refs_0_), channel_id=1, source_target_pairs={{0,12},{4,8},{8,4},{12,0},{1,13},{5,9},{9,5},{13,1},{2,14},{6,10},... | collective-permute-start | bytes 12296 | tf_op jit(solution)/shard_map/ppermute | solution.py:320

commit v3 on v2

v3 whole, which is shorter than its diff:
```python
import functools
import math

import jax
import jax.numpy as jnp
import ml_dtypes
import numpy as np
from jax import lax
from jax.experimental import pallas as pl
from jax.experimental.pallas import tpu as pltpu
from jax.sharding import PartitionSpec as P

GUARD = 64
MBLK = 16
LANES = 128
PACK = 8
CHUNK = 8
COST = 0.1
OWN, EARLY, REST, LAST = 1, 0.2, 0.4, 2

F32 = jnp.float32
BF16 = jnp.bfloat16
VMEM = pl.BlockSpec(memory_space=pltpu.VMEM)
SMEM = pl.BlockSpec(memory_space=pltpu.SMEM)


def params(mib):
    return pltpu.CompilerParams(vmem_limit_bytes=mib * 2**20)


def high_low(table):
    high = table.astype(np.float32).astype(ml_dtypes.bfloat16)
    low = (table - high.astype(np.float64)).astype(np.float32).astype(ml_dtypes.bfloat16)
    return high, low


def tables(side):
    span = 2 * side
    turn = 2.0 * math.pi * (np.arange(side) + 0.5) / span
    angles = np.outer(np.arange(span), turn)
    high, low = high_low(np.concatenate([np.cos(angles), np.sin(angles)], axis=1))
    middle = np.outer(np.arange(span) - (side - 1) / 2, turn)
    middle_high, middle_low = high_low(np.concatenate([np.cos(middle), np.sin(middle)], axis=1).T)
    away = np.outer(np.arange(side // 2) + 0.5, turn)
    ends = []
    for wave in (np.cos(away), np.sin(away)):
        wave_high, wave_low = high_low(wave)
        ends += [np.concatenate([wave_high, wave_high], axis=1), np.concatenate([wave_low, wave_low], axis=1)]
    return np.concatenate([high, low, high.T, low.T, *ends, middle_high, middle_low], axis=0)


def tall(tab_ref, count):
    span = tab_ref.shape[1]
    high, low = tab_ref[0:count, :], tab_ref[span : span + count, :]
    return jnp.concatenate([high, high, low], axis=0)


def wide(high, low):
    return jnp.concatenate([high, high, low], axis=1)


def back_cols(tab_ref, side):
    span = tab_ref.shape[1]
    both = jnp.concatenate([tab_ref[2 * span : 3 * span, 0:side], tab_ref[3 * span : 4 * span, 0:side]], axis=1)
    return jnp.concatenate([both, both], axis=0)


def split(x):
    high = x.astype(BF16)
    return high, (x - high.astype(F32)).astype(BF16)


def tripled(x, axis):
    high, low = split(x)
    return jnp.concatenate([high, low, high], axis=axis)


def doubled(x, axis):
    return jnp.concatenate(split(x), axis=axis)


def halves(x, axis):
    half = x.shape[axis] // 2
    return x[:half] + x[half:] if axis == 0 else x[:, :half] + x[:, half:]


def product(left, right):
    return jnp.dot(left, right, preferred_element_type=F32)


def paired(quads, side):
    cc, cs = quads[:side, :side], quads[:side, side:]
    sc, ss = quads[side:, :side], quads[side:, side:]
    return cc - ss, sc + cs, cc + ss, sc - cs


def image_spectra(spot_ref, inner_ref, own_ref, outer_ref, tab_ref, spec_ref):
    odd = spot_ref[0] % 2 == 1

    def edge(ref):
        lines = ref[...]
        return jnp.concatenate([lines[:, :GUARD], lines[:, GUARD:]], axis=0)

    inner, outer = edge(inner_ref), edge(outer_ref)
    left, right = jnp.where(odd, inner, outer), jnp.where(odd, outer, inner)
    image = jnp.concatenate([left, own_ref[...], right], axis=1)
    side = spec_ref.shape[-1]
    span = 2 * side
    rows, cols = image.shape[0] // side - 1, image.shape[1] // side - 1
    scale = 2.0 / (span * span)
    cols_table, rows_table = tall(tab_ref, span), wide(tab_ref[5 * span : 6 * span, :], tab_ref[6 * span :, :])
    for q in range(cols):
        half = product(tripled(image[:, q * side : q * side + span], 1), cols_table)
        for p in range(rows):
            full = product(rows_table, tripled(half[p * side : p * side + span], 0))
            for part, value in enumerate(paired(full, side)):
                spec_ref[p * cols + q, part] = value * scale


def transform(patches, tab_ref, half_ref, patch_ref):
    side = patch_ref.shape[-1]
    span = 2 * side
    patch_cols = tall(tab_ref, side)
    patch_rows = wide(tab_ref[2 * span : 3 * span, 0:side], tab_ref[3 * span : 4 * span, 0:side])
    for first in range(0, len(patches), 4):
        group = patches[first : first + 4]
        half = product(tripled(jnp.concatenate(group, axis=0), 1), patch_cols)
        for i in range(len(group)):
            high, low = split(half[i * side : (i + 1) * side])
            half_ref[first + i, 0:side] = high
            half_ref[first + i, side : 2 * side] = low
            half_ref[first + i, 2 * side : 3 * side] = high

    def finish(n, carry):
        for part, value in enumerate(paired(product(patch_rows, half_ref[n]), side)):
            patch_ref[n, part] = value
        return carry

    lax.fori_loop(0, len(patches), finish, 0, unroll=steps_at_once(len(patches), 8))


def steps_at_once(count, most):
    return max(u for u in range(1, most + 1) if count % u == 0)


def correlate(spec_ref, tab_ref, patch_refs, strip, score_ref):
    side = spec_ref.shape[-1]
    span = 2 * side
    cols = score_ref.shape[2] // side
    even_rows, odd_rows = tab_ref[4 * span : 4 * span + side, :], tab_ref[4 * span + side : 5 * span, :]
    cols_table = back_cols(tab_ref, side)
    first = 0
    for patch_ref in patch_refs:

        def score(n, carry, patch_ref=patch_ref, first=first):
            tr, tu, sr, si = (patch_ref[n, part] for part in range(4))
            for q in range(cols):
                ir, iu, jr, ji = (spec_ref[strip * cols + q, part] for part in range(4))
                a, b = ir * tr + iu * tu, iu * tr - ir * tu
                c, e = jr * sr + ji * si, jr * si - ji * sr
                top = jnp.concatenate([a + c, e + b], axis=1)
                low = jnp.concatenate([b - e, c - a], axis=1)
                even = halves(product(even_rows, doubled(top, 0)), 0)
                odd = halves(product(odd_rows, doubled(low, 0)), 0)
                lines = jnp.concatenate([even + odd, even - odd], axis=0)
                score_ref[first + n, :, q * side : (q + 1) * side] = halves(product(doubled(lines, 1), cols_table), 1)
            return carry

        count = patch_ref.shape[0]
        lax.fori_loop(0, count, score, 0, unroll=steps_at_once(count, 16 // cols))
        first += count


STRIP = 64


def fold(score_ref, weights, state, out):
    def strip(r, carry):
        rows = pl.ds(pl.multiple_of(r * STRIP, STRIP), STRIP)
        values = [score_ref[n, rows, :] + weight for n, weight in enumerate(weights)]
        top = values[0]
        for value in values[1:]:
            top = jnp.maximum(top, value)
        if state:
            old_top, old_sum = state[0][rows, :], state[1][rows, :]
            top = jnp.maximum(top, old_top)
        total = jnp.exp(values[0] - top)
        for value in values[1:]:
            total = total + jnp.exp(value - top)
        if state:
            total = total + old_sum * jnp.exp(old_top - top)
        if len(out) == 1:
            out[0][rows, :] = top + jnp.log(total)
        else:
            out[0][rows, :] = top
            out[1][rows, :] = total
        return carry

    lax.fori_loop(0, score_ref.shape[1] // STRIP, strip, 0, unroll=True)


def unpack(refs, side):
    patches, weights = [], []
    for ref in refs:
        places = [()] if len(ref.shape) == 2 else [(i,) for i in range(ref.shape[0])]
        for place in places:
            patches.append(ref[place + (slice(0, side), slice(None))])
            weights.append(ref[place + (slice(side, side + 1), slice(0, 1))])
    return patches, weights


def own_kernel(n_in, strip, *refs):
    tab_ref, packs = refs[4], refs[5 : 5 + n_in]
    spec_ref, *out, patch_ref, half_ref, score_ref = refs[5 + n_in :]
    image_spectra(*refs[:5], spec_ref)
    patches, weights = unpack(packs, spec_ref.shape[-1])
    transform(patches, tab_ref, half_ref, patch_ref)
    correlate(spec_ref, tab_ref, [patch_ref], strip, score_ref)
    fold(score_ref, weights, (), out)


def strip_kernel(n_in, n_spectra, n_state, strip, *refs):
    spec_ref, tab_ref, refs = refs[0], refs[1], refs[2:]
    state, packs, refs = refs[:n_state], refs[n_state : n_state + n_in], refs[n_state + n_in :]
    patches, weights = unpack(packs, spec_ref.shape[-1])
    if n_spectra:
        patch_refs, (*out, score_ref) = refs[:n_spectra], refs[n_spectra:]
    else:
        *out, patch_ref, half_ref, score_ref = refs
        transform(patches, tab_ref, half_ref, patch_ref)
        patch_refs = [patch_ref]
    correlate(spec_ref, tab_ref, patch_refs, strip, score_ref)
    fold(score_ref, weights, state, out)


def folded(stored, side):
    within = stored % side
    return stored - within + jnp.where(within < side // 2, within + side // 2, side - 1 - within)


def keeper(row, side):
    within = row % side
    return row - within + jnp.where(within < side // 2, side - 1 - within, within - side // 2)


def pixel_kernel(side, mask_ref, pixel_ref):
    blocks = (1.0 - mask_ref[...].astype(F32)).astype(BF16)
    rows, cols = blocks.shape
    pixel = folded(lax.broadcasted_iota(jnp.int32, (rows * MBLK, rows), 0), side)
    block = lax.broadcasted_iota(jnp.int32, (rows * MBLK, rows), 1)
    down = (pixel // MBLK == block).astype(F32).astype(BF16)
    pixel = lax.broadcasted_iota(jnp.int32, (cols, cols * MBLK), 1)
    block = lax.broadcasted_iota(jnp.int32, (cols, cols * MBLK), 0)
    across = (pixel // MBLK == block).astype(F32).astype(BF16)
    pixel_ref[...] = product(product(down, blocks).astype(BF16), across)


def join_kernel(n_map, strip, *refs):
    maps, (pixel_ref, *before, log_ref, stat_ref) = refs[:n_map], refs[n_map:]
    values = maps[0][...]
    for ref in maps[1:]:
        other = ref[...]
        top = jnp.maximum(values, other)
        values = top + jnp.log(1.0 + jnp.exp(jnp.minimum(values, other) - top))
    log_ref[...] = values
    side = values.shape[0]
    pixels = pixel_ref[strip * side : (strip + 1) * side, :]
    count = jnp.sum(pixels)
    total = jnp.sum(pixels * values)
    deviation = values - total / jnp.maximum(count, 1.0)
    squares = jnp.sum(pixels * deviation * deviation)
    lane = lax.broadcasted_iota(jnp.int32, stat_ref.shape, 1)
    stat = before[0][...] if before else jnp.zeros(stat_ref.shape, F32)
    for i, value in enumerate((count, total, squares)):
        stat = jnp.where(lane == 3 * strip + i, value, stat)
    stat_ref[...] = stat


def own_rows_kernel(n_strip, place_ref, *refs):
    strips, (pixel_ref, part_ref, open_ref, log_ref) = refs[:n_strip], refs[n_strip:]
    side = strips[0].shape[0]
    share = part_ref.shape[0]
    for i, ref in enumerate(strips):
        log_ref[i * side : (i + 1) * side, :] = ref[...]

    def unfold(i, carry):
        row = keeper(place_ref[0] * share + i, side)
        part_ref[pl.ds(i, 1), :] = log_ref[pl.ds(row, 1), :]
        open_ref[pl.ds(i, 1), :] = pixel_ref[pl.ds(row, 1), :]
        return carry

    lax.fori_loop(0, share, unfold, 0, unroll=8)


def norm_kernel(n_strip, part_ref, open_ref, *refs):
    stats, out_ref = refs[:-1], refs[-1]
    lanes = [(ref, 3 * strip) for ref in stats for strip in range(n_strip)]
    counts = [ref[:, i : i + 1] for ref, i in lanes]
    totals = [ref[:, i + 1 : i + 2] for ref, i in lanes]
    count, total = sum(counts), sum(totals)
    average = total / count
    squares = 0.0
    for (ref, i), n, s in zip(lanes, counts, totals):
        apart = s / jnp.maximum(n, 1.0) - average
        squares = squares + ref[:, i + 2 : i + 3] + n * apart * apart
    scale = 1.0 / jnp.sqrt(squares / count + 1e-05)
    out_ref[...] = open_ref[...] * (part_ref[...] - average[0:1]) * scale[0:1]


def shift(i, step, n):
    return i ^ step if n & (n - 1) == 0 else (i + step) % n


def peer(x, axis, step):
    n = lax.axis_size(axis)
    return lax.ppermute(x, axis, [(i, shift(i, step, n)) for i in range(n)])


def swap(x, axis):
    return lax.ppermute(x, axis, [(i, i ^ 1) for i in range(lax.axis_size(axis))])


def exchange(x, axis, start):
    pairs = [(i, i + 1) for i in range(start, lax.axis_size(axis) - 1, 2)]
    return lax.ppermute(x, axis, pairs + [(j, i) for i, j in pairs])


def pack_kernel(ids_ref, weight_ref, patch_ref, pack_ref, weights, sems):
    side = patch_ref.shape[0]
    pairs = ((patch_ref, pack_ref.at[0:side]), (weight_ref, weights))
    copies = [pltpu.make_async_copy(source, target, sems.at[i]) for i, (source, target) in enumerate(pairs)]
    for copy in copies:
        copy.start()
    for copy in copies:
        copy.wait()
    catalog = lax.broadcasted_iota(jnp.int32, weights.shape, 1)
    weight = jnp.sum(jnp.where(catalog == ids_ref[0, 0], weights[...], 0.0), axis=1, keepdims=True)
    pack_ref[side:, :] = jnp.broadcast_to(weight, (PACK, side))


def edge_kernel(spot_ref, own_ref, tab_ref, inner_ref, outer_ref):
    half = own_ref.shape[0] // 2
    own = own_ref[...]
    edges = [own[:, :GUARD], own[:, own.shape[1] - GUARD :]]
    left, right = [jnp.concatenate([x[:half], x[half:]], axis=1) for x in edges]
    odd = spot_ref[0] % 2 == 1
    inner_ref[...] = jnp.where(odd, left, right)
    outer_ref[...] = jnp.where(odd, right, left)


def stack_kernel(*refs):
    for i, ref in enumerate(refs[:-1]):
        refs[-1][i] = ref[...]


def cost(micros):
    return pl.CostEstimate(flops=int(micros * 1e9), bytes_accessed=0, transcendentals=0)


def body(micrograph, templates, orient_ids, log_weight, ice_mask):
    side = templates.shape[2]
    tile = micrograph.shape[1]
    blocks = (tile // side) ** 2
    tab = jnp.asarray(tables(side))
    n_tile, n_orient = lax.axis_size("tile"), lax.axis_size("orient")
    place = lax.axis_index("orient").astype(jnp.int32).reshape(1)
    spot = lax.axis_index("tile").astype(jnp.int32).reshape(1)
    stay = [pltpu.with_memory_space_constraint(x, pltpu.HBM) for x in (log_weight.reshape(1, -1), templates.reshape(side, side))]
    pack = pl.pallas_call(
        pack_kernel,
        out_shape=jax.ShapeDtypeStruct((side + PACK, side), F32),
        in_specs=[SMEM, pl.BlockSpec(memory_space=pltpu.HBM), pl.BlockSpec(memory_space=pltpu.HBM)],
        out_specs=VMEM,
        scratch_shapes=[pltpu.VMEM((1, log_weight.shape[0]), F32), pltpu.SemaphoreType.DMA((2,))],
        compiler_params=params(4),
        cost_estimate=cost(1),
        name="pack_weight",
    )(orient_ids, *stay)
    micrograph, pack = lax.optimization_barrier((micrograph, pack))
    edge = jax.ShapeDtypeStruct((micrograph.shape[0] // 2, 2 * GUARD), F32)
    inner_edge, outer_edge = pl.pallas_call(
        edge_kernel,
        out_shape=(edge, edge),
        in_specs=[SMEM, VMEM, VMEM],
        out_specs=(VMEM, VMEM),
        compiler_params=params(4),
        cost_estimate=cost(0.5),
        name="edges",
    )(spot, micrograph, tab)

    tile_pairs, orient_pairs = n_tile % 2 == 0, n_orient % 2 == 0
    tile_steps = range(0, n_tile, 2 if tile_pairs else 1)
    orient_steps = range(0, n_orient, 2 if orient_pairs else 1)
    far = [peer(pack, "orient", o) for o in orient_steps[1:]]
    inner, outer = exchange(inner_edge, "tile", 0), exchange(outer_edge, "tile", 1)
    mine = [pack] + ([swap(pack, "tile")] if tile_pairs else [])

    plane = jax.ShapeDtypeStruct((tile, tile), F32)

    strip_shape = jax.ShapeDtypeStruct((side, tile), F32)
    half_shape, patch_shape = (3 * side, 2 * side), (4, side, side)

    def size(arrays):
        return sum(x.shape[0] if x.ndim == 3 else 1 for x in arrays)

    def call(kernel, name, micros, shapes, scratch, *operands, places=(), mib=24):
        return pl.pallas_call(
            kernel,
            out_shape=shapes,
            in_specs=[SMEM] * len(places) + [VMEM] * len(operands),
            out_specs=jax.tree.map(lambda _: VMEM, shapes),
            scratch_shapes=scratch,
            compiler_params=params(mib),
            cost_estimate=cost(micros),
            name=name,
        )(*places, *operands)

    def spectra_shape(count):
        return jax.ShapeDtypeStruct((count, *patch_shape), F32)

    def halves_scratch(count):
        return pltpu.VMEM((count, *half_shape), BF16)

    def score_scratch(count):
        return pltpu.VMEM((count, side, tile), F32)

    n_strip = tile // side
    held = call(stack_kernel, "stack_packs", COST, jax.ShapeDtypeStruct((1 + len(far), *pack.shape), F32), [], pack, *far)
    near = [peer(held, "tile", t) for t in tile_steps[1:]]
    early = far + ([swap(x, "tile") for x in far] if tile_pairs else [])
    spec, *state, own_spectra = call(
        functools.partial(own_kernel, len(mine), 0),
        "own_block",
        OWN,
        (jax.ShapeDtypeStruct((blocks, 4, side, side), F32), strip_shape, strip_shape, spectra_shape(len(mine))),
        [halves_scratch(len(mine)), score_scratch(len(mine))],
        inner,
        micrograph,
        outer,
        tab,
        *mine,
        places=(spot,),
    )

    def score(arrays, spectra, state, strip, last, micros):
        count = size(arrays)
        shapes = (strip_shape,) * (1 if last else 2)
        scratch = [score_scratch(count)]
        if not spectra:
            shapes += (spectra_shape(count),)
            scratch = [halves_scratch(count)] + scratch
        out = call(
            functools.partial(strip_kernel, len(arrays), len(spectra), len(state), strip),
            "score_strip",
            micros,
            shapes,
            scratch,
            spec,
            tab,
            *state,
            *arrays,
            *spectra,
        )
        return (out, spectra) if spectra else (out[:-1], [out[-1]])

    def chunks(arrays):
        groups = []
        for x in arrays:
            if not groups or size(groups[-1]) + size([x]) > CHUNK:
                groups.append([])
            groups[-1].append(x)
        return groups

    done = [(mine, [own_spectra])]
    early, state = lax.optimization_barrier((early, state))
    for group in chunks(early):
        state, spectra = score(group, [], state, 0, False, EARLY)
        done.append((group, spectra))
    near, state = lax.optimization_barrier((near, state))
    groups = chunks(near + ([swap(x, "tile") for x in near] if tile_pairs else []))
    for i, group in enumerate(groups):
        state, spectra = score(group, [], state, 0, i == len(groups) - 1, REST)
        done.append((group, spectra))
    log_maps = [state[0]]
    swapped = [swap(state[0], "orient")] if orient_pairs else []
    if sum(size(arrays) for arrays, _ in done) <= CHUNK:
        done = [([x for arrays, _ in done for x in arrays], [x for _, spectra in done for x in spectra])]
    for strip in range(1, n_strip):
        state = ()
        for i, (arrays, spectra) in enumerate(done):
            state, _ = score(arrays, spectra, state, strip, i == len(done) - 1, LAST)
        log_maps.append(state[0])
        if orient_pairs:
            swapped.append(swap(state[0], "orient"))
    pixels = call(functools.partial(pixel_kernel, side), "open_pixels", 1, plane, [], ice_mask)
    stat_shape = jax.ShapeDtypeStruct((8, LANES), F32)
    stat, strips = (), []
    for strip, maps in enumerate(zip(log_maps, swapped) if orient_pairs else zip(log_maps)):
        joined, *stat = call(
            functools.partial(join_kernel, len(maps), strip),
            "join_maps",
            COST,
            (strip_shape, stat_shape),
            [],
            *maps,
            pixels,
            *stat,
        )
        strips.append(joined)
    stat = stat[0]
    share = tile // n_orient
    part = jax.ShapeDtypeStruct((share, tile), F32)
    part, opened = call(
        functools.partial(own_rows_kernel, n_strip),
        "own_rows",
        1,
        (part, part),
        [pltpu.VMEM((tile, tile), F32)],
        *strips,
        pixels,
        places=(place,),
    )
    stats = [stat] + [peer(stat, "tile", k) for k in range(1, n_tile)]
    return call(
        functools.partial(norm_kernel, n_strip),
        "normalise",
        1,
        jax.ShapeDtypeStruct((share, tile), F32),
        [],
        part,
        opened,
        *stats,
    )


def solution(mesh):
    return jax.shard_map(
        body,
        mesh=mesh,
        in_specs=(
            P("group", "tile"),
            P("orient", "tile", None, None),
            P("orient", "tile"),
            P(),
            P("group", "tile"),
        ),
        out_specs=P(("group", "orient"), "tile"),
        check_vma=False,
    )
```

time: 35.4 us -> 34.2 us (0.966)
  waiting for transfers between devices: 11.1 us -> 7.08 us
  starting transfers between devices: 11.5 us -> 14.7 us
  Pallas kernels: 11.8 us -> 11.4 us
    ppermute x5, starting transfers between devices: 2.89 us -> 5.93 us  [swap(): lax.ppermute(x, axis, [(i, i ^ 1) for i in range(lax.axis_size(axis))])]
    ppermute x5, waiting for transfers between devices: 4.43 us -> 1.76 us  [peer(): return lax.ppermute(x, axis, [(i, shift(i, step, n)) for i in range(n)])]
    ppermute x5, waiting for transfers between devices: 6.68 us -> 5.31 us  [swap(): lax.ppermute(x, axis, [(i, i ^ 1) for i in range(lax.axis_size(axis))])]
    pallas_call x1, Pallas kernels: 1.74 us -> 1.04 us  [body(): pl.pallas_call(pack_kernel, out_shape=jax.ShapeDtypeStruct((side + PACK,...]
    pallas_call x9 -> x10, Pallas kernels: 9.95 us -> 10.3 us  [call(): pl.pallas_call(kernel, out_shape=shapes, in_specs=[SMEM] * len(places) +...]
  transfers between devices with their start and end apart: 12 -> 12, of which waited for: 6 -> 6; matrix products, arithmetic and copies ran while one was open for 0% -> 0% of each run, Pallas kernels for 19% -> 21%
where the time goes in v3:
time: 34.2 us; the launch traced here: 34 us
  starting transfers between devices  14.7 us (43%)
  Pallas kernels  11.4 us (33%)
  waiting for transfers between devices  7.08 us (21%)
  between operations  0.79 us (2%)
    pallas_call x10, Pallas kernels, call(): pl.pallas_call(kernel, out_shape=shapes, in_specs=[SMEM] * len(places) +...  10.3 us
    ppermute x5, starting transfers between devices, peer(): return lax.ppermute(x, axis, [(i, shift(i, step, n)) for i in range(n)])  8.05 us
    ppermute x5, starting transfers between devices, swap(): lax.ppermute(x, axis, [(i, i ^ 1) for i in range(lax.axis_size(axis))])  5.93 us
    ppermute x5, waiting for transfers between devices, swap(): lax.ppermute(x, axis, [(i, i ^ 1) for i in range(lax.axis_size(axis))])  5.31 us
    ppermute x5, waiting for transfers between devices, peer(): return lax.ppermute(x, axis, [(i, shift(i, step, n)) for i in range(n)])  1.76 us
    pallas_call x1, Pallas kernels, body(): pl.pallas_call(pack_kernel, out_shape=jax.ShapeDtypeStruct((side + PACK,...  1.04 us
    ppermute x2, starting transfers between devices, exchange(): return lax.ppermute(x, axis, pairs + [(j, i) for i, j in pairs])  0.74 us
  transfers between devices with their start and end apart: 12, of which 6 were waited for; matrix products, arithmetic and copies ran while one was open for 0% of the time, Pallas kernels for 21%

profile of v3, /device:TPU:0, one launch (start us, length us, event | category | flops | bytes accessed | tf_op | source)
XLA Modules:
  0.0 34.0 jit_solution(13273724660994049879)
XLA Ops:
  0.7 1.0 %pack_weight.1.refs_5_.refs_0_.refs_2_ = f32[136,128]{1,0:T(8,128)S(1)} custom-call(s32[1,1]{1,0:T(1,128)S(6)} %copy.7.ids_ref, f32[1,16]{1,0:T(1,128)} %bitcast.5, f32[128,128]{1,0:T(8,128)} %bitcast.4), custom_call_target="tpu_custom_call" | custom-call | flops 1000000000 | tf_op jit(solution)/shard_map/pack_weight/pallas_call | solution.py:369
  1.7 4.1 %collective-permute-start.3 = (f32[136,128]{1,0:T(8,128)S(1)}, f32[136,128]{1,0:T(8,128)S(1)}, u32[]{:S(2)}, u32[]{:S(2)}) collective-permute-start(f32[136,128]{1,0:T(8,128)S(1)} %pack_weight.1.refs_5_.refs_0_.refs_2_), channel_id=1, source_target_pairs={{0,2},{1,3},{2,0},{3,1},{4,6},{5,7},{6,4},{7,5},{8,10},{9,11},{10,... | collective-permute-start | bytes 208904 | tf_op jit(solution)/shard_map/ppermute | solution.py:316
  6.0 0.7 %collective-permute-start.1 = (f32[192,128]{1,0:T(8,128)S(1)}, f32[192,128]{1,0:T(8,128)S(1)}, u32[]{:S(2)}, u32[]{:S(2)}) collective-permute-start(f32[192,128]{1,0:T(8,128)S(1)} %get-tuple-element.33), channel_id=1, source_target_pairs={{4,8},{8,4},{5,9},{9,5},{6,10},{10,6},{7,11},{11,7},{20,24},{24,20... | collective-permute-start | bytes 294920 | tf_op jit(solution)/shard_map/ppermute | solution.py:325
  6.7 2.9 %collective-permute-start.2 = (f32[136,128]{1,0:T(8,128)S(1)}, f32[136,128]{1,0:T(8,128)S(1)}, u32[]{:S(2)}, u32[]{:S(2)}) collective-permute-start(f32[136,128]{1,0:T(8,128)S(1)} %pack_weight.1.refs_5_.refs_0_.refs_2_), channel_id=1, source_target_pairs={{0,4},{4,0},{8,12},{12,8},{1,5},{5,1},{9,13},{13,9},{2,6},{6,2},{1... | collective-permute-start | bytes 208904 | tf_op jit(solution)/shard_map/ppermute | solution.py:320
  9.7 1.7 %collective-permute-start.4 = (f32[2,136,128]{2,1,0:T(8,128)S(1)}, f32[2,136,128]{2,1,0:T(8,128)S(1)}, u32[]{:S(2)}, u32[]{:S(2)}) collective-permute-start(f32[2,136,128]{2,1,0:T(8,128)S(1)} %stack_packs.1), channel_id=1, source_target_pairs={{0,8},{4,12},{8,0},{12,4},{1,9},{5,13},{9,1},{13,5},{2,10},{6,14},... | collective-permute-start | bytes 417800 | tf_op jit(solution)/shard_map/ppermute | solution.py:316
  11.4 2.2 %own_block.1 = (f32[4,4,128,128]{3,2,1,0:T(8,128)S(1)}, f32[128,256]{1,0:T(8,128)S(1)}, f32[128,256]{1,0:T(8,128)S(1)}, f32[2,4,128,128]{3,2,1,0:T(8,128)S(1)}) custom-call(s32[1]{0:T(128)} %bitcast.1.spot_ref.refs_0_, f32[192,128]{1,0:T(8,128)S(1)} %collective-permute-done.refs_1_, f32[384,256]{1,0:T(8,128)S(1)} %copy-done.1, ...), custom_call_target="tpu_custom_call" | custom-call | flops 1000000000 | tf_op jit(solution)/shard_map/own_block/pallas_call | solution.py:407
  13.7 1.4 %score_strip.3 = (f32[128,256]{1,0:T(8,128)S(1)}, f32[128,256]{1,0:T(8,128)S(1)}, f32[2,4,128,128]{3,2,1,0:T(8,128)S(1)}) custom-call(f32[4,4,128,128]{3,2,1,0:T(8,128)S(1)} %get-tuple-element.35.refs_0_, bf16[1792,256]{1,0:T(8,128)(2,1)S(1)} %copy-done, f32[128,256]{1,0:T(8,128)S(1)} %get-tuple-element.38.refs_2_, ...), custom_call_target="tpu_custom_call" | custom-call | flops 200000000 | tf_op jit(solution)/shard_map/score_strip/pallas_call | solution.py:407
  15.0 0.6 %collective-permute-done.4.refs_4_.refs_6_ = f32[2,136,128]{2,1,0:T(8,128)S(1)} collective-permute-done((f32[2,136,128]{2,1,0:T(8,128)S(1)}, f32[2,136,128]{2,1,0:T(8,128)S(1)}, u32[]{:S(2)}, u32[]{:S(2)}) %collective-permute-start.4) | collective-permute-done | bytes 139296 | tf_op jit(solution)/shard_map/ppermute | solution.py:316
  15.6 0.8 %collective-permute-start.6 = (f32[2,136,128]{2,1,0:T(8,128)S(1)}, f32[2,136,128]{2,1,0:T(8,128)S(1)}, u32[]{:S(2)}, u32[]{:S(2)}) collective-permute-start(f32[2,136,128]{2,1,0:T(8,128)S(1)} %collective-permute-done.4.refs_4_.refs_6_), channel_id=1, source_target_pairs={{0,4},{4,0},{8,12},{12,8},{1,5},{5,1},{9,13},{13,9},{2,6},{6,2},{1... | collective-permute-start | bytes 417800 | tf_op jit(solution)/shard_map/ppermute | solution.py:320
  16.4 1.0 %collective-permute-done.6.refs_5_.refs_7_ = f32[2,136,128]{2,1,0:T(8,128)S(1)} collective-permute-done((f32[2,136,128]{2,1,0:T(8,128)S(1)}, f32[2,136,128]{2,1,0:T(8,128)S(1)}, u32[]{:S(2)}, u32[]{:S(2)}) %collective-permute-start.6) | collective-permute-done | bytes 139296 | tf_op jit(solution)/shard_map/ppermute | solution.py:320
  17.4 1.8 %score_strip.4 = (f32[128,256]{1,0:T(8,128)S(1)}, f32[4,4,128,128]{3,2,1,0:T(8,128)S(1)}) custom-call(f32[4,4,128,128]{3,2,1,0:T(8,128)S(1)} %get-tuple-element.35.refs_0_, bf16[1792,256]{1,0:T(8,128)(2,1)S(1)} %copy-done, f32[128,256]{1,0:T(8,128)S(1)} %get-tuple-element.44.refs_2_, f32[128,256]{1,0:T(8,128)S(1)} %get-tuple-element.45.refs_3_, ...), custom_call_target="tpu_custom_call" | custom-call | flops 400000000 | tf_op jit(solution)/shard_map/score_strip/pallas_call | solution.py:407
  19.3 1.7 %collective-permute-start.7 = (f32[128,256]{1,0:T(8,128)S(1)}, f32[128,256]{1,0:T(8,128)S(1)}, u32[]{:S(2)}, u32[]{:S(2)}) collective-permute-start(f32[128,256]{1,0:T(8,128)S(1)} %get-tuple-element.47.refs_0_), channel_id=1, source_target_pairs={{0,1},{1,0},{2,3},{3,2},{4,5},{5,4},{6,7},{7,6},{8,9},{9,8},{10,11... | collective-permute-start | bytes 393224 | tf_op jit(solution)/shard_map/ppermute | solution.py:320
  20.9 2.1 %score_strip.5.refs_0_ = f32[128,256]{1,0:T(8,128)S(1)} custom-call(f32[4,4,128,128]{3,2,1,0:T(8,128)S(1)} %get-tuple-element.35.refs_0_, bf16[1792,256]{1,0:T(8,128)(2,1)S(1)} %copy-done, f32[136,128]{1,0:T(8,128)S(1)} %pack_weight.1.refs_5_.refs_0_.refs_2_, f32[136,128]{1,0:T(8,128)S(1)} %collective-permute-done.2.refs_6_.refs_3_, ...), custom_call_target="tpu_custom_call" | custom-call | flops 2000000000 | tf_op jit(solution)/shard_map/score_strip/pallas_call | solution.py:407
  23.0 0.5 %collective-permute-start.8 = (f32[128,256]{1,0:T(8,128)S(1)}, f32[128,256]{1,0:T(8,128)S(1)}, u32[]{:S(2)}, u32[]{:S(2)}) collective-permute-start(f32[128,256]{1,0:T(8,128)S(1)} %score_strip.5.refs_0_), channel_id=1, source_target_pairs={{0,1},{1,0},{2,3},{3,2},{4,5},{5,4},{6,7},{7,6},{8,9},{9,8},{10,11... | collective-permute-start | bytes 393224 | tf_op jit(solution)/shard_map/ppermute | solution.py:320
  23.6 0.3 open_pixels.1.refs_2_
  23.9 1.2 %collective-permute-done.7.refs_1_ = f32[128,256]{1,0:T(8,128)S(1)} collective-permute-done((f32[128,256]{1,0:T(8,128)S(1)}, f32[128,256]{1,0:T(8,128)S(1)}, u32[]{:S(2)}, u32[]{:S(2)}) %collective-permute-start.7) | collective-permute-done | bytes 131104 | tf_op jit(solution)/shard_map/ppermute | solution.py:320
  25.1 0.4 %join_maps.2 = (f32[128,256]{1,0:T(8,128)S(1)}, f32[8,128]{1,0:T(8,128)S(1)}) custom-call(f32[128,256]{1,0:T(8,128)S(1)} %get-tuple-element.47.refs_0_, f32[128,256]{1,0:T(8,128)S(1)} %collective-permute-done.7.refs_1_, f32[256,256]{1,0:T(8,128)S(1)} %open_pixels.1.refs_2_), custom_call_target="tpu_custom_call" | custom-call | flops 100000000 | tf_op jit(solution)/shard_map/join_maps/pallas_call | solution.py:407
  25.5 3.1 %collective-permute-done.8.refs_1_ = f32[128,256]{1,0:T(8,128)S(1)} collective-permute-done((f32[128,256]{1,0:T(8,128)S(1)}, f32[128,256]{1,0:T(8,128)S(1)}, u32[]{:S(2)}, u32[]{:S(2)}) %collective-permute-start.8) | collective-permute-done | bytes 131104 | tf_op jit(solution)/shard_map/ppermute | solution.py:320
  28.6 0.4 %join_maps.3 = (f32[128,256]{1,0:T(8,128)S(1)}, f32[8,128]{1,0:T(8,128)S(1)}) custom-call(f32[128,256]{1,0:T(8,128)S(1)} %score_strip.5.refs_0_, f32[128,256]{1,0:T(8,128)S(1)} %collective-permute-done.8.refs_1_, f32[256,256]{1,0:T(8,128)S(1)} %open_pixels.1.refs_2_, f32[8,128]{1,0:T(8,128)S(1)} %get-tuple-element.52.refs_3_), custom_call_target="tpu_custom_call" | custom-call | flops 100000000 | tf_op jit(solution)/shard_map/join_maps/pallas_call | solution.py:407
  28.9 0.9 %collective-permute-start.10 = (f32[8,128]{1,0:T(8,128)S(1)}, f32[8,128]{1,0:T(8,128)S(1)}, u32[]{:S(2)}, u32[]{:S(2)}) collective-permute-start(f32[8,128]{1,0:T(8,128)S(1)} %get-tuple-element.56.refs_0_), channel_id=1, source_target_pairs={{0,8},{4,12},{8,0},{12,4},{1,9},{5,13},{9,1},{13,5},{2,10},{6,14},... | collective-permute-start | bytes 12296 | tf_op jit(solution)/shard_map/ppermute | solution.py:316
  29.9 1.3 %collective-permute-start.9 = (f32[8,128]{1,0:T(8,128)S(1)}, f32[8,128]{1,0:T(8,128)S(1)}, u32[]{:S(2)}, u32[]{:S(2)}) collective-permute-start(f32[8,128]{1,0:T(8,128)S(1)} %get-tuple-element.56.refs_0_), channel_id=1, source_target_pairs={{0,4},{4,0},{8,12},{12,8},{1,5},{5,1},{9,13},{13,9},{2,6},{6,2},{1... | collective-permute-start | bytes 12296 | tf_op jit(solution)/shard_map/ppermute | solution.py:316
  31.2 0.6 %own_rows.1 = (f32[64,256]{1,0:T(8,128)S(1)}, f32[64,256]{1,0:T(8,128)S(1)}) custom-call(s32[1]{0:T(128)} %bitcast.place_ref, f32[128,256]{1,0:T(8,128)S(1)} %get-tuple-element.48.refs_0_, f32[128,256]{1,0:T(8,128)S(1)} %get-tuple-element.53.refs_1_, f32[256,256]{1,0:T(8,128)S(1)} %open_pixels.1.refs_2_), custom_call_target="tpu_custom_call" | custom-call | flops 1000000000 | tf_op jit(solution)/shard_map/own_rows/pallas_call | solution.py:407
  31.7 0.9 %collective-permute-done.10.refs_2_ = f32[8,128]{1,0:T(8,128)S(1)} collective-permute-done((f32[8,128]{1,0:T(8,128)S(1)}, f32[8,128]{1,0:T(8,128)S(1)}, u32[]{:S(2)}, u32[]{:S(2)}) %collective-permute-start.10) | collective-permute-done | bytes 4128 | tf_op jit(solution)/shard_map/ppermute | solution.py:316
  32.9 1.1 %normalise.1 = f32[64,256]{1,0:T(8,128)} custom-call(f32[64,256]{1,0:T(8,128)S(1)} %get-tuple-element.54.part_ref, f32[64,256]{1,0:T(8,128)S(1)} %get-tuple-element.55.open_ref, f32[8,128]{1,0:T(8,128)S(1)} %get-tuple-element.56.refs_0_, f32[8,128]{1,0:T(8,128)S(1)} %collective-permute-done.9.refs_1_, f32[8,128]{1,0:T(8,128)S(1)} %collective-permute-done.10.refs_2_, ...), custom_call_target="tpu_custom_call" | custom-call | flops 1000000000 | tf_op jit(solution)/shard_map/normalise/pallas_call | solution.py:407
  (18 shorter events, 0.5 us)
Async XLA Ops:
  0.7 5.2 %copy-start = (bf16[1792,256]{1,0:T(8,128)(2,1)S(1)}, bf16[1792,256]{1,0:T(8,128)(2,1)}, u32[]{:S(2)}) copy-start(bf16[1792,256]{1,0:T(8,128)(2,1)} %constant.9.clone.tab_ref.refs_4_.refs_1_) | copy-start | bytes 2752516
  0.7 5.2 %copy-start.1 = (f32[384,256]{1,0:T(8,128)S(1)}, f32[384,256]{1,0:T(8,128)}, u32[]{:S(2)}) copy-start(f32[384,256]{1,0:T(8,128)} %refs_2_) | copy-start | bytes 1179652
  1.7 7.9 %collective-permute-start.3 = (f32[136,128]{1,0:T(8,128)S(1)}, f32[136,128]{1,0:T(8,128)S(1)}, u32[]{:S(2)}, u32[]{:S(2)}) collective-permute-start(f32[136,128]{1,0:T(8,128)S(1)} %pack_weight.1.refs_5_.refs_0_.refs_2_), channel_id=1, source_target_pairs={{0,2},{1,3},{2,0},{3,1},{4,6},{5,7},{6,4},{7,5},{8,10},{9,11},{10,... | collective-permute-start | bytes 208904 | tf_op jit(solution)/shard_map/ppermute | solution.py:316
  6.0 5.5 %collective-permute-start = (f32[192,128]{1,0:T(8,128)S(1)}, f32[192,128]{1,0:T(8,128)S(1)}, u32[]{:S(2)}, u32[]{:S(2)}) collective-permute-start(f32[192,128]{1,0:T(8,128)S(1)} %get-tuple-element.32), channel_id=1, source_target_pairs={{0,4},{8,12},{4,0},{12,8},{1,5},{9,13},{5,1},{13,9},{2,6},{10,14},... | collective-permute-start | bytes 294920 | tf_op jit(solution)/shard_map/ppermute | solution.py:325
  6.0 5.4 %collective-permute-start.1 = (f32[192,128]{1,0:T(8,128)S(1)}, f32[192,128]{1,0:T(8,128)S(1)}, u32[]{:S(2)}, u32[]{:S(2)}) collective-permute-start(f32[192,128]{1,0:T(8,128)S(1)} %get-tuple-element.33), channel_id=1, source_target_pairs={{4,8},{8,4},{5,9},{9,5},{6,10},{10,6},{7,11},{11,7},{20,24},{24,20... | collective-permute-start | bytes 294920 | tf_op jit(solution)/shard_map/ppermute | solution.py:325
  6.7 4.7 %collective-permute-start.2 = (f32[136,128]{1,0:T(8,128)S(1)}, f32[136,128]{1,0:T(8,128)S(1)}, u32[]{:S(2)}, u32[]{:S(2)}) collective-permute-start(f32[136,128]{1,0:T(8,128)S(1)} %pack_weight.1.refs_5_.refs_0_.refs_2_), channel_id=1, source_target_pairs={{0,4},{4,0},{8,12},{12,8},{1,5},{5,1},{9,13},{13,9},{2,6},{6,2},{1... | collective-permute-start | bytes 208904 | tf_op jit(solution)/shard_map/ppermute | solution.py:320
  9.7 6.0 %collective-permute-start.4 = (f32[2,136,128]{2,1,0:T(8,128)S(1)}, f32[2,136,128]{2,1,0:T(8,128)S(1)}, u32[]{:S(2)}, u32[]{:S(2)}) collective-permute-start(f32[2,136,128]{2,1,0:T(8,128)S(1)} %stack_packs.1), channel_id=1, source_target_pairs={{0,8},{4,12},{8,0},{12,4},{1,9},{5,13},{9,1},{13,5},{2,10},{6,14},... | collective-permute-start | bytes 417800 | tf_op jit(solution)/shard_map/ppermute | solution.py:316
  11.4 2.3 %collective-permute-start.5 = (f32[136,128]{1,0:T(8,128)S(1)}, f32[136,128]{1,0:T(8,128)S(1)}, u32[]{:S(2)}, u32[]{:S(2)}) collective-permute-start(f32[136,128]{1,0:T(8,128)S(1)} %collective-permute-done.3.refs_1_.refs_4_), channel_id=1, source_target_pairs={{0,4},{4,0},{8,12},{12,8},{1,5},{5,1},{9,13},{13,9},{2,6},{6,2},{1... | collective-permute-start | bytes 208904 | tf_op jit(solution)/shard_map/ppermute | solution.py:320
  15.6 1.8 %collective-permute-start.6 = (f32[2,136,128]{2,1,0:T(8,128)S(1)}, f32[2,136,128]{2,1,0:T(8,128)S(1)}, u32[]{:S(2)}, u32[]{:S(2)}) collective-permute-start(f32[2,136,128]{2,1,0:T(8,128)S(1)} %collective-permute-done.4.refs_4_.refs_6_), channel_id=1, source_target_pairs={{0,4},{4,0},{8,12},{12,8},{1,5},{5,1},{9,13},{13,9},{2,6},{6,2},{1... | collective-permute-start | bytes 417800 | tf_op jit(solution)/shard_map/ppermute | solution.py:320
  19.3 5.8 %collective-permute-start.7 = (f32[128,256]{1,0:T(8,128)S(1)}, f32[128,256]{1,0:T(8,128)S(1)}, u32[]{:S(2)}, u32[]{:S(2)}) collective-permute-start(f32[128,256]{1,0:T(8,128)S(1)} %get-tuple-element.47.refs_0_), channel_id=1, source_target_pairs={{0,1},{1,0},{2,3},{3,2},{4,5},{5,4},{6,7},{7,6},{8,9},{9,8},{10,11... | collective-permute-start | bytes 393224 | tf_op jit(solution)/shard_map/ppermute | solution.py:320
  20.9 2.6 %copy-start.2 = (s32[16,16]{1,0:T(8,128)S(1)}, s32[16,16]{1,0:T(8,128)}, u32[]{:S(2)}) copy-start(s32[16,16]{1,0:T(8,128)} %mask_ref.1) | copy-start | bytes 3076
  23.0 5.5 %collective-permute-start.8 = (f32[128,256]{1,0:T(8,128)S(1)}, f32[128,256]{1,0:T(8,128)S(1)}, u32[]{:S(2)}, u32[]{:S(2)}) collective-permute-start(f32[128,256]{1,0:T(8,128)S(1)} %score_strip.5.refs_0_), channel_id=1, source_target_pairs={{0,1},{1,0},{2,3},{3,2},{4,5},{5,4},{6,7},{7,6},{8,9},{9,8},{10,11... | collective-permute-start | bytes 393224 | tf_op jit(solution)/shard_map/ppermute | solution.py:320
  28.9 3.7 %collective-permute-start.10 = (f32[8,128]{1,0:T(8,128)S(1)}, f32[8,128]{1,0:T(8,128)S(1)}, u32[]{:S(2)}, u32[]{:S(2)}) collective-permute-start(f32[8,128]{1,0:T(8,128)S(1)} %get-tuple-element.56.refs_0_), channel_id=1, source_target_pairs={{0,8},{4,12},{8,0},{12,4},{1,9},{5,13},{9,1},{13,5},{2,10},{6,14},... | collective-permute-start | bytes 12296 | tf_op jit(solution)/shard_map/ppermute | solution.py:316
  29.9 3.0 %collective-permute-start.11 = (f32[8,128]{1,0:T(8,128)S(1)}, f32[8,128]{1,0:T(8,128)S(1)}, u32[]{:S(2)}, u32[]{:S(2)}) collective-permute-start(f32[8,128]{1,0:T(8,128)S(1)} %get-tuple-element.56.refs_0_), channel_id=1, source_target_pairs={{0,12},{4,8},{8,4},{12,0},{1,13},{5,9},{9,5},{13,1},{2,14},{6,10},... | collective-permute-start | bytes 12296 | tf_op jit(solution)/shard_map/ppermute | solution.py:316
  29.9 3.0 %collective-permute-start.9 = (f32[8,128]{1,0:T(8,128)S(1)}, f32[8,128]{1,0:T(8,128)S(1)}, u32[]{:S(2)}, u32[]{:S(2)}) collective-permute-start(f32[8,128]{1,0:T(8,128)S(1)} %get-tuple-element.56.refs_0_), channel_id=1, source_target_pairs={{0,4},{4,0},{8,12},{12,8},{1,5},{5,1},{9,13},{13,9},{2,6},{6,2},{1... | collective-permute-start | bytes 12296 | tf_op jit(solution)/shard_map/ppermute | solution.py:316

commit v4 on v3

--- a/solution.py
+++ b/solution.py
@@ -269,10 +269,10 @@
     total = jnp.sum(pixels * values)
     deviation = values - total / jnp.maximum(count, 1.0)
     squares = jnp.sum(pixels * deviation * deviation)
-    lane = lax.broadcasted_iota(jnp.int32, stat_ref.shape, 1)
+    row = lax.broadcasted_iota(jnp.int32, stat_ref.shape, 0)
     stat = before[0][...] if before else jnp.zeros(stat_ref.shape, F32)
     for i, value in enumerate((count, total, squares)):
-        stat = jnp.where(lane == 3 * strip + i, value, stat)
+        stat = jnp.where(row == 3 * strip + i, value, stat)
     stat_ref[...] = stat
 
 
@@ -294,17 +294,19 @@
 
 def norm_kernel(n_strip, part_ref, open_ref, *refs):
     stats, out_ref = refs[:-1], refs[-1]
-    lanes = [(ref, 3 * strip) for ref in stats for strip in range(n_strip)]
-    counts = [ref[:, i : i + 1] for ref, i in lanes]
-    totals = [ref[:, i + 1 : i + 2] for ref, i in lanes]
+    rows = [(ref[...], 3 * strip) for ref in stats for strip in range(n_strip)]
+    counts = [stat[i : i + 1] for stat, i in rows]
+    totals = [stat[i + 1 : i + 2] for stat, i in rows]
     count, total = sum(counts), sum(totals)
     average = total / count
     squares = 0.0
-    for (ref, i), n, s in zip(lanes, counts, totals):
+    for (stat, i), n, s in zip(rows, counts, totals):
         apart = s / jnp.maximum(n, 1.0) - average
-        squares = squares + ref[:, i + 2 : i + 3] + n * apart * apart
+        squares = squares + stat[i + 2 : i + 3] + n * apart * apart
     scale = 1.0 / jnp.sqrt(squares / count + 1e-05)
-    out_ref[...] = open_ref[...] * (part_ref[...] - average[0:1]) * scale[0:1]
+    for i in range(0, out_ref.shape[1], LANES):
+        cols = slice(i, i + LANES)
+        out_ref[:, cols] = open_ref[:, cols] * (part_ref[:, cols] - average) * scale
 
 
 def shift(i, step, n):
@@ -426,7 +428,7 @@
 
     n_strip = tile // side
     held = call(stack_kernel, "stack_packs", COST, jax.ShapeDtypeStruct((1 + len(far), *pack.shape), F32), [], pack, *far)
-    near = [peer(held, "tile", t) for t in tile_steps[1:]]
+    relayed = [peer(held, "tile", t) for t in tile_steps[1:]]
     early = far + ([swap(x, "tile") for x in far] if tile_pairs else [])
     spec, *state, own_spectra = call(
         functools.partial(own_kernel, len(mine), 0),
@@ -476,8 +478,8 @@
     for group in chunks(early):
         state, spectra = score(group, [], state, 0, False, EARLY)
         done.append((group, spectra))
-    near, state = lax.optimization_barrier((near, state))
-    groups = chunks(near + ([swap(x, "tile") for x in near] if tile_pairs else []))
+    relayed, state = lax.optimization_barrier((relayed, state))
+    groups = chunks(relayed) + (chunks([swap(x, "tile") for x in relayed]) if tile_pairs else [])
     for i, group in enumerate(groups):
         state, spectra = score(group, [], state, 0, i == len(groups) - 1, REST)
         done.append((group, spectra))
@@ -493,7 +495,7 @@
         if orient_pairs:
             swapped.append(swap(state[0], "orient"))
     pixels = call(functools.partial(pixel_kernel, side), "open_pixels", 1, plane, [], ice_mask)
-    stat_shape = jax.ShapeDtypeStruct((8, LANES), F32)
+    stat_shape = jax.ShapeDtypeStruct((8 * (-(-3 * n_strip // 8)), LANES), F32)
     stat, strips = (), []
     for strip, maps in enumerate(zip(log_maps, swapped) if orient_pairs else zip(log_maps)):
         joined, *stat = call(

time: 34.2 us -> 33.7 us (0.985)
  waiting for transfers between devices: 7.08 us -> 6.13 us
  Pallas kernels: 11.4 us -> 11.9 us
    ppermute x5, waiting for transfers between devices: 5.31 us -> 3.98 us  [swap(): lax.ppermute(x, axis, [(i, i ^ 1) for i in range(lax.axis_size(axis))])]
    pallas_call x10 -> x11, Pallas kernels: 10.3 us -> 10.7 us  [call(): pl.pallas_call(kernel, out_shape=shapes, in_specs=[SMEM] * len(places) +...]
    ppermute x5, waiting for transfers between devices: 1.76 us -> 2.14 us  [peer(): return lax.ppermute(x, axis, [(i, shift(i, step, n)) for i in range(n)])]
  transfers between devices with their start and end apart: 12 -> 12, of which waited for: 6 -> 5; matrix products, arithmetic and copies ran while one was open for 0% -> 0% of each run, Pallas kernels for 21% -> 25%
where the time goes in v4:
time: 33.7 us; the launch traced here: 33.5 us
  starting transfers between devices  14.7 us (44%)
  Pallas kernels  11.9 us (35%)
  waiting for transfers between devices  6.13 us (18%)
  between operations  0.8 us (2%)
    pallas_call x11, Pallas kernels, call(): pl.pallas_call(kernel, out_shape=shapes, in_specs=[SMEM] * len(places) +...  10.7 us
    ppermute x5, starting transfers between devices, peer(): return lax.ppermute(x, axis, [(i, shift(i, step, n)) for i in range(n)])  8.05 us
    ppermute x5, starting transfers between devices, swap(): lax.ppermute(x, axis, [(i, i ^ 1) for i in range(lax.axis_size(axis))])  5.89 us
    ppermute x5, waiting for transfers between devices, swap(): lax.ppermute(x, axis, [(i, i ^ 1) for i in range(lax.axis_size(axis))])  3.98 us
    ppermute x5, waiting for transfers between devices, peer(): return lax.ppermute(x, axis, [(i, shift(i, step, n)) for i in range(n)])  2.14 us
    pallas_call x1, Pallas kernels, body(): pl.pallas_call(pack_kernel, out_shape=jax.ShapeDtypeStruct((side + PACK,...  1.04 us
    ppermute x2, starting transfers between devices, exchange(): return lax.ppermute(x, axis, pairs + [(j, i) for i, j in pairs])  0.74 us
  transfers between devices with their start and end apart: 12, of which 5 were waited for; matrix products, arithmetic and copies ran while one was open for 0% of the time, Pallas kernels for 25%

profile of v4, /device:TPU:0, one launch (start us, length us, event | category | flops | bytes accessed | tf_op | source)
XLA Modules:
  0.0 33.5 jit_solution(6440544391034052494)
XLA Ops:
  0.7 1.0 %pack_weight.1.refs_5_.refs_0_.refs_2_ = f32[136,128]{1,0:T(8,128)S(1)} custom-call(s32[1,1]{1,0:T(1,128)S(6)} %copy.7.ids_ref, f32[1,16]{1,0:T(1,128)} %bitcast.5, f32[128,128]{1,0:T(8,128)} %bitcast.4), custom_call_target="tpu_custom_call" | custom-call | flops 1000000000 | tf_op jit(solution)/shard_map/pack_weight/pallas_call | solution.py:371
  1.7 4.1 %collective-permute-start.3 = (f32[136,128]{1,0:T(8,128)S(1)}, f32[136,128]{1,0:T(8,128)S(1)}, u32[]{:S(2)}, u32[]{:S(2)}) collective-permute-start(f32[136,128]{1,0:T(8,128)S(1)} %pack_weight.1.refs_5_.refs_0_.refs_2_), channel_id=1, source_target_pairs={{0,2},{1,3},{2,0},{3,1},{4,6},{5,7},{6,4},{7,5},{8,10},{9,11},{10,... | collective-permute-start | bytes 208904 | tf_op jit(solution)/shard_map/ppermute | solution.py:318
  6.0 0.7 %collective-permute-start.1 = (f32[192,128]{1,0:T(8,128)S(1)}, f32[192,128]{1,0:T(8,128)S(1)}, u32[]{:S(2)}, u32[]{:S(2)}) collective-permute-start(f32[192,128]{1,0:T(8,128)S(1)} %get-tuple-element.36), channel_id=1, source_target_pairs={{4,8},{8,4},{5,9},{9,5},{6,10},{10,6},{7,11},{11,7},{20,24},{24,20... | collective-permute-start | bytes 294920 | tf_op jit(solution)/shard_map/ppermute | solution.py:327
  6.7 2.9 %collective-permute-start.2 = (f32[136,128]{1,0:T(8,128)S(1)}, f32[136,128]{1,0:T(8,128)S(1)}, u32[]{:S(2)}, u32[]{:S(2)}) collective-permute-start(f32[136,128]{1,0:T(8,128)S(1)} %pack_weight.1.refs_5_.refs_0_.refs_2_), channel_id=1, source_target_pairs={{0,4},{4,0},{8,12},{12,8},{1,5},{5,1},{9,13},{13,9},{2,6},{6,2},{1... | collective-permute-start | bytes 208904 | tf_op jit(solution)/shard_map/ppermute | solution.py:322
  9.7 1.7 %collective-permute-start.4 = (f32[2,136,128]{2,1,0:T(8,128)S(1)}, f32[2,136,128]{2,1,0:T(8,128)S(1)}, u32[]{:S(2)}, u32[]{:S(2)}) collective-permute-start(f32[2,136,128]{2,1,0:T(8,128)S(1)} %stack_packs.1), channel_id=1, source_target_pairs={{0,8},{4,12},{8,0},{12,4},{1,9},{5,13},{9,1},{13,5},{2,10},{6,14},... | collective-permute-start | bytes 417800 | tf_op jit(solution)/shard_map/ppermute | solution.py:318
  11.4 2.2 %own_block.1 = (f32[4,4,128,128]{3,2,1,0:T(8,128)S(1)}, f32[128,256]{1,0:T(8,128)S(1)}, f32[128,256]{1,0:T(8,128)S(1)}, f32[2,4,128,128]{3,2,1,0:T(8,128)S(1)}) custom-call(s32[1]{0:T(128)} %bitcast.1.spot_ref.refs_0_, f32[192,128]{1,0:T(8,128)S(1)} %collective-permute-done.refs_1_, f32[384,256]{1,0:T(8,128)S(1)} %copy-done.1, ...), custom_call_target="tpu_custom_call" | custom-call | flops 1000000000 | tf_op jit(solution)/shard_map/own_block/pallas_call | solution.py:409
  13.7 1.3 %score_strip.4 = (f32[128,256]{1,0:T(8,128)S(1)}, f32[128,256]{1,0:T(8,128)S(1)}, f32[2,4,128,128]{3,2,1,0:T(8,128)S(1)}) custom-call(f32[4,4,128,128]{3,2,1,0:T(8,128)S(1)} %get-tuple-element.38.refs_0_, bf16[1792,256]{1,0:T(8,128)(2,1)S(1)} %copy-done, f32[128,256]{1,0:T(8,128)S(1)} %get-tuple-element.41.refs_2_, ...), custom_call_target="tpu_custom_call" | custom-call | flops 200000000 | tf_op jit(solution)/shard_map/score_strip/pallas_call | solution.py:409
  15.0 0.6 %collective-permute-done.4.refs_4_.refs_6_ = f32[2,136,128]{2,1,0:T(8,128)S(1)} collective-permute-done((f32[2,136,128]{2,1,0:T(8,128)S(1)}, f32[2,136,128]{2,1,0:T(8,128)S(1)}, u32[]{:S(2)}, u32[]{:S(2)}) %collective-permute-start.4) | collective-permute-done | bytes 139296 | tf_op jit(solution)/shard_map/ppermute | solution.py:318
  15.6 0.8 %collective-permute-start.6 = (f32[2,136,128]{2,1,0:T(8,128)S(1)}, f32[2,136,128]{2,1,0:T(8,128)S(1)}, u32[]{:S(2)}, u32[]{:S(2)}) collective-permute-start(f32[2,136,128]{2,1,0:T(8,128)S(1)} %collective-permute-done.4.refs_4_.refs_6_), channel_id=1, source_target_pairs={{0,4},{4,0},{8,12},{12,8},{1,5},{5,1},{9,13},{13,9},{2,6},{6,2},{1... | collective-permute-start | bytes 417800 | tf_op jit(solution)/shard_map/ppermute | solution.py:322
  16.4 1.3 %score_strip.5 = (f32[128,256]{1,0:T(8,128)S(1)}, f32[128,256]{1,0:T(8,128)S(1)}, f32[2,4,128,128]{3,2,1,0:T(8,128)S(1)}) custom-call(f32[4,4,128,128]{3,2,1,0:T(8,128)S(1)} %get-tuple-element.38.refs_0_, bf16[1792,256]{1,0:T(8,128)(2,1)S(1)} %copy-done, f32[128,256]{1,0:T(8,128)S(1)} %get-tuple-element.47.refs_2_, ...), custom_call_target="tpu_custom_call" | custom-call | flops 400000000 | tf_op jit(solution)/shard_map/score_strip/pallas_call | solution.py:409
  17.8 1.4 %score_strip.6 = (f32[128,256]{1,0:T(8,128)S(1)}, f32[2,4,128,128]{3,2,1,0:T(8,128)S(1)}) custom-call(f32[4,4,128,128]{3,2,1,0:T(8,128)S(1)} %get-tuple-element.38.refs_0_, bf16[1792,256]{1,0:T(8,128)(2,1)S(1)} %copy-done, f32[128,256]{1,0:T(8,128)S(1)} %get-tuple-element.50.refs_2_, f32[128,256]{1,0:T(8,128)S(1)} %get-tuple-element.51.refs_3_, ...), custom_call_target="tpu_custom_call" | custom-call | flops 400000000 | tf_op jit(solution)/shard_map/score_strip/pallas_call | solution.py:409
  19.1 1.6 %collective-permute-start.7 = (f32[128,256]{1,0:T(8,128)S(1)}, f32[128,256]{1,0:T(8,128)S(1)}, u32[]{:S(2)}, u32[]{:S(2)}) collective-permute-start(f32[128,256]{1,0:T(8,128)S(1)} %get-tuple-element.52.refs_0_), channel_id=1, source_target_pairs={{0,1},{1,0},{2,3},{3,2},{4,5},{5,4},{6,7},{7,6},{8,9},{9,8},{10,11... | collective-permute-start | bytes 393224 | tf_op jit(solution)/shard_map/ppermute | solution.py:322
  20.8 2.1 %score_strip.7.refs_0_ = f32[128,256]{1,0:T(8,128)S(1)} custom-call(f32[4,4,128,128]{3,2,1,0:T(8,128)S(1)} %get-tuple-element.38.refs_0_, bf16[1792,256]{1,0:T(8,128)(2,1)S(1)} %copy-done, f32[136,128]{1,0:T(8,128)S(1)} %pack_weight.1.refs_5_.refs_0_.refs_2_, f32[136,128]{1,0:T(8,128)S(1)} %collective-permute-done.2.refs_6_.refs_3_, ...), custom_call_target="tpu_custom_call" | custom-call | flops 2000000000 | tf_op jit(solution)/shard_map/score_strip/pallas_call | solution.py:409
  22.9 0.5 %collective-permute-start.8 = (f32[128,256]{1,0:T(8,128)S(1)}, f32[128,256]{1,0:T(8,128)S(1)}, u32[]{:S(2)}, u32[]{:S(2)}) collective-permute-start(f32[128,256]{1,0:T(8,128)S(1)} %score_strip.7.refs_0_), channel_id=1, source_target_pairs={{0,1},{1,0},{2,3},{3,2},{4,5},{5,4},{6,7},{7,6},{8,9},{9,8},{10,11... | collective-permute-start | bytes 393224 | tf_op jit(solution)/shard_map/ppermute | solution.py:322
  23.8 0.8 %collective-permute-done.7.refs_1_ = f32[128,256]{1,0:T(8,128)S(1)} collective-permute-done((f32[128,256]{1,0:T(8,128)S(1)}, f32[128,256]{1,0:T(8,128)S(1)}, u32[]{:S(2)}, u32[]{:S(2)}) %collective-permute-start.7) | collective-permute-done | bytes 131104 | tf_op jit(solution)/shard_map/ppermute | solution.py:322
  24.6 0.4 %join_maps.2 = (f32[128,256]{1,0:T(8,128)S(1)}, f32[8,128]{1,0:T(8,128)S(1)}) custom-call(f32[128,256]{1,0:T(8,128)S(1)} %get-tuple-element.52.refs_0_, f32[128,256]{1,0:T(8,128)S(1)} %collective-permute-done.7.refs_1_, f32[256,256]{1,0:T(8,128)S(1)} %open_pixels.1.refs_2_), custom_call_target="tpu_custom_call" | custom-call | flops 100000000 | tf_op jit(solution)/shard_map/join_maps/pallas_call | solution.py:409
  25.0 3.1 %collective-permute-done.8.refs_1_ = f32[128,256]{1,0:T(8,128)S(1)} collective-permute-done((f32[128,256]{1,0:T(8,128)S(1)}, f32[128,256]{1,0:T(8,128)S(1)}, u32[]{:S(2)}, u32[]{:S(2)}) %collective-permute-start.8) | collective-permute-done | bytes 131104 | tf_op jit(solution)/shard_map/ppermute | solution.py:322
  28.1 0.4 %join_maps.3 = (f32[128,256]{1,0:T(8,128)S(1)}, f32[8,128]{1,0:T(8,128)S(1)}) custom-call(f32[128,256]{1,0:T(8,128)S(1)} %score_strip.7.refs_0_, f32[128,256]{1,0:T(8,128)S(1)} %collective-permute-done.8.refs_1_, f32[256,256]{1,0:T(8,128)S(1)} %open_pixels.1.refs_2_, f32[8,128]{1,0:T(8,128)S(1)} %get-tuple-element.58.refs_3_), custom_call_target="tpu_custom_call" | custom-call | flops 100000000 | tf_op jit(solution)/shard_map/join_maps/pallas_call | solution.py:409
  28.5 1.3 %collective-permute-start.10 = (f32[8,128]{1,0:T(8,128)S(1)}, f32[8,128]{1,0:T(8,128)S(1)}, u32[]{:S(2)}, u32[]{:S(2)}) collective-permute-start(f32[8,128]{1,0:T(8,128)S(1)} %get-tuple-element.62.refs_0_), channel_id=1, source_target_pairs={{0,8},{4,12},{8,0},{12,4},{1,9},{5,13},{9,1},{13,5},{2,10},{6,14},... | collective-permute-start | bytes 12296 | tf_op jit(solution)/shard_map/ppermute | solution.py:318
  29.8 0.9 %collective-permute-start.9 = (f32[8,128]{1,0:T(8,128)S(1)}, f32[8,128]{1,0:T(8,128)S(1)}, u32[]{:S(2)}, u32[]{:S(2)}) collective-permute-start(f32[8,128]{1,0:T(8,128)S(1)} %get-tuple-element.62.refs_0_), channel_id=1, source_target_pairs={{0,4},{4,0},{8,12},{12,8},{1,5},{5,1},{9,13},{13,9},{2,6},{6,2},{1... | collective-permute-start | bytes 12296 | tf_op jit(solution)/shard_map/ppermute | solution.py:318
  30.7 0.6 %own_rows.1 = (f32[64,256]{1,0:T(8,128)S(1)}, f32[64,256]{1,0:T(8,128)S(1)}) custom-call(s32[1]{0:T(128)} %bitcast.place_ref, f32[128,256]{1,0:T(8,128)S(1)} %get-tuple-element.53.refs_0_, f32[128,256]{1,0:T(8,128)S(1)} %get-tuple-element.59.refs_1_, f32[256,256]{1,0:T(8,128)S(1)} %open_pixels.1.refs_2_), custom_call_target="tpu_custom_call" | custom-call | flops 1000000000 | tf_op jit(solution)/shard_map/own_rows/pallas_call | solution.py:409
  31.3 0.9 %collective-permute-done.10.refs_2_ = f32[8,128]{1,0:T(8,128)S(1)} collective-permute-done((f32[8,128]{1,0:T(8,128)S(1)}, f32[8,128]{1,0:T(8,128)S(1)}, u32[]{:S(2)}, u32[]{:S(2)}) %collective-permute-start.10) | collective-permute-done | bytes 4128 | tf_op jit(solution)/shard_map/ppermute | solution.py:318
  32.2 0.6 %collective-permute-done.11.refs_3_ = f32[8,128]{1,0:T(8,128)S(1)} collective-permute-done((f32[8,128]{1,0:T(8,128)S(1)}, f32[8,128]{1,0:T(8,128)S(1)}, u32[]{:S(2)}, u32[]{:S(2)}) %collective-permute-start.11) | collective-permute-done | bytes 4128 | tf_op jit(solution)/shard_map/ppermute | solution.py:318
  32.8 0.7 %normalise.1 = f32[64,256]{1,0:T(8,128)} custom-call(f32[64,256]{1,0:T(8,128)S(1)} %get-tuple-element.60.part_ref, f32[64,256]{1,0:T(8,128)S(1)} %get-tuple-element.61.open_ref, f32[8,128]{1,0:T(8,128)S(1)} %get-tuple-element.62.refs_0_, f32[8,128]{1,0:T(8,128)S(1)} %collective-permute-done.9.refs_1_, f32[8,128]{1,0:T(8,128)S(1)} %collective-permute-done.10.refs_2_, ...), custom_call_target="tpu_custom_call" | custom-call | flops 1000000000 | tf_op jit(solution)/shard_map/normalise/pallas_call | solution.py:409
  (19 shorter events, 0.6 us)
Async XLA Ops:
  0.7 5.2 %copy-start = (bf16[1792,256]{1,0:T(8,128)(2,1)S(1)}, bf16[1792,256]{1,0:T(8,128)(2,1)}, u32[]{:S(2)}) copy-start(bf16[1792,256]{1,0:T(8,128)(2,1)} %constant.9.clone.tab_ref.refs_4_.refs_1_) | copy-start | bytes 2752516
  0.7 5.2 %copy-start.1 = (f32[384,256]{1,0:T(8,128)S(1)}, f32[384,256]{1,0:T(8,128)}, u32[]{:S(2)}) copy-start(f32[384,256]{1,0:T(8,128)} %refs_2_) | copy-start | bytes 1179652
  1.7 7.9 %collective-permute-start.3 = (f32[136,128]{1,0:T(8,128)S(1)}, f32[136,128]{1,0:T(8,128)S(1)}, u32[]{:S(2)}, u32[]{:S(2)}) collective-permute-start(f32[136,128]{1,0:T(8,128)S(1)} %pack_weight.1.refs_5_.refs_0_.refs_2_), channel_id=1, source_target_pairs={{0,2},{1,3},{2,0},{3,1},{4,6},{5,7},{6,4},{7,5},{8,10},{9,11},{10,... | collective-permute-start | bytes 208904 | tf_op jit(solution)/shard_map/ppermute | solution.py:318
  6.0 5.5 %collective-permute-start = (f32[192,128]{1,0:T(8,128)S(1)}, f32[192,128]{1,0:T(8,128)S(1)}, u32[]{:S(2)}, u32[]{:S(2)}) collective-permute-start(f32[192,128]{1,0:T(8,128)S(1)} %get-tuple-element.35), channel_id=1, source_target_pairs={{0,4},{8,12},{4,0},{12,8},{1,5},{9,13},{5,1},{13,9},{2,6},{10,14},... | collective-permute-start | bytes 294920 | tf_op jit(solution)/shard_map/ppermute | solution.py:327
  6.0 5.4 %collective-permute-start.1 = (f32[192,128]{1,0:T(8,128)S(1)}, f32[192,128]{1,0:T(8,128)S(1)}, u32[]{:S(2)}, u32[]{:S(2)}) collective-permute-start(f32[192,128]{1,0:T(8,128)S(1)} %get-tuple-element.36), channel_id=1, source_target_pairs={{4,8},{8,4},{5,9},{9,5},{6,10},{10,6},{7,11},{11,7},{20,24},{24,20... | collective-permute-start | bytes 294920 | tf_op jit(solution)/shard_map/ppermute | solution.py:327
  6.7 4.7 %collective-permute-start.2 = (f32[136,128]{1,0:T(8,128)S(1)}, f32[136,128]{1,0:T(8,128)S(1)}, u32[]{:S(2)}, u32[]{:S(2)}) collective-permute-start(f32[136,128]{1,0:T(8,128)S(1)} %pack_weight.1.refs_5_.refs_0_.refs_2_), channel_id=1, source_target_pairs={{0,4},{4,0},{8,12},{12,8},{1,5},{5,1},{9,13},{13,9},{2,6},{6,2},{1... | collective-permute-start | bytes 208904 | tf_op jit(solution)/shard_map/ppermute | solution.py:322
  9.7 6.0 %collective-permute-start.4 = (f32[2,136,128]{2,1,0:T(8,128)S(1)}, f32[2,136,128]{2,1,0:T(8,128)S(1)}, u32[]{:S(2)}, u32[]{:S(2)}) collective-permute-start(f32[2,136,128]{2,1,0:T(8,128)S(1)} %stack_packs.1), channel_id=1, source_target_pairs={{0,8},{4,12},{8,0},{12,4},{1,9},{5,13},{9,1},{13,5},{2,10},{6,14},... | collective-permute-start | bytes 417800 | tf_op jit(solution)/shard_map/ppermute | solution.py:318
  11.4 2.2 %collective-permute-start.5 = (f32[136,128]{1,0:T(8,128)S(1)}, f32[136,128]{1,0:T(8,128)S(1)}, u32[]{:S(2)}, u32[]{:S(2)}) collective-permute-start(f32[136,128]{1,0:T(8,128)S(1)} %collective-permute-done.3.refs_1_.refs_4_), channel_id=1, source_target_pairs={{0,4},{4,0},{8,12},{12,8},{1,5},{5,1},{9,13},{13,9},{2,6},{6,2},{1... | collective-permute-start | bytes 208904 | tf_op jit(solution)/shard_map/ppermute | solution.py:322
  15.6 2.1 %collective-permute-start.6 = (f32[2,136,128]{2,1,0:T(8,128)S(1)}, f32[2,136,128]{2,1,0:T(8,128)S(1)}, u32[]{:S(2)}, u32[]{:S(2)}) collective-permute-start(f32[2,136,128]{2,1,0:T(8,128)S(1)} %collective-permute-done.4.refs_4_.refs_6_), channel_id=1, source_target_pairs={{0,4},{4,0},{8,12},{12,8},{1,5},{5,1},{9,13},{13,9},{2,6},{6,2},{1... | collective-permute-start | bytes 417800 | tf_op jit(solution)/shard_map/ppermute | solution.py:322
  19.1 5.5 %collective-permute-start.7 = (f32[128,256]{1,0:T(8,128)S(1)}, f32[128,256]{1,0:T(8,128)S(1)}, u32[]{:S(2)}, u32[]{:S(2)}) collective-permute-start(f32[128,256]{1,0:T(8,128)S(1)} %get-tuple-element.52.refs_0_), channel_id=1, source_target_pairs={{0,1},{1,0},{2,3},{3,2},{4,5},{5,4},{6,7},{7,6},{8,9},{9,8},{10,11... | collective-permute-start | bytes 393224 | tf_op jit(solution)/shard_map/ppermute | solution.py:322
  20.8 2.7 %copy-start.2 = (s32[16,16]{1,0:T(8,128)S(1)}, s32[16,16]{1,0:T(8,128)}, u32[]{:S(2)}) copy-start(s32[16,16]{1,0:T(8,128)} %mask_ref.1) | copy-start | bytes 3076
  22.9 5.2 %collective-permute-start.8 = (f32[128,256]{1,0:T(8,128)S(1)}, f32[128,256]{1,0:T(8,128)S(1)}, u32[]{:S(2)}, u32[]{:S(2)}) collective-permute-start(f32[128,256]{1,0:T(8,128)S(1)} %score_strip.7.refs_0_), channel_id=1, source_target_pairs={{0,1},{1,0},{2,3},{3,2},{4,5},{5,4},{6,7},{7,6},{8,9},{9,8},{10,11... | collective-permute-start | bytes 393224 | tf_op jit(solution)/shard_map/ppermute | solution.py:322
  28.5 3.7 %collective-permute-start.10 = (f32[8,128]{1,0:T(8,128)S(1)}, f32[8,128]{1,0:T(8,128)S(1)}, u32[]{:S(2)}, u32[]{:S(2)}) collective-permute-start(f32[8,128]{1,0:T(8,128)S(1)} %get-tuple-element.62.refs_0_), channel_id=1, source_target_pairs={{0,8},{4,12},{8,0},{12,4},{1,9},{5,13},{9,1},{13,5},{2,10},{6,14},... | collective-permute-start | bytes 12296 | tf_op jit(solution)/shard_map/ppermute | solution.py:318
  29.8 3.0 %collective-permute-start.11 = (f32[8,128]{1,0:T(8,128)S(1)}, f32[8,128]{1,0:T(8,128)S(1)}, u32[]{:S(2)}, u32[]{:S(2)}) collective-permute-start(f32[8,128]{1,0:T(8,128)S(1)} %get-tuple-element.62.refs_0_), channel_id=1, source_target_pairs={{0,12},{4,8},{8,4},{12,0},{1,13},{5,9},{9,5},{13,1},{2,14},{6,10},... | collective-permute-start | bytes 12296 | tf_op jit(solution)/shard_map/ppermute | solution.py:318
  29.8 3.0 %collective-permute-start.9 = (f32[8,128]{1,0:T(8,128)S(1)}, f32[8,128]{1,0:T(8,128)S(1)}, u32[]{:S(2)}, u32[]{:S(2)}) collective-permute-start(f32[8,128]{1,0:T(8,128)S(1)} %get-tuple-element.62.refs_0_), channel_id=1, source_target_pairs={{0,4},{4,0},{8,12},{12,8},{1,5},{5,1},{9,13},{13,9},{2,6},{6,2},{1... | collective-permute-start | bytes 12296 | tf_op jit(solution)/shard_map/ppermute | solution.py:318

commit v5 on v4

--- a/solution.py
+++ b/solution.py
@@ -324,7 +324,7 @@
 
 def exchange(x, axis, start):
     pairs = [(i, i + 1) for i in range(start, lax.axis_size(axis) - 1, 2)]
-    return lax.ppermute(x, axis, pairs + [(j, i) for i, j in pairs])
+    return lax.ppermute(x, axis, pairs + [(j, i) for i, j in pairs]) if pairs else jnp.zeros_like(x)
 
 
 def pack_kernel(ids_ref, weight_ref, patch_ref, pack_ref, weights, sems):
@@ -483,8 +483,8 @@
     for i, group in enumerate(groups):
         state, spectra = score(group, [], state, 0, i == len(groups) - 1, REST)
         done.append((group, spectra))
-    log_maps = [state[0]]
-    swapped = [swap(state[0], "orient")] if orient_pairs else []
+    log_maps = [state[0] if groups else state[0] + jnp.log(state[1])]
+    swapped = [swap(log_maps[0], "orient")] if orient_pairs else []
     if sum(size(arrays) for arrays, _ in done) <= CHUNK:
         done = [([x for arrays, _ in done for x in arrays], [x for _, spectra in done for x in spectra])]
     for strip in range(1, n_strip):

time: 33.7 us -> 33.7 us (level)
  no operation moved by 1% of the time
where the time goes in v5:
time: 33.7 us; the launch traced here: 33.5 us
  starting transfers between devices  14.7 us (44%)
  Pallas kernels  11.9 us (35%)
  waiting for transfers between devices  6.13 us (18%)
  between operations  0.8 us (2%)
    pallas_call x11, Pallas kernels, call(): pl.pallas_call(kernel, out_shape=shapes, in_specs=[SMEM] * len(places) +...  10.7 us
    ppermute x5, starting transfers between devices, peer(): return lax.ppermute(x, axis, [(i, shift(i, step, n)) for i in range(n)])  8.05 us
    ppermute x5, starting transfers between devices, swap(): lax.ppermute(x, axis, [(i, i ^ 1) for i in range(lax.axis_size(axis))])  5.89 us
    ppermute x5, waiting for transfers between devices, swap(): lax.ppermute(x, axis, [(i, i ^ 1) for i in range(lax.axis_size(axis))])  3.98 us
    ppermute x5, waiting for transfers between devices, peer(): return lax.ppermute(x, axis, [(i, shift(i, step, n)) for i in range(n)])  2.14 us
    pallas_call x1, Pallas kernels, body(): pl.pallas_call(pack_kernel, out_shape=jax.ShapeDtypeStruct((side + PACK,...  1.04 us
    ppermute x2, starting transfers between devices, exchange(): lax.ppermute(x, axis, pairs + [(j, i) for i, j in pairs])  0.74 us
  transfers between devices with their start and end apart: 12, of which 5 were waited for; matrix products, arithmetic and copies ran while one was open for 0% of the time, Pallas kernels for 25%

profile of v5, /device:TPU:0, one launch (start us, length us, event | category | flops | bytes accessed | tf_op | source)
XLA Modules:
  0.0 33.5 jit_solution(6440544391034052494)
XLA Ops:
  0.7 1.0 %pack_weight.1.refs_5_.refs_0_.refs_2_ = f32[136,128]{1,0:T(8,128)S(1)} custom-call(s32[1,1]{1,0:T(1,128)S(6)} %copy.7.ids_ref, f32[1,16]{1,0:T(1,128)} %bitcast.5, f32[128,128]{1,0:T(8,128)} %bitcast.4), custom_call_target="tpu_custom_call" | custom-call | flops 1000000000 | tf_op jit(solution)/shard_map/pack_weight/pallas_call | solution.py:371
  1.7 4.1 %collective-permute-start.3 = (f32[136,128]{1,0:T(8,128)S(1)}, f32[136,128]{1,0:T(8,128)S(1)}, u32[]{:S(2)}, u32[]{:S(2)}) collective-permute-start(f32[136,128]{1,0:T(8,128)S(1)} %pack_weight.1.refs_5_.refs_0_.refs_2_), channel_id=1, source_target_pairs={{0,2},{1,3},{2,0},{3,1},{4,6},{5,7},{6,4},{7,5},{8,10},{9,11},{10,... | collective-permute-start | bytes 208904 | tf_op jit(solution)/shard_map/ppermute | solution.py:318
  6.0 0.7 %collective-permute-start.1 = (f32[192,128]{1,0:T(8,128)S(1)}, f32[192,128]{1,0:T(8,128)S(1)}, u32[]{:S(2)}, u32[]{:S(2)}) collective-permute-start(f32[192,128]{1,0:T(8,128)S(1)} %get-tuple-element.36), channel_id=1, source_target_pairs={{4,8},{8,4},{5,9},{9,5},{6,10},{10,6},{7,11},{11,7},{20,24},{24,20... | collective-permute-start | bytes 294920 | tf_op jit(solution)/shard_map/ppermute | solution.py:327
  6.7 2.9 %collective-permute-start.2 = (f32[136,128]{1,0:T(8,128)S(1)}, f32[136,128]{1,0:T(8,128)S(1)}, u32[]{:S(2)}, u32[]{:S(2)}) collective-permute-start(f32[136,128]{1,0:T(8,128)S(1)} %pack_weight.1.refs_5_.refs_0_.refs_2_), channel_id=1, source_target_pairs={{0,4},{4,0},{8,12},{12,8},{1,5},{5,1},{9,13},{13,9},{2,6},{6,2},{1... | collective-permute-start | bytes 208904 | tf_op jit(solution)/shard_map/ppermute | solution.py:322
  9.7 1.7 %collective-permute-start.4 = (f32[2,136,128]{2,1,0:T(8,128)S(1)}, f32[2,136,128]{2,1,0:T(8,128)S(1)}, u32[]{:S(2)}, u32[]{:S(2)}) collective-permute-start(f32[2,136,128]{2,1,0:T(8,128)S(1)} %stack_packs.1), channel_id=1, source_target_pairs={{0,8},{4,12},{8,0},{12,4},{1,9},{5,13},{9,1},{13,5},{2,10},{6,14},... | collective-permute-start | bytes 417800 | tf_op jit(solution)/shard_map/ppermute | solution.py:318
  11.4 2.2 %own_block.1 = (f32[4,4,128,128]{3,2,1,0:T(8,128)S(1)}, f32[128,256]{1,0:T(8,128)S(1)}, f32[128,256]{1,0:T(8,128)S(1)}, f32[2,4,128,128]{3,2,1,0:T(8,128)S(1)}) custom-call(s32[1]{0:T(128)} %bitcast.1.spot_ref.refs_0_, f32[192,128]{1,0:T(8,128)S(1)} %collective-permute-done.refs_1_, f32[384,256]{1,0:T(8,128)S(1)} %copy-done.1, ...), custom_call_target="tpu_custom_call" | custom-call | flops 1000000000 | tf_op jit(solution)/shard_map/own_block/pallas_call | solution.py:409
  13.7 1.3 %score_strip.4 = (f32[128,256]{1,0:T(8,128)S(1)}, f32[128,256]{1,0:T(8,128)S(1)}, f32[2,4,128,128]{3,2,1,0:T(8,128)S(1)}) custom-call(f32[4,4,128,128]{3,2,1,0:T(8,128)S(1)} %get-tuple-element.38.refs_0_, bf16[1792,256]{1,0:T(8,128)(2,1)S(1)} %copy-done, f32[128,256]{1,0:T(8,128)S(1)} %get-tuple-element.41.refs_2_, ...), custom_call_target="tpu_custom_call" | custom-call | flops 200000000 | tf_op jit(solution)/shard_map/score_strip/pallas_call | solution.py:409
  15.0 0.6 %collective-permute-done.4.refs_4_.refs_6_ = f32[2,136,128]{2,1,0:T(8,128)S(1)} collective-permute-done((f32[2,136,128]{2,1,0:T(8,128)S(1)}, f32[2,136,128]{2,1,0:T(8,128)S(1)}, u32[]{:S(2)}, u32[]{:S(2)}) %collective-permute-start.4) | collective-permute-done | bytes 139296 | tf_op jit(solution)/shard_map/ppermute | solution.py:318
  15.6 0.8 %collective-permute-start.6 = (f32[2,136,128]{2,1,0:T(8,128)S(1)}, f32[2,136,128]{2,1,0:T(8,128)S(1)}, u32[]{:S(2)}, u32[]{:S(2)}) collective-permute-start(f32[2,136,128]{2,1,0:T(8,128)S(1)} %collective-permute-done.4.refs_4_.refs_6_), channel_id=1, source_target_pairs={{0,4},{4,0},{8,12},{12,8},{1,5},{5,1},{9,13},{13,9},{2,6},{6,2},{1... | collective-permute-start | bytes 417800 | tf_op jit(solution)/shard_map/ppermute | solution.py:322
  16.4 1.3 %score_strip.5 = (f32[128,256]{1,0:T(8,128)S(1)}, f32[128,256]{1,0:T(8,128)S(1)}, f32[2,4,128,128]{3,2,1,0:T(8,128)S(1)}) custom-call(f32[4,4,128,128]{3,2,1,0:T(8,128)S(1)} %get-tuple-element.38.refs_0_, bf16[1792,256]{1,0:T(8,128)(2,1)S(1)} %copy-done, f32[128,256]{1,0:T(8,128)S(1)} %get-tuple-element.47.refs_2_, ...), custom_call_target="tpu_custom_call" | custom-call | flops 400000000 | tf_op jit(solution)/shard_map/score_strip/pallas_call | solution.py:409
  17.8 1.4 %score_strip.6 = (f32[128,256]{1,0:T(8,128)S(1)}, f32[2,4,128,128]{3,2,1,0:T(8,128)S(1)}) custom-call(f32[4,4,128,128]{3,2,1,0:T(8,128)S(1)} %get-tuple-element.38.refs_0_, bf16[1792,256]{1,0:T(8,128)(2,1)S(1)} %copy-done, f32[128,256]{1,0:T(8,128)S(1)} %get-tuple-element.50.refs_2_, f32[128,256]{1,0:T(8,128)S(1)} %get-tuple-element.51.refs_3_, ...), custom_call_target="tpu_custom_call" | custom-call | flops 400000000 | tf_op jit(solution)/shard_map/score_strip/pallas_call | solution.py:409
  19.1 1.6 %collective-permute-start.7 = (f32[128,256]{1,0:T(8,128)S(1)}, f32[128,256]{1,0:T(8,128)S(1)}, u32[]{:S(2)}, u32[]{:S(2)}) collective-permute-start(f32[128,256]{1,0:T(8,128)S(1)} %get-tuple-element.52.refs_0_), channel_id=1, source_target_pairs={{0,1},{1,0},{2,3},{3,2},{4,5},{5,4},{6,7},{7,6},{8,9},{9,8},{10,11... | collective-permute-start | bytes 393224 | tf_op jit(solution)/shard_map/ppermute | solution.py:322
  20.8 2.1 %score_strip.7.refs_0_ = f32[128,256]{1,0:T(8,128)S(1)} custom-call(f32[4,4,128,128]{3,2,1,0:T(8,128)S(1)} %get-tuple-element.38.refs_0_, bf16[1792,256]{1,0:T(8,128)(2,1)S(1)} %copy-done, f32[136,128]{1,0:T(8,128)S(1)} %pack_weight.1.refs_5_.refs_0_.refs_2_, f32[136,128]{1,0:T(8,128)S(1)} %collective-permute-done.2.refs_6_.refs_3_, ...), custom_call_target="tpu_custom_call" | custom-call | flops 2000000000 | tf_op jit(solution)/shard_map/score_strip/pallas_call | solution.py:409
  22.9 0.5 %collective-permute-start.8 = (f32[128,256]{1,0:T(8,128)S(1)}, f32[128,256]{1,0:T(8,128)S(1)}, u32[]{:S(2)}, u32[]{:S(2)}) collective-permute-start(f32[128,256]{1,0:T(8,128)S(1)} %score_strip.7.refs_0_), channel_id=1, source_target_pairs={{0,1},{1,0},{2,3},{3,2},{4,5},{5,4},{6,7},{7,6},{8,9},{9,8},{10,11... | collective-permute-start | bytes 393224 | tf_op jit(solution)/shard_map/ppermute | solution.py:322
  23.8 0.8 %collective-permute-done.7.refs_1_ = f32[128,256]{1,0:T(8,128)S(1)} collective-permute-done((f32[128,256]{1,0:T(8,128)S(1)}, f32[128,256]{1,0:T(8,128)S(1)}, u32[]{:S(2)}, u32[]{:S(2)}) %collective-permute-start.7) | collective-permute-done | bytes 131104 | tf_op jit(solution)/shard_map/ppermute | solution.py:322
  24.6 0.4 %join_maps.2 = (f32[128,256]{1,0:T(8,128)S(1)}, f32[8,128]{1,0:T(8,128)S(1)}) custom-call(f32[128,256]{1,0:T(8,128)S(1)} %get-tuple-element.52.refs_0_, f32[128,256]{1,0:T(8,128)S(1)} %collective-permute-done.7.refs_1_, f32[256,256]{1,0:T(8,128)S(1)} %open_pixels.1.refs_2_), custom_call_target="tpu_custom_call" | custom-call | flops 100000000 | tf_op jit(solution)/shard_map/join_maps/pallas_call | solution.py:409
  25.0 3.1 %collective-permute-done.8.refs_1_ = f32[128,256]{1,0:T(8,128)S(1)} collective-permute-done((f32[128,256]{1,0:T(8,128)S(1)}, f32[128,256]{1,0:T(8,128)S(1)}, u32[]{:S(2)}, u32[]{:S(2)}) %collective-permute-start.8) | collective-permute-done | bytes 131104 | tf_op jit(solution)/shard_map/ppermute | solution.py:322
  28.1 0.4 %join_maps.3 = (f32[128,256]{1,0:T(8,128)S(1)}, f32[8,128]{1,0:T(8,128)S(1)}) custom-call(f32[128,256]{1,0:T(8,128)S(1)} %score_strip.7.refs_0_, f32[128,256]{1,0:T(8,128)S(1)} %collective-permute-done.8.refs_1_, f32[256,256]{1,0:T(8,128)S(1)} %open_pixels.1.refs_2_, f32[8,128]{1,0:T(8,128)S(1)} %get-tuple-element.58.refs_3_), custom_call_target="tpu_custom_call" | custom-call | flops 100000000 | tf_op jit(solution)/shard_map/join_maps/pallas_call | solution.py:409
  28.5 1.3 %collective-permute-start.10 = (f32[8,128]{1,0:T(8,128)S(1)}, f32[8,128]{1,0:T(8,128)S(1)}, u32[]{:S(2)}, u32[]{:S(2)}) collective-permute-start(f32[8,128]{1,0:T(8,128)S(1)} %get-tuple-element.62.refs_0_), channel_id=1, source_target_pairs={{0,8},{4,12},{8,0},{12,4},{1,9},{5,13},{9,1},{13,5},{2,10},{6,14},... | collective-permute-start | bytes 12296 | tf_op jit(solution)/shard_map/ppermute | solution.py:318
  29.8 0.9 %collective-permute-start.9 = (f32[8,128]{1,0:T(8,128)S(1)}, f32[8,128]{1,0:T(8,128)S(1)}, u32[]{:S(2)}, u32[]{:S(2)}) collective-permute-start(f32[8,128]{1,0:T(8,128)S(1)} %get-tuple-element.62.refs_0_), channel_id=1, source_target_pairs={{0,4},{4,0},{8,12},{12,8},{1,5},{5,1},{9,13},{13,9},{2,6},{6,2},{1... | collective-permute-start | bytes 12296 | tf_op jit(solution)/shard_map/ppermute | solution.py:318
  30.7 0.6 %own_rows.1 = (f32[64,256]{1,0:T(8,128)S(1)}, f32[64,256]{1,0:T(8,128)S(1)}) custom-call(s32[1]{0:T(128)} %bitcast.place_ref, f32[128,256]{1,0:T(8,128)S(1)} %get-tuple-element.53.refs_0_, f32[128,256]{1,0:T(8,128)S(1)} %get-tuple-element.59.refs_1_, f32[256,256]{1,0:T(8,128)S(1)} %open_pixels.1.refs_2_), custom_call_target="tpu_custom_call" | custom-call | flops 1000000000 | tf_op jit(solution)/shard_map/own_rows/pallas_call | solution.py:409
  31.3 0.9 %collective-permute-done.10.refs_2_ = f32[8,128]{1,0:T(8,128)S(1)} collective-permute-done((f32[8,128]{1,0:T(8,128)S(1)}, f32[8,128]{1,0:T(8,128)S(1)}, u32[]{:S(2)}, u32[]{:S(2)}) %collective-permute-start.10) | collective-permute-done | bytes 4128 | tf_op jit(solution)/shard_map/ppermute | solution.py:318
  32.2 0.6 %collective-permute-done.11.refs_3_ = f32[8,128]{1,0:T(8,128)S(1)} collective-permute-done((f32[8,128]{1,0:T(8,128)S(1)}, f32[8,128]{1,0:T(8,128)S(1)}, u32[]{:S(2)}, u32[]{:S(2)}) %collective-permute-start.11) | collective-permute-done | bytes 4128 | tf_op jit(solution)/shard_map/ppermute | solution.py:318
  32.8 0.7 %normalise.1 = f32[64,256]{1,0:T(8,128)} custom-call(f32[64,256]{1,0:T(8,128)S(1)} %get-tuple-element.60.part_ref, f32[64,256]{1,0:T(8,128)S(1)} %get-tuple-element.61.open_ref, f32[8,128]{1,0:T(8,128)S(1)} %get-tuple-element.62.refs_0_, f32[8,128]{1,0:T(8,128)S(1)} %collective-permute-done.9.refs_1_, f32[8,128]{1,0:T(8,128)S(1)} %collective-permute-done.10.refs_2_, ...), custom_call_target="tpu_custom_call" | custom-call | flops 1000000000 | tf_op jit(solution)/shard_map/normalise/pallas_call | solution.py:409
  (19 shorter events, 0.6 us)
Async XLA Ops:
  0.7 5.2 %copy-start = (bf16[1792,256]{1,0:T(8,128)(2,1)S(1)}, bf16[1792,256]{1,0:T(8,128)(2,1)}, u32[]{:S(2)}) copy-start(bf16[1792,256]{1,0:T(8,128)(2,1)} %constant.9.clone.tab_ref.refs_4_.refs_1_) | copy-start | bytes 2752516
  0.7 5.2 %copy-start.1 = (f32[384,256]{1,0:T(8,128)S(1)}, f32[384,256]{1,0:T(8,128)}, u32[]{:S(2)}) copy-start(f32[384,256]{1,0:T(8,128)} %refs_2_) | copy-start | bytes 1179652
  1.7 7.9 %collective-permute-start.3 = (f32[136,128]{1,0:T(8,128)S(1)}, f32[136,128]{1,0:T(8,128)S(1)}, u32[]{:S(2)}, u32[]{:S(2)}) collective-permute-start(f32[136,128]{1,0:T(8,128)S(1)} %pack_weight.1.refs_5_.refs_0_.refs_2_), channel_id=1, source_target_pairs={{0,2},{1,3},{2,0},{3,1},{4,6},{5,7},{6,4},{7,5},{8,10},{9,11},{10,... | collective-permute-start | bytes 208904 | tf_op jit(solution)/shard_map/ppermute | solution.py:318
  6.0 5.5 %collective-permute-start = (f32[192,128]{1,0:T(8,128)S(1)}, f32[192,128]{1,0:T(8,128)S(1)}, u32[]{:S(2)}, u32[]{:S(2)}) collective-permute-start(f32[192,128]{1,0:T(8,128)S(1)} %get-tuple-element.35), channel_id=1, source_target_pairs={{0,4},{8,12},{4,0},{12,8},{1,5},{9,13},{5,1},{13,9},{2,6},{10,14},... | collective-permute-start | bytes 294920 | tf_op jit(solution)/shard_map/ppermute | solution.py:327
  6.0 5.4 %collective-permute-start.1 = (f32[192,128]{1,0:T(8,128)S(1)}, f32[192,128]{1,0:T(8,128)S(1)}, u32[]{:S(2)}, u32[]{:S(2)}) collective-permute-start(f32[192,128]{1,0:T(8,128)S(1)} %get-tuple-element.36), channel_id=1, source_target_pairs={{4,8},{8,4},{5,9},{9,5},{6,10},{10,6},{7,11},{11,7},{20,24},{24,20... | collective-permute-start | bytes 294920 | tf_op jit(solution)/shard_map/ppermute | solution.py:327
  6.7 4.7 %collective-permute-start.2 = (f32[136,128]{1,0:T(8,128)S(1)}, f32[136,128]{1,0:T(8,128)S(1)}, u32[]{:S(2)}, u32[]{:S(2)}) collective-permute-start(f32[136,128]{1,0:T(8,128)S(1)} %pack_weight.1.refs_5_.refs_0_.refs_2_), channel_id=1, source_target_pairs={{0,4},{4,0},{8,12},{12,8},{1,5},{5,1},{9,13},{13,9},{2,6},{6,2},{1... | collective-permute-start | bytes 208904 | tf_op jit(solution)/shard_map/ppermute | solution.py:322
  9.7 6.0 %collective-permute-start.4 = (f32[2,136,128]{2,1,0:T(8,128)S(1)}, f32[2,136,128]{2,1,0:T(8,128)S(1)}, u32[]{:S(2)}, u32[]{:S(2)}) collective-permute-start(f32[2,136,128]{2,1,0:T(8,128)S(1)} %stack_packs.1), channel_id=1, source_target_pairs={{0,8},{4,12},{8,0},{12,4},{1,9},{5,13},{9,1},{13,5},{2,10},{6,14},... | collective-permute-start | bytes 417800 | tf_op jit(solution)/shard_map/ppermute | solution.py:318
  11.4 2.2 %collective-permute-start.5 = (f32[136,128]{1,0:T(8,128)S(1)}, f32[136,128]{1,0:T(8,128)S(1)}, u32[]{:S(2)}, u32[]{:S(2)}) collective-permute-start(f32[136,128]{1,0:T(8,128)S(1)} %collective-permute-done.3.refs_1_.refs_4_), channel_id=1, source_target_pairs={{0,4},{4,0},{8,12},{12,8},{1,5},{5,1},{9,13},{13,9},{2,6},{6,2},{1... | collective-permute-start | bytes 208904 | tf_op jit(solution)/shard_map/ppermute | solution.py:322
  15.6 2.1 %collective-permute-start.6 = (f32[2,136,128]{2,1,0:T(8,128)S(1)}, f32[2,136,128]{2,1,0:T(8,128)S(1)}, u32[]{:S(2)}, u32[]{:S(2)}) collective-permute-start(f32[2,136,128]{2,1,0:T(8,128)S(1)} %collective-permute-done.4.refs_4_.refs_6_), channel_id=1, source_target_pairs={{0,4},{4,0},{8,12},{12,8},{1,5},{5,1},{9,13},{13,9},{2,6},{6,2},{1... | collective-permute-start | bytes 417800 | tf_op jit(solution)/shard_map/ppermute | solution.py:322
  19.1 5.5 %collective-permute-start.7 = (f32[128,256]{1,0:T(8,128)S(1)}, f32[128,256]{1,0:T(8,128)S(1)}, u32[]{:S(2)}, u32[]{:S(2)}) collective-permute-start(f32[128,256]{1,0:T(8,128)S(1)} %get-tuple-element.52.refs_0_), channel_id=1, source_target_pairs={{0,1},{1,0},{2,3},{3,2},{4,5},{5,4},{6,7},{7,6},{8,9},{9,8},{10,11... | collective-permute-start | bytes 393224 | tf_op jit(solution)/shard_map/ppermute | solution.py:322
  20.8 2.7 %copy-start.2 = (s32[16,16]{1,0:T(8,128)S(1)}, s32[16,16]{1,0:T(8,128)}, u32[]{:S(2)}) copy-start(s32[16,16]{1,0:T(8,128)} %mask_ref.1) | copy-start | bytes 3076
  22.9 5.2 %collective-permute-start.8 = (f32[128,256]{1,0:T(8,128)S(1)}, f32[128,256]{1,0:T(8,128)S(1)}, u32[]{:S(2)}, u32[]{:S(2)}) collective-permute-start(f32[128,256]{1,0:T(8,128)S(1)} %score_strip.7.refs_0_), channel_id=1, source_target_pairs={{0,1},{1,0},{2,3},{3,2},{4,5},{5,4},{6,7},{7,6},{8,9},{9,8},{10,11... | collective-permute-start | bytes 393224 | tf_op jit(solution)/shard_map/ppermute | solution.py:322
  28.5 3.7 %collective-permute-start.10 = (f32[8,128]{1,0:T(8,128)S(1)}, f32[8,128]{1,0:T(8,128)S(1)}, u32[]{:S(2)}, u32[]{:S(2)}) collective-permute-start(f32[8,128]{1,0:T(8,128)S(1)} %get-tuple-element.62.refs_0_), channel_id=1, source_target_pairs={{0,8},{4,12},{8,0},{12,4},{1,9},{5,13},{9,1},{13,5},{2,10},{6,14},... | collective-permute-start | bytes 12296 | tf_op jit(solution)/shard_map/ppermute | solution.py:318
  29.8 3.0 %collective-permute-start.11 = (f32[8,128]{1,0:T(8,128)S(1)}, f32[8,128]{1,0:T(8,128)S(1)}, u32[]{:S(2)}, u32[]{:S(2)}) collective-permute-start(f32[8,128]{1,0:T(8,128)S(1)} %get-tuple-element.62.refs_0_), channel_id=1, source_target_pairs={{0,12},{4,8},{8,4},{12,0},{1,13},{5,9},{9,5},{13,1},{2,14},{6,10},... | collective-permute-start | bytes 12296 | tf_op jit(solution)/shard_map/ppermute | solution.py:318
  29.8 3.0 %collective-permute-start.9 = (f32[8,128]{1,0:T(8,128)S(1)}, f32[8,128]{1,0:T(8,128)S(1)}, u32[]{:S(2)}, u32[]{:S(2)}) collective-permute-start(f32[8,128]{1,0:T(8,128)S(1)} %get-tuple-element.62.refs_0_), channel_id=1, source_target_pairs={{0,4},{4,0},{8,12},{12,8},{1,5},{5,1},{9,13},{13,9},{2,6},{6,2},{1... | collective-permute-start | bytes 12296 | tf_op jit(solution)/shard_map/ppermute | solution.py:318
